TPU v7x, 32 devices: a whole 2x2x4 slice. The times are simulated.
32 devices in a mesh: blk: 16 (over z, x, core), grp: 2 (over y).
Axes of the slice: x: 2, y: 2, z: 4, core: 2. Of those that a mesh axis runs over, the one named last changes fastest.
Arguments:
- residents: bfloat16 [64, 32, 1024], P(('blk', 'grp')), may hold values from -6 to 6
- travellers: bfloat16 [32, 32, 1024], P('blk'), may hold values from -6 to 6
- pair_list: int32 [32, 4, 2, 3], P(('blk', 'grp')), may hold values from 0 to 1, as said below
Outputs:
- resident_exchange: float32 [64, 32, 1024], P(('blk', 'grp'))
- traveller_exchange: float32 [32, 32, 1024], P('blk', 'grp')
Inputs may be any that keep to these rules, and one draw needn't show every extreme that they name: `pair_list`: entry 0 is a resident index below 2, entry 1 a traveller index below 2, entry 2 is 0 or 1; the number of active slots differs from device to device.
All inputs are finite; a program needn't handle non-finite values.
Results may differ from a plain program's by a relative error of at most 0.0003.
Values may be sent and summed in bfloat16 or wider, within the bound.
No kernel may reach another device: no remote copies, remote signals or barrier semaphores. Data moves between devices by JAX's collectives and lax.ppermute only.
A program may use at most 64 MiB of HBM per device.

v0:
```python
import jax
import jax.numpy as jnp
from jax import lax
from jax.sharding import PartitionSpec as P


def from_behind(value, axis, by):
    peers = lax.axis_size(axis)
    return lax.ppermute(value, axis, [(i, (i + by) % peers) for i in range(peers)])


def sine_table(size):
    index = jnp.arange(size, dtype=jnp.float32) + 1.0
    return jnp.sqrt(2.0 / (size + 1)) * jnp.sin(jnp.pi * jnp.outer(index, index) / (size + 1))


def inverse_eigen(size):
    index = jnp.arange(size, dtype=jnp.float32) + 1.0
    eigen = 2.0 - 2.0 * jnp.cos(jnp.pi * index / (size + 1))
    total = eigen[:, None, None] + eigen[None, :, None] + eigen[None, None, :]
    return (1.0 / total).reshape(size, size * size)


def transform(field, table, plane_table):
    high = lax.Precision.HIGHEST
    field = jnp.einsum("ai,pim->pam", table, field, precision=high)
    return jnp.einsum("nm,pam->pan", plane_table, field, precision=high)


def arrival_terms(residents, moving, pairs, table, plane_table, inverse):
    res_count = residents.shape[0]
    trav_count = moving.shape[0]
    pick_res = (pairs[:, 0][:, None] == jnp.arange(res_count)[None, :]).astype(jnp.float32)
    pick_trav = (pairs[:, 1][:, None] == jnp.arange(trav_count)[None, :]).astype(jnp.float32)
    active = pairs[:, 2].astype(jnp.float32)[:, None, None]
    resident = jnp.einsum(
        "pr,rxm->pxm", pick_res.astype(jnp.bfloat16), residents, preferred_element_type=jnp.float32
    )
    traveller = jnp.einsum(
        "pt,txm->pxm", pick_trav.astype(jnp.bfloat16), moving, preferred_element_type=jnp.float32
    )
    potential = transform(
        transform(resident * traveller, table, plane_table) * inverse, table, plane_table
    )
    high = lax.Precision.HIGHEST
    res_terms = jnp.einsum("pr,pxm->rxm", pick_res, active * potential * traveller, precision=high)
    trav_terms = jnp.einsum("pt,pxm->txm", pick_trav, active * potential * resident, precision=high)
    return (res_terms, trav_terms)


def local(residents, travellers, pair_list):
    edge = residents.shape[1]
    arrivals_count = pair_list.shape[1]
    table = sine_table(edge)
    plane_table = jnp.kron(table, table)
    inverse = inverse_eigen(edge)
    res_total = jnp.zeros(residents.shape, jnp.float32)
    carried = jnp.zeros(travellers.shape, jnp.float32)
    home_total = None
    moving = travellers
    for arrival in range(arrivals_count):
        moving = from_behind(moving, "blk", 1)
        if arrival > 0:
            carried = from_behind(carried, "blk", 1)
        res_terms, trav_terms = arrival_terms(
            residents, moving, pair_list[0, arrival], table, plane_table, inverse
        )
        res_total = res_total + res_terms
        carried = carried + trav_terms
    reduced = lax.psum_scatter(carried, "grp", scatter_dimension=1, tiled=True)
    home_total = from_behind(reduced, "blk", -arrivals_count)
    return (res_total, home_total)


def solution(mesh):
    return jax.shard_map(
        local,
        mesh=mesh,
        in_specs=(
            P(("blk", "grp"), None, None),
            P("blk", None, None),
            P(("blk", "grp"), None, None, None),
        ),
        out_specs=(P(("blk", "grp"), None, None), P("blk", "grp", None)),
        check_vma=False,
    )
```

profile of v0, /device:TPU:0, one launch (start us, length us, event | category | flops | bytes accessed | tf_op | source)
XLA Modules:
  0.0 141.4 jit_solution(6960851741082830887)
XLA Ops:
  7.2 1.1 copy.54
  8.9 0.9 fusion.120
  11.3 8.0 %broadcast_multiply_fusion = f32[32,32,32,32]{3,2,1,0:T(8,128)} fusion(f32[32,32]{1,0:T(8,128)S(1)} %sine_multiply_fusion), kind=kLoop, calls=%fused_computation | loop fusion | flops 1048576 | bytes 4198400 | tf_op jit(solution)/shard_map/jit(kron)/mul | solution.py:55
  20.2 14.2 %reshape.178 = f32[1024,1024,1]{1,0,2:T(8,128)} reshape(f32[32,32,32,32]{3,2,1,0:T(8,128)} %broadcast_multiply_fusion) | data formatting | bytes 8388608 | tf_op jit(solution)/shard_map/jit(kron)/mul | solution.py:55
  37.2 6.3 %convolution_multiply_fusion.3 = f32[2,32,1024]{2,1,0:T(8,128)S(1)} fusion(f32[2,32,1024]{2,1,0:T(8,128)S(1)} %convolution_bitcast_fusion.7, f32[1024,1024,1]{1,0,2:T(8,128)} %reshape.178, f32[32,1024]{1,0:T(8,128)S(1)} %add_divide_fusion), kind=kOutput, calls=%fused_computation.4 | convolution fusion | flops 805371904 | bytes 4849664 | tf_op jit(solution)/shard_map/nm,pam->pan/dot_general | solution.py:27
  43.9 4.1 %fusion.129 = f32[2,32,1024]{2,1,0:T(8,128)S(1)} fusion(f32[2,32,1024]{2,1,0:T(8,128)S(1)} %convolution_bitcast_fusion.6, f32[1024,1024,1]{1,0,2:T(8,128)S(1)} %copy-done.1), kind=kOutput, calls=%fused_computation.176 | convolution fusion | flops 805306368 | bytes 4718592 | tf_op jit(solution)/shard_map/nm,pam->pan/dot_general | solution.py:27
  48.1 0.8 fusion.9
  48.9 2.7 %collective-permute-start.4 = (f32[2,32,1024]{2,0,1:T(2,128)S(1)}, f32[2,32,1024]{2,0,1:T(2,128)S(1)}, u32[]{:S(2)}, u32[]{:S(2)}) collective-permute-start(f32[2,32,1024]{2,0,1:T(2,128)S(1)} %fusion.9), channel_id=1, source_target_pairs={{0,2},{2,4},{4,6},{6,8},{8,10},{10,12},{12,14},{14,16},{16,18},{18... | collective-permute-start | bytes 786440 | tf_op jit(solution)/shard_map/ppermute | solution.py:9
  51.8 0.8 fusion.14
  52.6 6.8 %collective-permute-done.1 = bf16[2,32,1024]{2,0,1:T(2,128)(2,1)S(1)} collective-permute-done((bf16[2,32,1024]{2,0,1:T(2,128)(2,1)S(1)}, bf16[2,32,1024]{2,0,1:T(2,128)(2,1)S(1)}, u32[]{:S(2)}, u32[]{:S(2)}) %collective-permute-start.1) | collective-permute-done | bytes 131104 | tf_op jit(solution)/shard_map/ppermute | solution.py:9
  60.7 4.1 %convolution_multiply_fusion.2 = f32[2,32,1024]{2,1,0:T(8,128)S(1)} fusion(f32[2,32,1024]{2,1,0:T(8,128)S(1)} %convolution_bitcast_fusion.5, f32[1024,1024,1]{1,0,2:T(8,128)S(1)} %copy-done.1, f32[32,1024]{1,0:T(8,128)S(1)} %add_divide_fusion), kind=kOutput, calls=%fused_computation.3 | convolution fusion | flops 805371904 | bytes 4849664 | tf_op jit(solution)/shard_map/nm,pam->pan/dot_general | solution.py:27
  65.4 4.1 %fusion.130 = f32[2,32,1024]{2,1,0:T(8,128)S(1)} fusion(f32[2,32,1024]{2,1,0:T(8,128)S(1)} %convolution_bitcast_fusion.4, f32[1024,1024,1]{1,0,2:T(8,128)S(1)} %copy-done.1), kind=kOutput, calls=%fused_computation.177 | convolution fusion | flops 805306368 | bytes 4718592 | tf_op jit(solution)/shard_map/nm,pam->pan/dot_general | solution.py:27
  69.5 0.9 convolution_add_fusion
  70.6 1.8 %collective-permute-done.2 = bf16[2,32,1024]{2,0,1:T(2,128)(2,1)S(1)} collective-permute-done((bf16[2,32,1024]{2,0,1:T(2,128)(2,1)S(1)}, bf16[2,32,1024]{2,0,1:T(2,128)(2,1)S(1)}, u32[]{:S(2)}, u32[]{:S(2)}) %collective-permute-start.2) | collective-permute-done | bytes 131104 | tf_op jit(solution)/shard_map/ppermute | solution.py:9
  73.7 4.1 %convolution_multiply_fusion.1 = f32[2,32,1024]{2,1,0:T(8,128)S(1)} fusion(f32[2,32,1024]{2,1,0:T(8,128)S(1)} %convolution_bitcast_fusion.3, f32[1024,1024,1]{1,0,2:T(8,128)S(1)} %copy-done.1, f32[32,1024]{1,0:T(8,128)S(1)} %add_divide_fusion), kind=kOutput, calls=%fused_computation.2 | convolution fusion | flops 805371904 | bytes 4849664 | tf_op jit(solution)/shard_map/nm,pam->pan/dot_general | solution.py:27
  78.3 4.1 %fusion.131 = f32[2,32,1024]{2,1,0:T(8,128)S(1)} fusion(f32[2,32,1024]{2,1,0:T(8,128)S(1)} %convolution_bitcast_fusion.2, f32[1024,1024,1]{1,0,2:T(8,128)S(1)} %copy-done.1), kind=kOutput, calls=%fused_computation.178 | convolution fusion | flops 805306368 | bytes 4718592 | tf_op jit(solution)/shard_map/nm,pam->pan/dot_general | solution.py:27
  82.8 0.8 fusion.6
  83.6 6.3 %collective-permute-done.3 = bf16[2,32,1024]{2,0,1:T(2,128)(2,1)S(1)} collective-permute-done((bf16[2,32,1024]{2,0,1:T(2,128)(2,1)S(1)}, bf16[2,32,1024]{2,0,1:T(2,128)(2,1)S(1)}, u32[]{:S(2)}, u32[]{:S(2)}) %collective-permute-start.3) | collective-permute-done | bytes 131104 | tf_op jit(solution)/shard_map/ppermute | solution.py:9
  91.1 4.1 %convolution_multiply_fusion = f32[2,32,1024]{2,1,0:T(8,128)S(1)} fusion(f32[2,32,1024]{2,1,0:T(8,128)S(1)} %convolution_bitcast_fusion.1, f32[1024,1024,1]{1,0,2:T(8,128)S(1)} %copy-done.1, f32[32,1024]{1,0:T(8,128)S(1)} %add_divide_fusion), kind=kOutput, calls=%fused_computation.1 | convolution fusion | flops 805371904 | bytes 4849664 | tf_op jit(solution)/shard_map/nm,pam->pan/dot_general | solution.py:27
  96.0 4.1 %fusion.132 = f32[2,32,1024]{2,1,0:T(8,128)S(1)} fusion(f32[2,32,1024]{2,1,0:T(8,128)S(1)} %convolution_bitcast_fusion, f32[1024,1024,1]{1,0,2:T(8,128)S(1)} %copy-done.1), kind=kOutput, calls=%fused_computation.179 | convolution fusion | flops 805306368 | bytes 4718592 | tf_op jit(solution)/shard_map/nm,pam->pan/dot_general | solution.py:27
  100.1 0.8 fusion.4
  100.9 3.5 %collective-permute-done.6 = f32[2,32,1024]{2,0,1:T(2,128)S(1)} collective-permute-done((f32[2,32,1024]{2,0,1:T(2,128)S(1)}, f32[2,32,1024]{2,0,1:T(2,128)S(1)}, u32[]{:S(2)}, u32[]{:S(2)}) %collective-permute-start.6) | collective-permute-done | bytes 262176 | tf_op jit(solution)/shard_map/ppermute | solution.py:9
  104.5 0.8 add.183
  105.3 0.9 convolution_add_fusion.3
  106.2 0.9 convolution_add_fusion.2
  107.1 19.7 %all-reduce.3.cloned.1.call-done = f32[2,32,1024]{2,0,1:T(2,128)} async-done(((f32[2,32,1024]{2,0,1:T(2,128)}), f32[2,32,1024]{2,0,1:T(2,128)}) %all-reduce.3.cloned.1.call-update) | async-done | bytes 262160
  126.8 0.9 constant_dynamic-slice_fusion
  127.7 3.4 %collective-permute-start.7 = (f32[2,16,1024]{2,0,1:T(2,128)S(1)}, f32[2,16,1024]{2,0,1:T(2,128)S(1)}, u32[]{:S(2)}, u32[]{:S(2)}) collective-permute-start(f32[2,16,1024]{2,0,1:T(2,128)S(1)} %constant_dynamic-slice_fusion), channel_id=1, source_target_pairs={{0,24},{2,26},{4,28},{6,30},{8,0},{10,2},{12,4},{14,6},{16,8},{18,... | collective-permute-start | bytes 393224 | tf_op jit(solution)/shard_map/ppermute | solution.py:9
  131.1 0.9 convolution_add_fusion.1
  132.0 0.8 copy.76
  132.8 0.9 collective-permute-done.7
  133.6 0.7 copy.77
  (56 shorter events, 11.9 us)
Async XLA Ops:
  7.2 29.1 %copy-start = (bf16[2,32,1024]{2,1,0:T(8,128)(2,1)S(1)}, bf16[2,32,1024]{2,1,0:T(8,128)(2,1)}, u32[]{:S(2)}) copy-start(bf16[2,32,1024]{2,1,0:T(8,128)(2,1)} %param.3) | copy-start | bytes 393220
  7.2 119.6 %all-reduce.3.cloned.1.call-start = ((), (), s32[]{:S(2)}) async-start(), calls=%async_computation | async-start | bytes 524288
  8.3 27.6 %collective-permute-start = (bf16[2,32,1024]{2,0,1:T(2,128)(2,1)S(1)}, bf16[2,32,1024]{2,0,1:T(2,128)(2,1)S(1)}, u32[]{:S(2)}, u32[]{:S(2)}) collective-permute-start(bf16[2,32,1024]{2,0,1:T(2,128)(2,1)S(1)} %copy.54), channel_id=1, source_target_pairs={{0,2},{2,4},{4,6},{6,8},{8,10},{10,12},{12,14},{14,16},{16,18},{18... | collective-permute-start | bytes 393224 | tf_op jit(solution)/shard_map/ppermute | solution.py:9
  20.2 14.2 %copy-start.2 = (u32[32]{0:T(128)S(1)}, u32[32]{0:T(128)}, u32[]{:S(2)}) copy-start(u32[32]{0:T(128)} %constant.25) | copy-start | bytes 388
  35.7 8.3 %copy-start.1 = (f32[1024,1024,1]{1,0,2:T(8,128)S(1)}, f32[1024,1024,1]{1,0,2:T(8,128)}, u32[]{:S(2)}) copy-start(f32[1024,1024,1]{1,0,2:T(8,128)} %reshape.178) | copy-start | bytes 12582916
  48.9 20.6 %collective-permute-start.4 = (f32[2,32,1024]{2,0,1:T(2,128)S(1)}, f32[2,32,1024]{2,0,1:T(2,128)S(1)}, u32[]{:S(2)}, u32[]{:S(2)}) collective-permute-start(f32[2,32,1024]{2,0,1:T(2,128)S(1)} %fusion.9), channel_id=1, source_target_pairs={{0,2},{2,4},{4,6},{6,8},{8,10},{10,12},{12,14},{14,16},{16,18},{18... | collective-permute-start | bytes 786440 | tf_op jit(solution)/shard_map/ppermute | solution.py:9
  51.5 7.8 %collective-permute-start.1 = (bf16[2,32,1024]{2,0,1:T(2,128)(2,1)S(1)}, bf16[2,32,1024]{2,0,1:T(2,128)(2,1)S(1)}, u32[]{:S(2)}, u32[]{:S(2)}) collective-permute-start(bf16[2,32,1024]{2,0,1:T(2,128)(2,1)S(1)} %collective-permute-done), channel_id=1, source_target_pairs={{0,2},{2,4},{4,6},{6,8},{8,10},{10,12},{12,14},{14,16},{16,18},{18... | collective-permute-start | bytes 393224 | tf_op jit(solution)/shard_map/ppermute | solution.py:9
  65.3 7.1 %collective-permute-start.2 = (bf16[2,32,1024]{2,0,1:T(2,128)(2,1)S(1)}, bf16[2,32,1024]{2,0,1:T(2,128)(2,1)S(1)}, u32[]{:S(2)}, u32[]{:S(2)}) collective-permute-start(bf16[2,32,1024]{2,0,1:T(2,128)(2,1)S(1)} %collective-permute-done.1), channel_id=1, source_target_pairs={{0,2},{2,4},{4,6},{6,8},{8,10},{10,12},{12,14},{14,16},{16,18},{18... | collective-permute-start | bytes 393224 | tf_op jit(solution)/shard_map/ppermute | solution.py:9
  70.3 25.4 %collective-permute-start.5 = (f32[2,32,1024]{2,0,1:T(2,128)S(1)}, f32[2,32,1024]{2,0,1:T(2,128)S(1)}, u32[]{:S(2)}, u32[]{:S(2)}) collective-permute-start(f32[2,32,1024]{2,0,1:T(2,128)S(1)} %convolution_add_fusion), channel_id=1, source_target_pairs={{0,2},{2,4},{4,6},{6,8},{8,10},{10,12},{12,14},{14,16},{16,18},{18... | collective-permute-start | bytes 786440 | tf_op jit(solution)/shard_map/ppermute | solution.py:9
  82.5 7.4 %collective-permute-start.3 = (bf16[2,32,1024]{2,0,1:T(2,128)(2,1)S(1)}, bf16[2,32,1024]{2,0,1:T(2,128)(2,1)S(1)}, u32[]{:S(2)}, u32[]{:S(2)}) collective-permute-start(bf16[2,32,1024]{2,0,1:T(2,128)(2,1)S(1)} %collective-permute-done.2), channel_id=1, source_target_pairs={{0,2},{2,4},{4,6},{6,8},{8,10},{10,12},{12,14},{14,16},{16,18},{18... | collective-permute-start | bytes 393224 | tf_op jit(solution)/shard_map/ppermute | solution.py:9
  95.9 8.5 %collective-permute-start.6 = (f32[2,32,1024]{2,0,1:T(2,128)S(1)}, f32[2,32,1024]{2,0,1:T(2,128)S(1)}, u32[]{:S(2)}, u32[]{:S(2)}) collective-permute-start(f32[2,32,1024]{2,0,1:T(2,128)S(1)} %add.182), channel_id=1, source_target_pairs={{0,2},{2,4},{4,6},{6,8},{8,10},{10,12},{12,14},{14,16},{16,18},{18... | collective-permute-start | bytes 786440 | tf_op jit(solution)/shard_map/ppermute | solution.py:9
  127.7 5.9 %collective-permute-start.7 = (f32[2,16,1024]{2,0,1:T(2,128)S(1)}, f32[2,16,1024]{2,0,1:T(2,128)S(1)}, u32[]{:S(2)}, u32[]{:S(2)}) collective-permute-start(f32[2,16,1024]{2,0,1:T(2,128)S(1)} %constant_dynamic-slice_fusion), channel_id=1, source_target_pairs={{0,24},{2,26},{4,28},{6,30},{8,0},{10,2},{12,4},{14,6},{16,8},{18,... | collective-permute-start | bytes 393224 | tf_op jit(solution)/shard_map/ppermute | solution.py:9
Sparse Core Ops, SparseCore 0:
  105.4 21.3 all-reduce.2
where the time goes:
time: 144 us; the launch traced here: 141 us
  matrix products  48.8 us (34%)
  waiting for transfers between devices  39 us (27%)
  local copies, waits for them, and re-layouts  20.8 us (14%)
  between operations  15.3 us (11%)
  other arithmetic  9.98 us (7%)
  starting transfers between devices  7.5 us (5%)
    dot_general x8, matrix products, transform(): return jnp.einsum('nm,pam->pan', plane_table, field, precision=high)  35.1 us
    unnamed x2, waiting for transfers between devices  19.7 us
    ppermute x8, waiting for transfers between devices, from_behind(): lax.ppermute(value, axis, [(i, (i + by) % peers) for i in range(peers)])  19.3 us
    mul x1, local copies, waits for them, and re-layouts, local(): plane_table = jnp.kron(table, table)  14.2 us
    mul x1, other arithmetic, local(): plane_table = jnp.kron(table, table)  7.97 us
    ppermute x8, starting transfers between devices, from_behind(): lax.ppermute(value, axis, [(i, (i + by) % peers) for i in range(peers)])  7.47 us
    dot_general x8, matrix products, transform(): field = jnp.einsum('ai,pim->pam', table, field, precision=high)  4.13 us
    unnamed x11, local copies, waits for them, and re-layouts  4.07 us
  transfers between devices with their start and end apart: 9, of which 6 were waited for; matrix products, arithmetic and copies ran while one was open for 45% of the time, Pallas kernels for 0%

commit v1 on v0

v1 whole, which is shorter than its diff:
```python
import functools

import jax
import jax.numpy as jnp
import ml_dtypes
import numpy as np
from jax import lax
from jax.experimental import pallas as pl
from jax.experimental.pallas import tpu as pltpu
from jax.sharding import PartitionSpec as P

LANES = 128


def split16(table):
    high = table.astype(ml_dtypes.bfloat16)
    return high, (table - high.astype(np.float64)).astype(ml_dtypes.bfloat16)


@functools.lru_cache
def tables(edge, fields):
    index = np.arange(edge) + 1.0
    sine = np.sqrt(2.0 / (edge + 1)) * np.sin(np.pi * np.outer(index, index) / (edge + 1))
    eigen = 2.0 - 2.0 * np.cos(np.pi * index / (edge + 1))
    parts = []
    for parity in (0, 1):
        plane = np.kron(sine[parity::2, : edge // 2], sine).T
        parts += [*split16(plane), *split16(np.ascontiguousarray(plane.T))]
    parts += split16(np.kron(np.eye(fields), sine))
    by_plane = np.concatenate(
        [(eigen[parity::2, None] + eigen[None, :]).reshape(-1) for parity in (0, 1)]
    )
    parts.append((1.0 / (eigen[:, None] + by_plane[None, :])).astype(np.float32))
    return tuple(parts)


def dot(x, y):
    return jnp.dot(x, y, preferred_element_type=jnp.float32)


def halves(x):
    high = x.astype(jnp.bfloat16)
    return high, (x - high.astype(jnp.float32)).astype(jnp.bfloat16)


def times_table(x, high, low):
    x_high, x_low = halves(x)
    return dot(x_high, high) + (dot(x_low, high) + dot(x_high, low))


def table_times(high, low, x):
    x_high, x_low = halves(x)
    return dot(high, x_high) + (dot(high, x_low) + dot(low, x_high))


def reverse_groups(x, edge):
    blocks = []
    lane = lax.broadcasted_iota(jnp.int32, (x.shape[0], LANES), 1)
    for start in range(x.shape[1] - LANES, -1, -LANES):
        block = x[:, start : start + LANES]
        width = LANES // 2
        while width >= edge:
            block = jnp.where(
                lane % (2 * width) < width,
                pltpu.roll(block, LANES - width, 1),
                pltpu.roll(block, width, 1),
            )
            width //= 2
        blocks.append(block)
    return jnp.concatenate(blocks, axis=1)


def fold(field, edge):
    half = field.shape[1] // 2
    return field[:, :half], reverse_groups(field[:, half:], edge)


def unfold(first, second, edge):
    return jnp.concatenate([first, reverse_groups(second, edge)], axis=1)


def store_folded(source, target):
    edge = source.shape[1]
    for i in range(source.shape[0]):
        first, second = fold(source[i].astype(jnp.float32), edge)
        target[i, 0] = first
        target[i, 1] = second


def gather_terms(slots, home, total, table_refs):
    (even_in, even_in_low, even_out, even_out_low, odd_in, odd_in_low, odd_out, odd_out_low,
     along, along_low, inverse) = (ref[...] for ref in table_refs)
    edge = inverse.shape[0]
    half = inverse.shape[1] // 2
    evens, odds = [], []
    for moving, i, j, _ in slots:
        first = moving[i, 0] * home[j, 0]
        second = moving[i, 1] * home[j, 1]
        evens.append(first + second)
        odds.append(first - second)
    even = times_table(jnp.concatenate(evens, axis=0), even_in, even_in_low)
    odd = times_table(jnp.concatenate(odds, axis=0), odd_in, odd_in_low)
    modes = table_times(along, along_low, jnp.concatenate([even, odd], axis=1))
    modes = (modes.reshape(len(slots), edge, 2 * half) * inverse[None]).reshape(modes.shape)
    modes = table_times(along, along_low, modes)
    even = times_table(modes[:, :half], even_out, even_out_low)
    odd = times_table(modes[:, half:], odd_out, odd_out_low)
    first, second = even + odd, even - odd
    for slot, (moving, i, j, active) in enumerate(slots):
        rows = slice(slot * edge, (slot + 1) * edge)
        total[j, 0] += active * (first[rows] * moving[i, 0])
        total[j, 1] += active * (second[rows] * moving[i, 1])


def slots_of(pairs, arrival, moving, moving_entry):
    return [
        (
            moving,
            pairs[0, arrival, slot, moving_entry],
            pairs[0, arrival, slot, 1 - moving_entry],
            pairs[0, arrival, slot, 2].astype(jnp.float32),
        )
        for slot in range(pairs.shape[2])
    ]


def store_swapped(near, swapped, moving):
    count = len(swapped) - 1

    @pl.when(near == 1)
    def _():
        for k in range(count):
            store_folded(swapped[k], moving.at[k])

    @pl.when(near == 0)
    def _():
        for k in range(count):
            store_folded(swapped[k + 1], moving.at[k])


def early_kernel(count, *refs):
    pairs, refs = refs[:count], refs[count:]
    arrived, refs = refs[:count], refs[count:]
    home, table_refs, (total, home_folded, moving) = refs[0], refs[1:12], refs[12:]
    store_folded(home, home_folded)
    total[...] = jnp.zeros_like(total)
    slots = []
    for k in range(count):
        store_folded(arrived[k], moving.at[k])
        slots += slots_of(pairs[k], 2 * k + 1, moving.at[k], 0)
    gather_terms(slots, home_folded, total, table_refs)


def late_kernel(count, where, *refs):
    pairs, refs = refs[:count], refs[count:]
    swapped, refs = refs[: count + 1], refs[count + 1 :]
    home, early, table_refs = refs[0], refs[1], refs[2:13]
    mine, others, home_folded, moving, total, whole = refs[13:]
    edge = home.shape[1]
    store_folded(home, home_folded)
    store_swapped(where[0], swapped, moving)
    slots = []
    for k in range(count):
        slots += slots_of(pairs[k], 2 * k, moving.at[k], 0)
    total[...] = early[...]
    gather_terms(slots, home_folded, total, table_refs)
    parts, rows = whole.shape[1:3]
    for i in range(home.shape[0]):
        field = unfold(total[i, 0], total[i, 1], edge)
        for part in range(parts):
            whole[i, part] = field[part * rows : (part + 1) * rows]
    for k in range(parts):
        part = lax.rem(where[1] + k, parts)
        for i in range(home.shape[0]):
            if k == 0:
                mine[i] = whole[i, part]
            else:
                others[k - 1, i] = whole[i, part]


def resident_kernel(count, where, pairs, *refs):
    arrived, refs = refs[:count], refs[count:]
    swapped, refs = refs[: count + 1], refs[count + 1 :]
    home, table_refs = refs[0], refs[1:12]
    result, home_folded, moving, moving_swapped, total = refs[12:]
    edge = home.shape[1]
    store_folded(home, home_folded)
    total[...] = jnp.zeros_like(total)
    slots = []
    for k in range(count):
        store_folded(arrived[k], moving.at[k])
        slots += slots_of(pairs, 2 * k + 1, moving.at[k], 1)
    gather_terms(slots, home_folded, total, table_refs)
    store_swapped(where[0], swapped, moving_swapped)
    slots = []
    for k in range(count):
        slots += slots_of(pairs, 2 * k, moving_swapped.at[k], 1)
    gather_terms(slots, home_folded, total, table_refs)
    for i in range(home.shape[0]):
        result[i] = unfold(total[i, 0], total[i, 1], edge)


SMEM = pl.BlockSpec(memory_space=pltpu.SMEM)
VMEM = pl.BlockSpec(memory_space=pltpu.VMEM)
LIMIT = pltpu.CompilerParams(vmem_limit_bytes=32 * 1024 * 1024)


def from_behind(value, by):
    peers = lax.axis_size("blk")
    return lax.ppermute(value, "blk", [(i, (i + by) % peers) for i in range(peers)])


def other_core(value, only_to=None):
    peers = lax.axis_size("blk")
    return lax.ppermute(
        value, "blk", [(i, i ^ 1) for i in range(peers) if only_to in (None, (i ^ 1) % 2)]
    )


def local(residents, travellers, pair_list):
    count, edge, plane = residents.shape
    steps = pair_list.shape[1]
    direct = range(2, steps + 1, 2)
    arrivals = len(direct)
    groups = lax.axis_size("grp")
    part = edge // groups
    fields = arrivals * pair_list.shape[2]
    consts = [jnp.asarray(table) for table in tables(edge, fields)]

    res_moved = [from_behind(residents, -s) for s in direct]
    res_swapped = [other_core(residents, 0)]
    pairs = [from_behind(pair_list, -s) for s in range(1, steps + 1)]
    trav_moved = [from_behind(travellers, s) for s in direct]
    trav_swapped = [other_core(travellers, 1)]
    for k in range(arrivals):
        last = k == arrivals - 1
        res_swapped.append(other_core(res_moved[k], 1 if last else None))
        trav_swapped.append(other_core(trav_moved[k], 0 if last else None))

    core = lax.axis_index("blk") % 2
    group = lax.axis_index("grp")
    res_where = jnp.stack([1 - core, group]).astype(jnp.int32)
    trav_where = jnp.stack([core, group]).astype(jnp.int32)

    folded = (count, 2, edge, plane // 2)
    early = pl.pallas_call(
        functools.partial(early_kernel, arrivals),
        out_shape=jax.ShapeDtypeStruct(folded, jnp.float32),
        in_specs=[SMEM] * arrivals + [VMEM] * (arrivals + 1 + len(consts)),
        out_specs=VMEM,
        scratch_shapes=[
            pltpu.VMEM(folded, jnp.float32),
            pltpu.VMEM((arrivals, *folded), jnp.float32),
        ],
        compiler_params=LIMIT,
        name="early_terms",
    )(*pairs[1::2], *res_moved, travellers, *consts)
    mine, others = pl.pallas_call(
        functools.partial(late_kernel, arrivals),
        out_shape=(
            jax.ShapeDtypeStruct((count, part, plane), jnp.float32),
            jax.ShapeDtypeStruct((groups - 1, count, part, plane), jnp.float32),
        ),
        in_specs=[SMEM] * (1 + arrivals) + [VMEM] * (arrivals + 3 + len(consts)),
        out_specs=(VMEM, VMEM),
        scratch_shapes=[
            pltpu.VMEM(folded, jnp.float32),
            pltpu.VMEM((arrivals, *folded), jnp.float32),
            pltpu.VMEM(folded, jnp.float32),
            pltpu.VMEM((count, groups, part, plane), jnp.float32),
        ],
        compiler_params=LIMIT,
        name="late_terms",
    )(res_where, *pairs[0::2], *res_swapped, travellers, early, *consts)
    sent = [
        lax.ppermute(others[k - 1], "grp", [(g, (g + k) % groups) for g in range(groups)])
        for k in range(1, groups)
    ]
    res_total = pl.pallas_call(
        functools.partial(resident_kernel, arrivals),
        out_shape=jax.ShapeDtypeStruct(residents.shape, jnp.float32),
        in_specs=[SMEM] * 2 + [VMEM] * (2 * arrivals + 2 + len(consts)),
        out_specs=VMEM,
        scratch_shapes=[
            pltpu.VMEM(folded, jnp.float32),
            pltpu.VMEM((arrivals, *folded), jnp.float32),
            pltpu.VMEM((arrivals, *folded), jnp.float32),
            pltpu.VMEM(folded, jnp.float32),
        ],
        compiler_params=LIMIT,
        name="resident_terms",
    )(trav_where, pair_list, *trav_moved, *trav_swapped, residents, *consts)
    for value in sent:
        mine = mine + value
    return res_total, mine


def solution(mesh):
    return jax.shard_map(
        local,
        mesh=mesh,
        in_specs=(
            P(("blk", "grp"), None, None),
            P("blk", None, None),
            P(("blk", "grp"), None, None, None),
        ),
        out_specs=(P(("blk", "grp"), None, None), P("blk", "grp", None)),
        check_vma=False,
    )
```

time: 144 us -> 47.3 us (0.33); the launches traced: 141 us -> 46.7 us
  matrix products: 48.8 us -> 0 us
  waiting for transfers between devices: 39 us -> 3.12 us
  between operations: 15.3 us -> 0.88 us
  starting transfers between devices: 7.5 us -> 21.2 us
  local copies, waits for them, and re-layouts: 20.8 us -> 8.74 us
  Pallas kernels: 0 us -> 12 us
  other arithmetic: 9.98 us -> 0.83 us
    dot_general x32 -> x0, matrix products: 48.8 us -> none  [the longest x8 35.1 us: transform(): return jnp.einsum('nm,pam->pan', plane_table, field, precision=high)]
    unnamed x2 -> x0, waiting for transfers between devices: 19.7 us -> none
    ppermute x8 -> x15, waiting for transfers between devices: 19.3 us -> 3.12 us  [the longest x8 3.1 us: from_behind(): lax.ppermute(value, 'blk', [(i, (i + by) % peers) for i in range(peers)])]
    mul x1 -> x0, local copies, waits for them, and re-layouts: 14.2 us -> none  [local(): plane_table = jnp.kron(table, table)]
    ppermute x8 -> x15, starting transfers between devices: 7.47 us -> 21.2 us  [the longest x8 10.6 us: from_behind(): lax.ppermute(value, 'blk', [(i, (i + by) % peers) for i in range(peers)])]
    pallas_call x0 -> x3, Pallas kernels: none -> 12 us  [the longest x1 5.7 us: local(): pl.pallas_call(functools.partial(resident_kernel, arrivals), out_shape=ja...]
    mul x2 -> x0, other arithmetic: 8.11 us -> none  [the longest x1 7.97 us: local(): plane_table = jnp.kron(table, table)]
    unnamed x11 -> x33, local copies, waits for them, and re-layouts: 4.07 us -> 8.74 us
  transfers between devices with their start and end apart: 9 -> 15, of which waited for: 6 -> 1; matrix products, arithmetic and copies ran while one was open for 45% -> 2% of each run, Pallas kernels for 0% -> 26%
where the time goes in v1:
time: 47.3 us; the launch traced here: 46.7 us
  starting transfers between devices  21.2 us (45%)
  Pallas kernels  12 us (25%)
  local copies, waits for them, and re-layouts  8.74 us (18%)
  waiting for transfers between devices  3.12 us (7%)
  between operations  0.88 us (2%)
  other arithmetic  0.83 us (2%)
    ppermute x8, starting transfers between devices, from_behind(): lax.ppermute(value, 'blk', [(i, (i + by) % peers) for i in range(peers)])  10.6 us
    ppermute x6, starting transfers between devices, other_core(): lax.ppermute(value, 'blk', [(i, i ^ 1) for i in range(peers) if only_to i...  8.97 us
    unnamed x33, local copies, waits for them, and re-layouts  8.74 us
    pallas_call x1, Pallas kernels, local(): pl.pallas_call(functools.partial(resident_kernel, arrivals), out_shape=ja...  5.7 us
    pallas_call x1, Pallas kernels, local(): pl.pallas_call(functools.partial(late_kernel, arrivals), out_shape=(jax.S...  3.31 us
    ppermute x8, waiting for transfers between devices, from_behind(): lax.ppermute(value, 'blk', [(i, (i + by) % peers) for i in range(peers)])  3.1 us
    pallas_call x1, Pallas kernels, local(): pl.pallas_call(functools.partial(early_kernel, arrivals), out_shape=jax.S...  2.98 us
    ppermute x1, starting transfers between devices, local(): lax.ppermute(others[k - 1], 'grp', [(g, (g + k) % groups) for g in range(...  1.59 us
  transfers between devices with their start and end apart: 15, of which 1 were waited for; matrix products, arithmetic and copies ran while one was open for 2% of the time, Pallas kernels for 26%

profile of v1, /device:TPU:0, one launch (start us, length us, event | category | flops | bytes accessed | tf_op | source)
XLA Modules:
  0.0 46.7 jit_solution(14301147365929747240)
XLA Ops:
  0.6 5.1 %collective-permute-start.10 = (bf16[2,32,1024]{2,1,0:T(8,128)(2,1)}, bf16[2,32,1024]{2,1,0:T(8,128)(2,1)S(1)}, u32[]{:S(2)}, u32[]{:S(2)}) collective-permute-start(bf16[2,32,1024]{2,1,0:T(8,128)(2,1)} %refs_5_.3), channel_id=1, source_target_pairs={{0,24},{2,26},{4,28},{6,30},{8,0},{10,2},{12,4},{14,6},{16,8},{18,... | collective-permute-start | bytes 393224 | tf_op jit(solution)/shard_map/ppermute | solution.py:210
  5.7 1.4 %collective-permute-start.8 = (bf16[2,32,1024]{2,1,0:T(8,128)(2,1)}, bf16[2,32,1024]{2,1,0:T(8,128)(2,1)S(1)}, u32[]{:S(2)}, u32[]{:S(2)}) collective-permute-start(bf16[2,32,1024]{2,1,0:T(8,128)(2,1)} %refs_5_.3), channel_id=1, source_target_pairs={{0,28},{2,30},{4,0},{6,2},{8,4},{10,6},{12,8},{14,10},{16,12},{18,... | collective-permute-start | bytes 393224 | tf_op jit(solution)/shard_map/ppermute | solution.py:210
  7.1 0.8 %copy.16.pairs = s32[1,4,2,3]{3,2,1,0:T(2,128)S(1)} copy(s32[1,4,2,3]{1,2,3,0:T(2,128)} %param.16) | data formatting | bytes 192 | tf_op args[2]
  7.9 0.4 collective-permute-start.13
  8.3 0.5 %collective-permute-start.12 = (s32[1,4,2,3]{3,2,1,0:T(2,128)S(1)}, s32[1,4,2,3]{3,2,1,0:T(2,128)S(1)}, u32[]{:S(2)}, u32[]{:S(2)}) collective-permute-start(s32[1,4,2,3]{3,2,1,0:T(2,128)S(1)} %copy.16.pairs), channel_id=1, source_target_pairs={{0,28},{2,30},{4,0},{6,2},{8,4},{10,6},{12,8},{14,10},{16,12},{18,... | collective-permute-start | bytes 296 | tf_op jit(solution)/shard_map/ppermute | solution.py:210
  8.9 3.1 %collective-permute-done.13.refs_1_ = s32[1,4,2,3]{3,2,1,0:T(2,128)S(1)} collective-permute-done((s32[1,4,2,3]{3,2,1,0:T(2,128)S(1)}, s32[1,4,2,3]{3,2,1,0:T(2,128)S(1)}, u32[]{:S(2)}, u32[]{:S(2)}) %collective-permute-start.13) | collective-permute-done | bytes 128 | tf_op jit(solution)/shard_map/ppermute | solution.py:210
  12.0 0.6 %collective-permute-start.5 = (s32[1,4,2,3]{3,2,1,0:T(2,128)S(1)}, s32[1,4,2,3]{3,2,1,0:T(2,128)S(1)}, u32[]{:S(2)}, u32[]{:S(2)}) collective-permute-start(s32[1,4,2,3]{3,2,1,0:T(2,128)S(1)} %copy.16.pairs), channel_id=1, source_target_pairs={{0,30},{2,0},{4,2},{6,4},{8,6},{10,8},{12,10},{14,12},{16,14},{18,... | collective-permute-start | bytes 296 | tf_op jit(solution)/shard_map/ppermute | solution.py:210
  12.6 1.3 %collective-permute-start.7 = (bf16[2,32,1024]{2,1,0:T(8,128)(2,1)}, bf16[2,32,1024]{2,1,0:T(8,128)(2,1)S(1)}, u32[]{:S(2)}, u32[]{:S(2)}) collective-permute-start(bf16[2,32,1024]{2,1,0:T(8,128)(2,1)} %refs_5_.3), channel_id=1, source_target_pairs={{2,0},{6,4},{10,8},{14,12},{18,16},{22,20},{26,24},{30,28},{3,1},{... | collective-permute-start | bytes 393224 | tf_op jit(solution)/shard_map/ppermute | solution.py:215
  13.9 1.0 %collective-permute-start.1 = (bf16[2,32,1024]{2,1,0:T(8,128)(2,1)}, bf16[2,32,1024]{2,1,0:T(8,128)(2,1)S(1)}, u32[]{:S(2)}, u32[]{:S(2)}) collective-permute-start(bf16[2,32,1024]{2,1,0:T(8,128)(2,1)} %refs_5_.4), channel_id=1, source_target_pairs={{0,8},{2,10},{4,12},{6,14},{8,16},{10,18},{12,20},{14,22},{16,24},... | collective-permute-start | bytes 393224 | tf_op jit(solution)/shard_map/ppermute | solution.py:210
  14.9 1.5 %collective-permute-start = (bf16[2,32,1024]{2,1,0:T(8,128)(2,1)}, bf16[2,32,1024]{2,1,0:T(8,128)(2,1)S(1)}, u32[]{:S(2)}, u32[]{:S(2)}) collective-permute-start(bf16[2,32,1024]{2,1,0:T(8,128)(2,1)} %refs_5_.4), channel_id=1, source_target_pairs={{0,4},{2,6},{4,8},{6,10},{8,12},{10,14},{12,16},{14,18},{16,20},{1... | collective-permute-start | bytes 393224 | tf_op jit(solution)/shard_map/ppermute | solution.py:210
  16.4 2.5 %collective-permute-start.11 = (bf16[2,32,1024]{2,1,0:T(8,128)(2,1)S(1)}, bf16[2,32,1024]{2,1,0:T(8,128)(2,1)S(1)}, u32[]{:S(2)}, u32[]{:S(2)}) collective-permute-start(bf16[2,32,1024]{2,1,0:T(8,128)(2,1)S(1)} %collective-permute-done.10.refs_3_), channel_id=1, source_target_pairs={{0,2},{4,6},{8,10},{12,14},{16,18},{20,22},{24,26},{28,30},{1,3},{... | collective-permute-start | bytes 393224 | tf_op jit(solution)/shard_map/ppermute | solution.py:215
  18.9 0.1 collective-permute-start.9
  19.0 0.1 pad_add_fusion.1.where
  19.1 1.0 %copy-done = bf16[512,512]{1,0:T(8,128)(2,1)S(1)} copy-done((bf16[512,512]{1,0:T(8,128)(2,1)S(1)}, bf16[512,512]{1,0:T(8,128)(2,1)}, u32[]{:S(2)}) %copy-start) | copy-done | bytes 524312
  20.1 1.0 %copy-done.2 = bf16[512,512]{1,0:T(8,128)(2,1)S(1)} copy-done((bf16[512,512]{1,0:T(8,128)(2,1)S(1)}, bf16[512,512]{1,0:T(8,128)(2,1)}, u32[]{:S(2)}) %copy-start.2) | copy-done | bytes 524312
  21.2 1.0 %copy-done.4 = bf16[512,512]{1,0:T(8,128)(2,1)S(1)} copy-done((bf16[512,512]{1,0:T(8,128)(2,1)S(1)}, bf16[512,512]{1,0:T(8,128)(2,1)}, u32[]{:S(2)}) %copy-start.4) | copy-done | bytes 524312
  22.2 1.0 %copy-done.6 = bf16[512,512]{1,0:T(8,128)(2,1)S(1)} copy-done((bf16[512,512]{1,0:T(8,128)(2,1)S(1)}, bf16[512,512]{1,0:T(8,128)(2,1)}, u32[]{:S(2)}) %copy-start.6) | copy-done | bytes 524312
  23.3 1.0 %copy-done.8 = bf16[512,512]{1,0:T(8,128)(2,1)S(1)} copy-done((bf16[512,512]{1,0:T(8,128)(2,1)S(1)}, bf16[512,512]{1,0:T(8,128)(2,1)}, u32[]{:S(2)}) %copy-start.8) | copy-done | bytes 524312
  24.3 1.0 %copy-done.10 = bf16[512,512]{1,0:T(8,128)(2,1)S(1)} copy-done((bf16[512,512]{1,0:T(8,128)(2,1)S(1)}, bf16[512,512]{1,0:T(8,128)(2,1)}, u32[]{:S(2)}) %copy-start.10) | copy-done | bytes 524312
  25.4 0.9 %copy-done.12 = f32[32,1024]{1,0:T(8,128)S(1)} copy-done((f32[32,1024]{1,0:T(8,128)S(1)}, f32[32,1024]{1,0:T(8,128)}, u32[]{:S(2)}) %copy-start.12) | copy-done | bytes 131096
  26.3 0.8 %copy-done.14 = bf16[128,128]{1,0:T(8,128)(2,1)S(1)} copy-done((bf16[128,128]{1,0:T(8,128)(2,1)S(1)}, bf16[128,128]{1,0:T(8,128)(2,1)}, u32[]{:S(2)}) %copy-start.14) | copy-done | bytes 32792
  27.0 3.0 %early_terms.1.refs_6_ = f32[2,2,32,512]{3,2,1,0:T(8,128)S(1)} custom-call(s32[1,4,2,3]{3,2,1,0:T(2,128)S(1)} %collective-permute-done.12.refs_0_, s32[1,4,2,3]{3,2,1,0:T(2,128)S(1)} %collective-permute-done.13.refs_1_, bf16[2,32,1024]{2,1,0:T(8,128)(2,1)S(1)} %collective-permute-done.8.refs_2_, bf16[2,32,1024]{2,1,0:T(8,128)(2,1)S(1)} %collective-permute-done.10.refs_3_, ...), custom_call_target="tpu_custom_call" | custom-call | tf_op jit(solution)/shard_map/early_terms/pallas_call | solution.py:246
  30.0 0.0 copy-start.1
  30.0 0.0 copy-start.3
  30.1 2.7 %collective-permute-start.2 = (bf16[2,32,1024]{2,1,0:T(8,128)(2,1)}, bf16[2,32,1024]{2,1,0:T(8,128)(2,1)S(1)}, u32[]{:S(2)}, u32[]{:S(2)}) collective-permute-start(bf16[2,32,1024]{2,1,0:T(8,128)(2,1)} %refs_5_.4), channel_id=1, source_target_pairs={{0,2},{4,6},{8,10},{12,14},{16,18},{20,22},{24,26},{28,30},{1,3},{... | collective-permute-start | bytes 393224 | tf_op jit(solution)/shard_map/ppermute | solution.py:215
  32.8 1.3 %collective-permute-start.4 = (bf16[2,32,1024]{2,1,0:T(8,128)(2,1)S(1)}, bf16[2,32,1024]{2,1,0:T(8,128)(2,1)S(1)}, u32[]{:S(2)}, u32[]{:S(2)}) collective-permute-start(bf16[2,32,1024]{2,1,0:T(8,128)(2,1)S(1)} %collective-permute-done.1.refs_1_), channel_id=1, source_target_pairs={{2,0},{6,4},{10,8},{14,12},{18,16},{22,20},{26,24},{30,28},{3,1},{... | collective-permute-start | bytes 393224 | tf_op jit(solution)/shard_map/ppermute | solution.py:215
  34.1 1.2 %collective-permute-start.3 = (bf16[2,32,1024]{2,1,0:T(8,128)(2,1)S(1)}, bf16[2,32,1024]{2,1,0:T(8,128)(2,1)S(1)}, u32[]{:S(2)}, u32[]{:S(2)}) collective-permute-start(bf16[2,32,1024]{2,1,0:T(8,128)(2,1)S(1)} %collective-permute-done.refs_0_), channel_id=1, source_target_pairs={{0,2},{2,0},{4,6},{6,4},{8,10},{10,8},{12,14},{14,12},{16,18},{18,... | collective-permute-start | bytes 393224 | tf_op jit(solution)/shard_map/ppermute | solution.py:215
  35.3 3.3 %late_terms.1 = (f32[2,16,1024]{2,1,0:T(8,128)S(1)}, f32[1,2,16,1024]{3,2,1,0:T(8,128)S(1)}) custom-call(s32[2]{0:T(128)S(1)} %pad_add_fusion.1.where, s32[1,4,2,3]{3,2,1,0:T(2,128)S(1)} %collective-permute-done.5.refs_0_, s32[1,4,2,3]{3,2,1,0:T(2,128)S(1)} %collective-permute-done.6.refs_1_, bf16[2,32,1024]{2,1,0:T(8,128)(2,1)S(1)} %collective-permute-done.7.refs_2_, ...), custom_call_target="tpu_custom_call" | custom-call | tf_op jit(solution)/shard_map/late_terms/pallas_call | solution.py:258
  38.6 1.6 %collective-permute-start.14 = (f32[2,16,1024]{2,1,0:T(8,128)S(1)}, f32[2,16,1024]{2,1,0:T(8,128)S(1)}, u32[]{:S(2)}, u32[]{:S(2)}) collective-permute-start(f32[2,16,1024]{2,1,0:T(8,128)S(1)} %bitcast.4), channel_id=1, source_target_pairs={{0,1},{1,0},{2,3},{3,2},{4,5},{5,4},{6,7},{7,6},{8,9},{9,8},{10,11... | collective-permute-start | bytes 393224 | tf_op jit(solution)/shard_map/ppermute | solution.py:276
  40.2 0.1 pad_add_fusion.where
  40.3 5.7 %resident_terms.1 = f32[2,32,1024]{2,1,0:T(8,128)} custom-call(s32[2]{0:T(128)S(1)} %pad_add_fusion.where, s32[1,4,2,3]{3,2,1,0:T(2,128)S(1)} %copy.16.pairs, bf16[2,32,1024]{2,1,0:T(8,128)(2,1)S(1)} %collective-permute-done.refs_0_, bf16[2,32,1024]{2,1,0:T(8,128)(2,1)S(1)} %collective-permute-done.1.refs_1_, ...), custom_call_target="tpu_custom_call" | custom-call | tf_op jit(solution)/shard_map/resident_terms/pallas_call | solution.py:279
  46.1 0.7 %add.8 = f32[2,16,1024]{2,1,0:T(8,128)} add(f32[2,16,1024]{2,1,0:T(8,128)S(1)} %get-tuple-element.4, f32[2,16,1024]{2,1,0:T(8,128)S(1)} %collective-permute-done.14) | non-fusion elementwise | flops 32768 | bytes 393216 | tf_op jit(solution)/shard_map/add | solution.py:294
  (37 shorter events, 0.1 us)
Async XLA Ops:
  0.6 18.5 %copy-start.13 = (bf16[128,128]{1,0:T(8,128)(2,1)S(1)}, bf16[128,128]{1,0:T(8,128)(2,1)}, u32[]{:S(2)}) copy-start(bf16[128,128]{1,0:T(8,128)(2,1)} %constant.47.clone.refs_15_.refs_14_.refs_16_) | copy-start | bytes 98308
  0.6 15.8 %collective-permute-start.10 = (bf16[2,32,1024]{2,1,0:T(8,128)(2,1)}, bf16[2,32,1024]{2,1,0:T(8,128)(2,1)S(1)}, u32[]{:S(2)}, u32[]{:S(2)}) collective-permute-start(bf16[2,32,1024]{2,1,0:T(8,128)(2,1)} %refs_5_.3), channel_id=1, source_target_pairs={{0,24},{2,26},{4,28},{6,30},{8,0},{10,2},{12,4},{14,6},{16,8},{18,... | collective-permute-start | bytes 393224 | tf_op jit(solution)/shard_map/ppermute | solution.py:210
  5.7 13.2 %collective-permute-start.8 = (bf16[2,32,1024]{2,1,0:T(8,128)(2,1)}, bf16[2,32,1024]{2,1,0:T(8,128)(2,1)S(1)}, u32[]{:S(2)}, u32[]{:S(2)}) collective-permute-start(bf16[2,32,1024]{2,1,0:T(8,128)(2,1)} %refs_5_.3), channel_id=1, source_target_pairs={{0,28},{2,30},{4,0},{6,2},{8,4},{10,6},{12,8},{14,10},{16,12},{18,... | collective-permute-start | bytes 393224 | tf_op jit(solution)/shard_map/ppermute | solution.py:210
  7.9 4.1 %collective-permute-start.13 = (s32[1,4,2,3]{3,2,1,0:T(2,128)S(1)}, s32[1,4,2,3]{3,2,1,0:T(2,128)S(1)}, u32[]{:S(2)}, u32[]{:S(2)}) collective-permute-start(s32[1,4,2,3]{3,2,1,0:T(2,128)S(1)} %copy.16.pairs), channel_id=1, source_target_pairs={{0,24},{2,26},{4,28},{6,30},{8,0},{10,2},{12,4},{14,6},{16,8},{18,... | collective-permute-start | bytes 296 | tf_op jit(solution)/shard_map/ppermute | solution.py:210
  8.3 4.2 %collective-permute-start.12 = (s32[1,4,2,3]{3,2,1,0:T(2,128)S(1)}, s32[1,4,2,3]{3,2,1,0:T(2,128)S(1)}, u32[]{:S(2)}, u32[]{:S(2)}) collective-permute-start(s32[1,4,2,3]{3,2,1,0:T(2,128)S(1)} %copy.16.pairs), channel_id=1, source_target_pairs={{0,28},{2,30},{4,0},{6,2},{8,4},{10,6},{12,8},{14,10},{16,12},{18,... | collective-permute-start | bytes 296 | tf_op jit(solution)/shard_map/ppermute | solution.py:210
  8.9 5.0 %collective-permute-start.6 = (s32[1,4,2,3]{3,2,1,0:T(2,128)S(1)}, s32[1,4,2,3]{3,2,1,0:T(2,128)S(1)}, u32[]{:S(2)}, u32[]{:S(2)}) collective-permute-start(s32[1,4,2,3]{3,2,1,0:T(2,128)S(1)} %copy.16.pairs), channel_id=1, source_target_pairs={{0,26},{2,28},{4,30},{6,0},{8,2},{10,4},{12,6},{14,8},{16,10},{18,... | collective-permute-start | bytes 296 | tf_op jit(solution)/shard_map/ppermute | solution.py:210
  12.0 2.9 %collective-permute-start.5 = (s32[1,4,2,3]{3,2,1,0:T(2,128)S(1)}, s32[1,4,2,3]{3,2,1,0:T(2,128)S(1)}, u32[]{:S(2)}, u32[]{:S(2)}) collective-permute-start(s32[1,4,2,3]{3,2,1,0:T(2,128)S(1)} %copy.16.pairs), channel_id=1, source_target_pairs={{0,30},{2,0},{4,2},{6,4},{8,6},{10,8},{12,10},{14,12},{16,14},{18,... | collective-permute-start | bytes 296 | tf_op jit(solution)/shard_map/ppermute | solution.py:210
  12.6 17.5 %collective-permute-start.7 = (bf16[2,32,1024]{2,1,0:T(8,128)(2,1)}, bf16[2,32,1024]{2,1,0:T(8,128)(2,1)S(1)}, u32[]{:S(2)}, u32[]{:S(2)}) collective-permute-start(bf16[2,32,1024]{2,1,0:T(8,128)(2,1)} %refs_5_.3), channel_id=1, source_target_pairs={{2,0},{6,4},{10,8},{14,12},{18,16},{22,20},{26,24},{30,28},{3,1},{... | collective-permute-start | bytes 393224 | tf_op jit(solution)/shard_map/ppermute | solution.py:215
  13.9 18.9 %collective-permute-start.1 = (bf16[2,32,1024]{2,1,0:T(8,128)(2,1)}, bf16[2,32,1024]{2,1,0:T(8,128)(2,1)S(1)}, u32[]{:S(2)}, u32[]{:S(2)}) collective-permute-start(bf16[2,32,1024]{2,1,0:T(8,128)(2,1)} %refs_5_.4), channel_id=1, source_target_pairs={{0,8},{2,10},{4,12},{6,14},{8,16},{10,18},{12,20},{14,22},{16,24},... | collective-permute-start | bytes 393224 | tf_op jit(solution)/shard_map/ppermute | solution.py:210
  14.9 19.2 %collective-permute-start = (bf16[2,32,1024]{2,1,0:T(8,128)(2,1)}, bf16[2,32,1024]{2,1,0:T(8,128)(2,1)S(1)}, u32[]{:S(2)}, u32[]{:S(2)}) collective-permute-start(bf16[2,32,1024]{2,1,0:T(8,128)(2,1)} %refs_5_.4), channel_id=1, source_target_pairs={{0,4},{2,6},{4,8},{6,10},{8,12},{10,14},{12,16},{14,18},{16,20},{1... | collective-permute-start | bytes 393224 | tf_op jit(solution)/shard_map/ppermute | solution.py:210
  16.4 18.8 %collective-permute-start.11 = (bf16[2,32,1024]{2,1,0:T(8,128)(2,1)S(1)}, bf16[2,32,1024]{2,1,0:T(8,128)(2,1)S(1)}, u32[]{:S(2)}, u32[]{:S(2)}) collective-permute-start(bf16[2,32,1024]{2,1,0:T(8,128)(2,1)S(1)} %collective-permute-done.10.refs_3_), channel_id=1, source_target_pairs={{0,2},{4,6},{8,10},{12,14},{16,18},{20,22},{24,26},{28,30},{1,3},{... | collective-permute-start | bytes 393224 | tf_op jit(solution)/shard_map/ppermute | solution.py:215
  18.9 16.4 %collective-permute-start.9 = (bf16[2,32,1024]{2,1,0:T(8,128)(2,1)S(1)}, bf16[2,32,1024]{2,1,0:T(8,128)(2,1)S(1)}, u32[]{:S(2)}, u32[]{:S(2)}) collective-permute-start(bf16[2,32,1024]{2,1,0:T(8,128)(2,1)S(1)} %collective-permute-done.8.refs_2_), channel_id=1, source_target_pairs={{0,2},{2,0},{4,6},{6,4},{8,10},{10,8},{12,14},{14,12},{16,18},{18,... | collective-permute-start | bytes 393224 | tf_op jit(solution)/shard_map/ppermute | solution.py:215
  19.1 1.0 %copy-start = (bf16[512,512]{1,0:T(8,128)(2,1)S(1)}, bf16[512,512]{1,0:T(8,128)(2,1)}, u32[]{:S(2)}) copy-start(bf16[512,512]{1,0:T(8,128)(2,1)} %constant.45.clone.refs_11_.refs_13_.refs_10_.refs_12_.refs_14_) | copy-start | bytes 1572868
  20.1 1.0 %copy-start.2 = (bf16[512,512]{1,0:T(8,128)(2,1)S(1)}, bf16[512,512]{1,0:T(8,128)(2,1)}, u32[]{:S(2)}) copy-start(bf16[512,512]{1,0:T(8,128)(2,1)} %constant.44.clone.refs_10_.refs_12_.refs_9_.refs_11_.refs_13_) | copy-start | bytes 1572868
  21.2 1.0 %copy-start.4 = (bf16[512,512]{1,0:T(8,128)(2,1)S(1)}, bf16[512,512]{1,0:T(8,128)(2,1)}, u32[]{:S(2)}) copy-start(bf16[512,512]{1,0:T(8,128)(2,1)} %constant.43.clone.refs_9_.refs_8_.refs_10_) | copy-start | bytes 1572868
  22.2 1.0 %copy-start.6 = (bf16[512,512]{1,0:T(8,128)(2,1)S(1)}, bf16[512,512]{1,0:T(8,128)(2,1)}, u32[]{:S(2)}) copy-start(bf16[512,512]{1,0:T(8,128)(2,1)} %constant.42.clone.refs_8_.refs_7_.refs_9_) | copy-start | bytes 1572868
  23.3 1.0 %copy-start.8 = (bf16[512,512]{1,0:T(8,128)(2,1)S(1)}, bf16[512,512]{1,0:T(8,128)(2,1)}, u32[]{:S(2)}) copy-start(bf16[512,512]{1,0:T(8,128)(2,1)} %constant.41.clone.refs_7_.refs_6_.refs_8_) | copy-start | bytes 1572868
  24.3 1.0 %copy-start.10 = (bf16[512,512]{1,0:T(8,128)(2,1)S(1)}, bf16[512,512]{1,0:T(8,128)(2,1)}, u32[]{:S(2)}) copy-start(bf16[512,512]{1,0:T(8,128)(2,1)} %constant.40.clone.refs_6_.refs_5_.refs_7_) | copy-start | bytes 1572868
  25.4 0.9 %copy-start.12 = (f32[32,1024]{1,0:T(8,128)S(1)}, f32[32,1024]{1,0:T(8,128)}, u32[]{:S(2)}) copy-start(f32[32,1024]{1,0:T(8,128)} %constant.48.clone.refs_16_.refs_15_.refs_17_) | copy-start | bytes 393220
  26.3 0.8 %copy-start.14 = (bf16[128,128]{1,0:T(8,128)(2,1)S(1)}, bf16[128,128]{1,0:T(8,128)(2,1)}, u32[]{:S(2)}) copy-start(bf16[128,128]{1,0:T(8,128)(2,1)} %constant.46.clone.refs_14_.refs_13_.refs_15_) | copy-start | bytes 98308
  30.0 10.3 %copy-start.1 = (bf16[512,512]{1,0:T(8,128)(2,1)S(1)}, bf16[512,512]{1,0:T(8,128)(2,1)}, u32[]{:S(2)}) copy-start(bf16[512,512]{1,0:T(8,128)(2,1)} %constant.45.clone.refs_11_.refs_13_.refs_10_.refs_12_.refs_14_) | copy-start | bytes 1572868
  30.0 10.3 %copy-start.3 = (bf16[512,512]{1,0:T(8,128)(2,1)S(1)}, bf16[512,512]{1,0:T(8,128)(2,1)}, u32[]{:S(2)}) copy-start(bf16[512,512]{1,0:T(8,128)(2,1)} %constant.44.clone.refs_10_.refs_12_.refs_9_.refs_11_.refs_13_) | copy-start | bytes 1572868
  30.0 10.3 %copy-start.5 = (bf16[512,512]{1,0:T(8,128)(2,1)S(1)}, bf16[512,512]{1,0:T(8,128)(2,1)}, u32[]{:S(2)}) copy-start(bf16[512,512]{1,0:T(8,128)(2,1)} %constant.43.clone.refs_9_.refs_8_.refs_10_) | copy-start | bytes 1572868
  30.0 10.3 %copy-start.7 = (bf16[512,512]{1,0:T(8,128)(2,1)S(1)}, bf16[512,512]{1,0:T(8,128)(2,1)}, u32[]{:S(2)}) copy-start(bf16[512,512]{1,0:T(8,128)(2,1)} %constant.42.clone.refs_8_.refs_7_.refs_9_) | copy-start | bytes 1572868
  30.0 10.3 %copy-start.9 = (bf16[512,512]{1,0:T(8,128)(2,1)S(1)}, bf16[512,512]{1,0:T(8,128)(2,1)}, u32[]{:S(2)}) copy-start(bf16[512,512]{1,0:T(8,128)(2,1)} %constant.41.clone.refs_7_.refs_6_.refs_8_) | copy-start | bytes 1572868
  30.1 10.3 %copy-start.11 = (bf16[512,512]{1,0:T(8,128)(2,1)S(1)}, bf16[512,512]{1,0:T(8,128)(2,1)}, u32[]{:S(2)}) copy-start(bf16[512,512]{1,0:T(8,128)(2,1)} %constant.40.clone.refs_6_.refs_5_.refs_7_) | copy-start | bytes 1572868
  30.1 10.3 %copy-start.15 = (bf16[2,32,1024]{2,1,0:T(8,128)(2,1)S(1)}, bf16[2,32,1024]{2,1,0:T(8,128)(2,1)}, u32[]{:S(2)}) copy-start(bf16[2,32,1024]{2,1,0:T(8,128)(2,1)} %refs_5_.3) | copy-start | bytes 393220
  30.1 10.2 %collective-permute-start.2 = (bf16[2,32,1024]{2,1,0:T(8,128)(2,1)}, bf16[2,32,1024]{2,1,0:T(8,128)(2,1)S(1)}, u32[]{:S(2)}, u32[]{:S(2)}) collective-permute-start(bf16[2,32,1024]{2,1,0:T(8,128)(2,1)} %refs_5_.4), channel_id=1, source_target_pairs={{0,2},{4,6},{8,10},{12,14},{16,18},{20,22},{24,26},{28,30},{1,3},{... | collective-permute-start | bytes 393224 | tf_op jit(solution)/shard_map/ppermute | solution.py:215
  32.8 7.5 %collective-permute-start.4 = (bf16[2,32,1024]{2,1,0:T(8,128)(2,1)S(1)}, bf16[2,32,1024]{2,1,0:T(8,128)(2,1)S(1)}, u32[]{:S(2)}, u32[]{:S(2)}) collective-permute-start(bf16[2,32,1024]{2,1,0:T(8,128)(2,1)S(1)} %collective-permute-done.1.refs_1_), channel_id=1, source_target_pairs={{2,0},{6,4},{10,8},{14,12},{18,16},{22,20},{26,24},{30,28},{3,1},{... | collective-permute-start | bytes 393224 | tf_op jit(solution)/shard_map/ppermute | solution.py:215
  34.1 6.2 %collective-permute-start.3 = (bf16[2,32,1024]{2,1,0:T(8,128)(2,1)S(1)}, bf16[2,32,1024]{2,1,0:T(8,128)(2,1)S(1)}, u32[]{:S(2)}, u32[]{:S(2)}) collective-permute-start(bf16[2,32,1024]{2,1,0:T(8,128)(2,1)S(1)} %collective-permute-done.refs_0_), channel_id=1, source_target_pairs={{0,2},{2,0},{4,6},{6,4},{8,10},{10,8},{12,14},{14,12},{16,18},{18,... | collective-permute-start | bytes 393224 | tf_op jit(solution)/shard_map/ppermute | solution.py:215
  38.6 7.5 %collective-permute-start.14 = (f32[2,16,1024]{2,1,0:T(8,128)S(1)}, f32[2,16,1024]{2,1,0:T(8,128)S(1)}, u32[]{:S(2)}, u32[]{:S(2)}) collective-permute-start(f32[2,16,1024]{2,1,0:T(8,128)S(1)} %bitcast.4), channel_id=1, source_target_pairs={{0,1},{1,0},{2,3},{3,2},{4,5},{5,4},{6,7},{7,6},{8,9},{9,8},{10,11... | collective-permute-start | bytes 393224 | tf_op jit(solution)/shard_map/ppermute | solution.py:276

commit v2 on v0

v2 whole, which is shorter than its diff:
```python
import functools

import jax
import jax.numpy as jnp
import numpy as np
from jax import lax
from jax.experimental import pallas as pl
from jax.experimental.pallas import tpu as pltpu
from jax.sharding import PartitionSpec as P


@functools.lru_cache
def small_tables(edge, fields):
    index = np.arange(edge) + 1.0
    sine = np.sqrt(2.0 / (edge + 1)) * np.sin(np.pi * np.outer(index, index) / (edge + 1))
    eigen = 2.0 - 2.0 * np.cos(np.pi * index / (edge + 1))
    part = sine[::2, ::2]
    split = (eigen[::2], eigen[::-1][::2])
    plane = [np.add.outer(split[b], split[c]).reshape(-1) for b in (0, 1) for c in (0, 1)]
    lanes = max(edge * edge // 4, 2 * fields * edge)
    rows = [
        np.repeat(part, edge // 2, axis=1),
        np.tile(part, (1, edge // 2)),
        np.concatenate([np.tile(sine, (1, fields)), np.tile(eigen[:, None], (1, fields * edge))], axis=1),
        np.stack(plane),
        np.zeros((4, 1)),
    ]
    return np.concatenate([np.pad(r, ((0, 0), (0, lanes - r.shape[1]))) for r in rows]).astype(np.float32)


def make_tables(small, edge, fields, plane_table, along, inverse):
    part, lanes, rows = edge // 2, edge * edge // 4, fields * edge
    second = small[part : 2 * part, :lanes]
    for n in range(part):
        high, low = halves(small[n : n + 1, :lanes] * second)
        plane_table[n * part : (n + 1) * part, :] = high
        plane_table[lanes + n * part : lanes + (n + 1) * part, :] = low
    sine = jnp.concatenate([small[edge : 2 * edge, :rows]] * fields, axis=0)
    row = lax.broadcasted_iota(jnp.int32, (rows, rows), 0)
    column = lax.broadcasted_iota(jnp.int32, (rows, rows), 1)
    high, low = halves(jnp.where(row // edge == column // edge, sine, 0.0))
    along[:rows, :] = high
    along[rows:, :] = low
    eigen = small[edge : 2 * edge, rows : rows + 1]
    for q in range(4):
        plane = small[2 * edge + q : 2 * edge + q + 1, :lanes]
        inverse[:, q * lanes : (q + 1) * lanes] = 1.0 / (eigen + plane)


def fold_source(lane, edge):
    small = edge // 2
    point_c = lane % small
    point_b = (lane // small) % (edge // 4)
    quadrant = lane // (small * (edge // 4))
    b = jnp.where(quadrant < 2, 2 * point_b, small - 1 - 2 * point_b)
    c = jnp.where(quadrant % 2 == 0, 2 * point_c, edge - 1 - 2 * point_c)
    return b * edge + c


def fold_table(edge, transposed):
    lanes = edge * edge // 2
    dim = 0 if transposed else 1
    folded = fold_source(lax.broadcasted_iota(jnp.int32, (lanes, 1) if transposed else (1, lanes), dim), edge)
    plain = lax.broadcasted_iota(jnp.int32, (lanes, lanes), 1 - dim)
    return jnp.where(plain == folded, 1.0, 0.0).astype(jnp.bfloat16)


def tile_of(quadrant, half):
    return 2 * quadrant + (half if quadrant < 2 else 1 - half)


def dot(x, y):
    return jnp.dot(x, y, preferred_element_type=jnp.float32)


def halves(x):
    high = x.astype(jnp.bfloat16)
    return high, (x - high.astype(jnp.float32)).astype(jnp.bfloat16)


def times_table(x, table):
    x_high, x_low = halves(x)
    high, low = table[: table.shape[0] // 2], table[table.shape[0] // 2 :]
    return dot(x_high, high) + (dot(x_low, high) + dot(x_high, low))


def table_times(table, x):
    x_high, x_low = halves(x)
    high, low = table[: table.shape[0] // 2], table[table.shape[0] // 2 :]
    return dot(high, x_high) + (dot(high, x_low) + dot(low, x_high))


def spread(quadrants):
    a, b, c, d = quadrants
    return [a + b + (c + d), a - b + (c - d), a + b - (c + d), a - b - (c - d)]


def info_rows(steps, slots):
    return -(-(steps * slots * 3 + 2) // 16) * 16


def store_folded(fields, target):
    count, edge, plane = fields.shape
    half, lanes = plane // 2, plane // 8
    rows = [fields[i, :, h * half : (h + 1) * half] for i in range(count) for h in (0, 1)]
    folded = dot(jnp.concatenate(rows, axis=0), fold_table(edge, False)).astype(jnp.bfloat16)
    for i in range(count):
        for h in (0, 1):
            start = (2 * i + h) * edge
            for q in range(4):
                row = (tile_of(q, h) * count + i) * edge
                target[row : row + edge, :] = folded[start : start + edge, q * lanes : (q + 1) * lanes]


def pack_kernel(axes, residents, travellers, pairs, packed, moving, fields, moving_fields, entries_ref, sems):
    count, edge, plane = residents.shape
    load = pltpu.make_async_copy(residents, fields, sems.at[0])
    load_entries = pltpu.make_async_copy(pairs, entries_ref, sems.at[1])
    load_moving = pltpu.make_async_copy(travellers, moving_fields, sems.at[2])
    load.start()
    load_moving.start()
    load_entries.start()
    load_entries.wait()
    _, entries, slots, steps = pairs.shape
    row = lax.broadcasted_iota(jnp.int32, (info_rows(steps, slots), packed.shape[1]), 0)
    values = jnp.zeros(row.shape, jnp.int32)
    scalars = [entries_ref[0, e, p, s] for s in range(steps) for p in range(slots) for e in range(entries)]
    for k, value in enumerate([lax.axis_index(axes[0]) % 2, lax.axis_index(axes[1]), *scalars]):
        values = jnp.where(row == k, value, values)
    packed[8 * count * edge :, :] = values.astype(jnp.float32).astype(jnp.bfloat16)
    load.wait()
    store_folded(fields, packed)
    load_moving.wait()
    store_folded(moving_fields, moving)


def tables_kernel(count, small, plane_table, along, inverse):
    make_tables(small, inverse.shape[0], count, plane_table, along, inverse)


class Fields:
    def __init__(self, count, edge, *refs, near=None):
        self.count, self.edge, self.refs, self.near = count, edge, refs, near

    def rows(self, start, size):
        values = [ref[start : start + size, :].astype(jnp.float32) for ref in self.refs]
        return jnp.where(self.near, *values) if len(values) == 2 else values[0]

    def quadrants(self, i):
        tiles = [self.rows((t * self.count + i) * self.edge, self.edge) for t in range(8)]
        return [jnp.concatenate(tiles[2 * q : 2 * q + 2], axis=1) for q in range(4)]

    def info(self, count=None):
        start = 8 * self.count * self.edge
        return self.rows(start, self.refs[0].shape[0] - start)


def wide(row, edge, lanes):
    return jnp.broadcast_to(jnp.concatenate([row] * (lanes // row.shape[1]), axis=1), (edge, lanes))


def choose(fields, index):
    chosen = fields[0]
    for i in range(1, len(fields)):
        chosen = [jnp.where(index == i, new, old) for new, old in zip(fields[i], chosen)]
    return chosen


def slot_rows(info, arrival, slots):
    start = 2 + arrival * slots * 3
    return [info[start + 3 * p : start + 3 * p + 3] for p in range(slots)]


def gather_terms(slots, home, total, tables):
    plane_table, along, inverse = (table[...] for table in tables)
    edge = inverse.shape[0]
    rows = len(slots) * edge
    densities = []
    for moving, index, _ in slots:
        densities.append(spread([m * h for m, h in zip(moving, choose(home, index))]))
    field = jnp.concatenate([density[q] for q in range(4) for density in densities], axis=0)
    field = times_table(field, plane_table)
    field = jnp.concatenate([field[q * rows : (q + 1) * rows] for q in range(4)], axis=1)
    size = along.shape[0] // 2
    along = jnp.concatenate([along[:rows, :rows], along[size : size + rows, :rows]], axis=0)
    field = table_times(along, field)
    field = (field.reshape(len(slots), edge, -1) * inverse[None]).reshape(field.shape)
    field = table_times(along, field)
    lanes = field.shape[1] // 4
    field = jnp.concatenate([field[:, q * lanes : (q + 1) * lanes] for q in range(4)], axis=0)
    field = times_table(field, plane_table)
    for slot, (moving, index, active) in enumerate(slots):
        potential = spread([field[q * rows + slot * edge : q * rows + (slot + 1) * edge] for q in range(4)])
        terms = [active * p * m for p, m in zip(potential, moving)]
        for j in range(len(home)):
            total[j] = [old + jnp.where(index == j, new, 0.0) for old, new in zip(total[j], terms)]


def zero_total(home):
    return [[jnp.zeros_like(q) for q in field] for field in home]


def unfold(total, edge):
    table = fold_table(edge, True)
    lanes = edge * edge // 8
    stack = []
    for field in total:
        for h in (0, 1):
            tiles = [tile_of(q, h) for q in range(4)]
            stack.append(
                jnp.concatenate(
                    [field[t // 2][:, (t % 2) * lanes : (t % 2 + 1) * lanes] for t in tiles], axis=1
                )
            )
    high, low = halves(jnp.concatenate(stack, axis=0))
    plain = dot(high, table) + dot(low, table)
    return [
        jnp.concatenate([plain[2 * i * edge : (2 * i + 1) * edge], plain[(2 * i + 1) * edge : (2 * i + 2) * edge]], axis=1)
        for i in range(len(total))
    ]


def slots_of(block, info, near, arrivals, slots, entry):
    edge = block.edge
    fields = [block.quadrants(i) for i in range(block.count)]
    lanes = fields[0][0].shape[1]
    found = []
    for row, far in zip(slot_rows(info, arrivals[0], slots), slot_rows(info, arrivals[1], slots)):
        row = jnp.where(near, row, far)
        own, other, active = (wide(row[e : e + 1], edge, lanes) for e in (entry, 1 - entry, 2))
        found.append((choose(fields, own), other, active))
    return found


def terms_kernel(plan, accumulate, finish, slots, edge, for_travellers, *refs):
    blocks = sum(number for number, _ in plan)
    outputs = 2 if finish and for_travellers else 1
    refs, outs = refs[:-outputs], refs[-outputs:]
    moving, (own, home, *refs) = refs[:blocks], refs[blocks:]
    tables, early = refs[:3], refs[3:]
    held = home.shape[0] // (8 * edge)
    count = moving[0].shape[0] // (8 * edge)
    own = Fields(own.shape[0] // (8 * edge), edge, own).info()
    near = own[0:1] == (0 if for_travellers else 1)
    home = Fields(held, edge, home)
    home = [home.quadrants(j) for j in range(held)]
    found = []
    for number, arrivals in plan:
        block, moving = Fields(count, edge, *moving[:number], near=near), moving[number:]
        info = block.info() if for_travellers else own
        found += slots_of(block, info, near, arrivals, slots, 0 if for_travellers else 1)
    total = [[early[0][j, q] for q in range(4)] for j in range(held)] if accumulate else zero_total(home)
    gather_terms(found, home, total, tables)
    if not finish:
        for j, field in enumerate(total):
            for q in range(4):
                outs[0][j, q] = field[q]
        return
    total = unfold(total, edge)
    if not for_travellers:
        for j, field in enumerate(total):
            outs[0][j] = field
        return
    mine, others = outs
    rows = mine.shape[1]
    parts = edge // rows
    for j, field in enumerate(total):
        cuts = [[field[p * rows : (p + 1) * rows]] for p in range(parts)]
        for k in range(parts):
            group = wide(own[1:2], rows, field.shape[1]) + k
            group = jnp.where(group >= parts, group - parts, group)
            cut = choose(cuts, group)[0]
            if k == 0:
                mine[j] = cut
            else:
                others[k - 1, j] = cut


VMEM = pl.BlockSpec(memory_space=pltpu.VMEM)
HBM = pl.BlockSpec(memory_space=pl.ANY)
LIMIT = pltpu.CompilerParams(vmem_limit_bytes=32 * 1024 * 1024)
LIMIT_U = pltpu.CompilerParams(vmem_limit_bytes=60 * 1024 * 1024)
LIMIT_W = pltpu.CompilerParams(vmem_limit_bytes=32 * 1024 * 1024)


def cost(microseconds):
    return pl.CostEstimate(flops=int(microseconds * 1e9), bytes_accessed=1024, transcendentals=0)


def from_behind(value, by):
    peers = lax.axis_size("blk")
    return lax.ppermute(value, "blk", [(i, (i + by) % peers) for i in range(peers)])


def other_core(value):
    peers = lax.axis_size("blk")
    return lax.ppermute(value, "blk", [(i, i ^ 1) for i in range(peers)])


def local(residents, travellers, pair_list):
    count, edge, plane = residents.shape
    held = travellers.shape[0]
    steps, slots = pair_list.shape[1:3]
    direct = range(2, steps + 1, 2)
    arrivals = len(direct)
    groups = lax.axis_size("grp")
    part = edge // groups
    fields = 2 * arrivals * slots
    small = jnp.asarray(small_tables(edge, fields))

    packed, moving = pl.pallas_call(
        functools.partial(pack_kernel, ("blk", "grp")),
        out_shape=(
            jax.ShapeDtypeStruct((8 * count * edge + info_rows(steps, slots), plane // 8), jnp.bfloat16),
            jax.ShapeDtypeStruct((8 * held * edge, plane // 8), jnp.bfloat16),
        ),
        in_specs=[HBM, HBM, HBM],
        out_specs=(VMEM, VMEM),
        scratch_shapes=[
            pltpu.VMEM(residents.shape, jnp.bfloat16),
            pltpu.VMEM(travellers.shape, jnp.bfloat16),
            pltpu.SMEM((1, 3, slots, steps), jnp.int32),
            pltpu.SemaphoreType.DMA((3,)),
        ],
        compiler_params=LIMIT_U,
        cost_estimate=cost(1),
        name="pack",
    )(residents, travellers, jnp.transpose(pair_list, (0, 3, 2, 1)))
    tables = pl.pallas_call(
        functools.partial(tables_kernel, fields),
        out_shape=(
            jax.ShapeDtypeStruct((plane // 2, plane // 4), jnp.bfloat16),
            jax.ShapeDtypeStruct((2 * fields * edge, fields * edge), jnp.bfloat16),
            jax.ShapeDtypeStruct((edge, plane), jnp.float32),
        ),
        in_specs=[VMEM],
        out_specs=(VMEM,) * 3,
        compiler_params=LIMIT,
        cost_estimate=cost(20),
        name="tables",
    )(small)

    def stage(plan, operands, home, accumulate, finish, for_travellers, microseconds, name):
        number = home[1].shape[0] // (8 * edge)
        if not finish:
            out_shape = jax.ShapeDtypeStruct((number, 4, edge, plane // 4), jnp.float32)
        elif for_travellers:
            out_shape = (
                jax.ShapeDtypeStruct((number, part, plane), jnp.float32),
                jax.ShapeDtypeStruct((groups - 1, number, part, plane), jnp.float32),
            )
        else:
            out_shape = jax.ShapeDtypeStruct((number, edge, plane), jnp.float32)
        operands = (*operands, *home, *tables, *([] if accumulate is None else [accumulate]))
        return pl.pallas_call(
            functools.partial(terms_kernel, plan, accumulate is not None, finish, slots, edge, for_travellers),
            out_shape=out_shape,
            in_specs=[VMEM] * len(operands),
            out_specs=jax.tree.map(lambda _: VMEM, out_shape),
            compiler_params=LIMIT,
            cost_estimate=cost(microseconds),
            name=name,
        )(*operands)

    last = arrivals - 1

    def straight(k):
        return 1, (2 * k + 1, 2 * k + 1)

    middle = [(1, (2 * k + 2, 2 * k)) for k in range(last)]
    ends = [(2, (0, 2 * last))]

    res_moved = [from_behind(packed, -s) for s in direct]
    res_swapped = [other_core(packed)] + [other_core(value) for value in res_moved]
    trav_moved = [from_behind(moving, s) for s in direct]
    trav_swapped = [other_core(moving)]

    home = (packed, moving)
    early = stage(
        [straight(k) for k in range(last)] + middle,
        res_moved[:last] + res_swapped[1:-1],
        home,
        None,
        False,
        True,
        10,
        "early_traveller_terms",
    )
    mine, others = stage(
        [straight(last)] + ends,
        [res_moved[last], res_swapped[0], res_swapped[-1]],
        home,
        early,
        True,
        True,
        2,
        "late_traveller_terms",
    )
    trav_moved, mine, others = lax.optimization_barrier((trav_moved, mine, others))
    trav_swapped += [other_core(value) for value in trav_moved]
    sent = [
        lax.ppermute(others[k - 1], "grp", [(g, (g + k) % groups) for g in range(groups)])
        for k in range(1, groups)
    ]
    res_total = stage(
        [straight(k) for k in range(arrivals)] + middle + ends,
        [*trav_moved, *trav_swapped[1:-1], trav_swapped[0], trav_swapped[-1]],
        (packed, packed),
        None,
        True,
        False,
        0.5,
        "resident_terms",
    )
    res_total, sent = lax.optimization_barrier((res_total, sent))
    for value in sent:
        mine = mine + value
    return res_total, mine


def solution(mesh):
    return jax.shard_map(
        local,
        mesh=mesh,
        in_specs=(
            P(("blk", "grp"), None, None),
            P("blk", None, None),
            P(("blk", "grp"), None, None, None),
        ),
        out_specs=(P(("blk", "grp"), None, None), P("blk", "grp", None)),
        check_vma=False,
    )
```

time: 144 us -> 28.2 us (0.20); the launches traced: 141 us -> 28.1 us
  matrix products: 48.8 us -> 0 us
  waiting for transfers between devices: 39 us -> 5.22 us
  local copies, waits for them, and re-layouts: 20.8 us -> 0.01 us
  between operations: 15.3 us -> 0.71 us
  Pallas kernels: 0 us -> 10.7 us
  other arithmetic: 9.98 us -> 0.67 us
  starting transfers between devices: 7.5 us -> 10.7 us
    dot_general x32 -> x0, matrix products: 48.8 us -> none  [the longest x8 35.1 us: transform(): return jnp.einsum('nm,pam->pan', plane_table, field, precision=high)]
    unnamed x2 -> x0, waiting for transfers between devices: 19.7 us -> none
    mul x1 -> x0, local copies, waits for them, and re-layouts: 14.2 us -> none  [local(): plane_table = jnp.kron(table, table)]
    ppermute x8 -> x11, waiting for transfers between devices: 19.3 us -> 5.22 us  [the longest x4 5.2 us: from_behind(): lax.ppermute(value, 'blk', [(i, (i + by) % peers) for i in range(peers)])]
    pallas_call x0 -> x5, Pallas kernels: none -> 10.7 us  [the longest x3 8.43 us: stage(): pl.pallas_call(functools.partial(terms_kernel, plan, accumulate is not No...]
    mul x2 -> x0, other arithmetic: 8.11 us -> none  [the longest x1 7.97 us: local(): plane_table = jnp.kron(table, table)]
    unnamed x11 -> x6, local copies, waits for them, and re-layouts: 4.07 us -> 0.01 us
    ppermute x8 -> x11, starting transfers between devices: 7.47 us -> 10.7 us  [the longest x4 8.11 us: from_behind(): lax.ppermute(value, 'blk', [(i, (i + by) % peers) for i in range(peers)])]
  transfers between devices with their start and end apart: 9 -> 11, of which waited for: 6 -> 2; matrix products, arithmetic and copies ran while one was open for 45% -> 0% of each run, Pallas kernels for 0% -> 30%
where the time goes in v2:
time: 28.2 us; the launch traced here: 28.1 us
  Pallas kernels  10.7 us (38%)
  starting transfers between devices  10.7 us (38%)
  waiting for transfers between devices  5.22 us (19%)
  between operations  0.71 us (3%)
  other arithmetic  0.67 us (2%)
    pallas_call x3, Pallas kernels, stage(): pl.pallas_call(functools.partial(terms_kernel, plan, accumulate is not No...  8.43 us
    ppermute x4, starting transfers between devices, from_behind(): lax.ppermute(value, 'blk', [(i, (i + by) % peers) for i in range(peers)])  8.11 us
    ppermute x4, waiting for transfers between devices, from_behind(): lax.ppermute(value, 'blk', [(i, (i + by) % peers) for i in range(peers)])  5.2 us
    pallas_call x1, Pallas kernels, local(): pl.pallas_call(functools.partial(pack_kernel, ('blk', 'grp')), out_shape=...  2.16 us
    ppermute x1, starting transfers between devices, local(): lax.ppermute(others[k - 1], 'grp', [(g, (g + k) % groups) for g in range(...  1.52 us
    ppermute x6, starting transfers between devices, other_core(): return lax.ppermute(value, 'blk', [(i, i ^ 1) for i in range(peers)])  1.09 us
    add x1, other arithmetic, local(): mine = mine + value  0.67 us
  transfers between devices with their start and end apart: 11, of which 2 were waited for; matrix products, arithmetic and copies ran while one was open for 0% of the time, Pallas kernels for 30%

profile of v2, /device:TPU:0, one launch (start us, length us, event | category | flops | bytes accessed | tf_op | source)
XLA Modules:
  0.0 28.1 jit_solution(16533503281031951280)
XLA Ops:
  0.6 0.0 copy-start.2
  0.6 2.2 %pack.1 = (bf16[544,128]{1,0:T(8,128)(2,1)}, bf16[512,128]{1,0:T(8,128)(2,1)}) custom-call(bf16[2,32,1024]{2,1,0:T(8,128)(2,1)} %residents.1, bf16[2,32,1024]{2,1,0:T(8,128)(2,1)} %travellers.1, s32[1,3,2,4]{3,2,1,0:T(2,128)} %bitcast.3), custom_call_target="tpu_custom_call" | custom-call | flops 1000000000 | bytes 1024 | tf_op jit(solution)/shard_map/pack/pallas_call | solution.py:311
  2.8 6.0 %collective-permute-start.5 = (bf16[544,128]{1,0:T(8,128)(2,1)}, bf16[544,128]{1,0:T(8,128)(2,1)S(1)}, u32[]{:S(2)}, u32[]{:S(2)}) collective-permute-start(bf16[544,128]{1,0:T(8,128)(2,1)} %get-tuple-element.16.refs_2_.refs_3_.refs_5_.refs_6_), channel_id=1, source_target_pairs={{0,28},{2,30},{4,0},{6,2},{8,4},{10,6},{12,8},{14,10},{16,12},{18,... | collective-permute-start | bytes 417800 | tf_op jit(solution)/shard_map/ppermute | solution.py:292
  8.8 0.5 %collective-permute-start.2 = (bf16[544,128]{1,0:T(8,128)(2,1)}, bf16[544,128]{1,0:T(8,128)(2,1)S(1)}, u32[]{:S(2)}, u32[]{:S(2)}) collective-permute-start(bf16[544,128]{1,0:T(8,128)(2,1)} %get-tuple-element.16.refs_2_.refs_3_.refs_5_.refs_6_), channel_id=1, source_target_pairs={{0,24},{2,26},{4,28},{6,30},{8,0},{10,2},{12,4},{14,6},{16,8},{18,... | collective-permute-start | bytes 417800 | tf_op jit(solution)/shard_map/ppermute | solution.py:292
  9.3 0.0 collective-permute-start.3
  9.3 0.6 %collective-permute-start = (bf16[512,128]{1,0:T(8,128)(2,1)}, bf16[512,128]{1,0:T(8,128)(2,1)S(1)}, u32[]{:S(2)}, u32[]{:S(2)}) collective-permute-start(bf16[512,128]{1,0:T(8,128)(2,1)} %get-tuple-element.15.refs_3_.refs_4_), channel_id=1, source_target_pairs={{0,4},{2,6},{4,8},{6,10},{8,12},{10,14},{12,16},{14,18},{16,20},{1... | collective-permute-start | bytes 393224 | tf_op jit(solution)/shard_map/ppermute | solution.py:292
  9.9 1.0 %collective-permute-start.1 = (bf16[512,128]{1,0:T(8,128)(2,1)}, bf16[512,128]{1,0:T(8,128)(2,1)S(1)}, u32[]{:S(2)}, u32[]{:S(2)}) collective-permute-start(bf16[512,128]{1,0:T(8,128)(2,1)} %get-tuple-element.15.refs_3_.refs_4_), channel_id=1, source_target_pairs={{0,8},{2,10},{4,12},{6,14},{8,16},{10,18},{12,20},{14,22},{16,24},... | collective-permute-start | bytes 393224 | tf_op jit(solution)/shard_map/ppermute | solution.py:292
  10.9 2.3 %collective-permute-done.5.refs_0_ = bf16[544,128]{1,0:T(8,128)(2,1)S(1)} collective-permute-done((bf16[544,128]{1,0:T(8,128)(2,1)}, bf16[544,128]{1,0:T(8,128)(2,1)S(1)}, u32[]{:S(2)}, u32[]{:S(2)}) %collective-permute-start.5) | collective-permute-done | bytes 139296 | tf_op jit(solution)/shard_map/ppermute | solution.py:292
  13.3 0.0 collective-permute-start.6
  13.3 0.0 copy-done.2
  13.3 0.1 tables.1
  13.4 2.9 %collective-permute-done.2.refs_0_ = bf16[544,128]{1,0:T(8,128)(2,1)S(1)} collective-permute-done((bf16[544,128]{1,0:T(8,128)(2,1)}, bf16[544,128]{1,0:T(8,128)(2,1)S(1)}, u32[]{:S(2)}, u32[]{:S(2)}) %collective-permute-start.2) | collective-permute-done | bytes 139296 | tf_op jit(solution)/shard_map/ppermute | solution.py:292
  16.3 0.0 copy-done.1
  16.3 0.0 collective-permute-start.8
  16.3 0.0 collective-permute-done.6.refs_1_
  16.3 0.5 %collective-permute-start.4 = (bf16[544,128]{1,0:T(8,128)(2,1)S(1)}, bf16[544,128]{1,0:T(8,128)(2,1)S(1)}, u32[]{:S(2)}, u32[]{:S(2)}) collective-permute-start(bf16[544,128]{1,0:T(8,128)(2,1)S(1)} %collective-permute-done.2.refs_0_), channel_id=1, source_target_pairs={{0,2},{2,0},{4,6},{6,4},{8,10},{10,8},{12,14},{14,12},{16,18},{18,... | collective-permute-start | bytes 417800 | tf_op jit(solution)/shard_map/ppermute | solution.py:297
  16.8 0.0 copy-done
  16.8 1.8 %early_traveller_terms.1.refs_8_ = f32[2,4,32,256]{3,2,1,0:T(8,128)S(1)} custom-call(bf16[544,128]{1,0:T(8,128)(2,1)S(1)} %collective-permute-done.5.refs_0_, bf16[544,128]{1,0:T(8,128)(2,1)S(1)} %collective-permute-done.6.refs_1_, bf16[544,128]{1,0:T(8,128)(2,1)S(1)} %copy-done, bf16[512,128]{1,0:T(8,128)(2,1)S(1)} %copy-done.1, ...), custom_call_target="tpu_custom_call" | custom-call | flops 10000000000 | bytes 1024 | tf_op jit(solution)/shard_map/early_traveller_terms/pallas_call | solution.py:355
  18.5 0.0 collective-permute-done.3.refs_1_
  18.6 0.0 collective-permute-done.4.refs_2_
  18.6 2.4 %late_traveller_terms.1 = (f32[2,16,1024]{2,1,0:T(8,128)S(1)}, f32[1,2,16,1024]{3,2,1,0:T(8,128)S(1)}) custom-call(bf16[544,128]{1,0:T(8,128)(2,1)S(1)} %collective-permute-done.2.refs_0_, bf16[544,128]{1,0:T(8,128)(2,1)S(1)} %collective-permute-done.3.refs_1_, bf16[544,128]{1,0:T(8,128)(2,1)S(1)} %collective-permute-done.4.refs_2_, ...), custom_call_target="tpu_custom_call" | custom-call | flops 2000000000 | bytes 1024 | tf_op jit(solution)/shard_map/late_traveller_terms/pallas_call | solution.py:355
  21.0 0.0 collective-permute-done.refs_0_
  21.0 0.0 collective-permute-done.1.refs_1_
  21.0 0.1 collective-permute-start.7
  21.1 0.4 %collective-permute-start.9 = (bf16[512,128]{1,0:T(8,128)(2,1)S(1)}, bf16[512,128]{1,0:T(8,128)(2,1)S(1)}, u32[]{:S(2)}, u32[]{:S(2)}) collective-permute-start(bf16[512,128]{1,0:T(8,128)(2,1)S(1)} %collective-permute-done.1.refs_1_), channel_id=1, source_target_pairs={{0,2},{2,0},{4,6},{6,4},{8,10},{10,8},{12,14},{14,12},{16,18},{18,... | collective-permute-start | bytes 393224 | tf_op jit(solution)/shard_map/ppermute | solution.py:297
  21.5 1.5 %collective-permute-start.10 = (f32[2,16,1024]{2,1,0:T(8,128)S(1)}, f32[2,16,1024]{2,1,0:T(8,128)S(1)}, u32[]{:S(2)}, u32[]{:S(2)}) collective-permute-start(f32[2,16,1024]{2,1,0:T(8,128)S(1)} %bitcast.2), channel_id=1, source_target_pairs={{0,1},{1,0},{2,3},{3,2},{4,5},{5,4},{6,7},{7,6},{8,9},{9,8},{10,11... | collective-permute-start | bytes 393224 | tf_op jit(solution)/shard_map/ppermute | solution.py:402
  23.1 0.0 collective-permute-done.8.refs_3_
  23.1 0.0 collective-permute-done.7.refs_2_
  23.1 0.0 collective-permute-done.9.refs_4_
  23.1 4.3 %resident_terms.1 = f32[2,32,1024]{2,1,0:T(8,128)} custom-call(bf16[512,128]{1,0:T(8,128)(2,1)S(1)} %collective-permute-done.refs_0_, bf16[512,128]{1,0:T(8,128)(2,1)S(1)} %collective-permute-done.1.refs_1_, bf16[512,128]{1,0:T(8,128)(2,1)S(1)} %collective-permute-done.7.refs_2_, bf16[512,128]{1,0:T(8,128)(2,1)S(1)} %collective-permute-done.8.refs_3_, ...), custom_call_target="tpu_custom_call" | custom-call | flops 500000000 | bytes 1024 | tf_op jit(solution)/shard_map/resident_terms/pallas_call | solution.py:355
  27.4 0.0 collective-permute-done.10
  27.4 0.7 %add.3 = f32[2,16,1024]{2,1,0:T(8,128)} add(f32[2,16,1024]{2,1,0:T(8,128)S(1)} %get-tuple-element.26, f32[2,16,1024]{2,1,0:T(8,128)S(1)} %collective-permute-done.10) | non-fusion elementwise | flops 32768 | bytes 393216 | tf_op jit(solution)/shard_map/add | solution.py:417
  (2 shorter events, 0.0 us)
Async XLA Ops:
  0.6 12.7 %copy-start.2 = (f32[72,512]{1,0:T(8,128)S(1)}, f32[72,512]{1,0:T(8,128)}, u32[]{:S(2)}) copy-start(f32[72,512]{1,0:T(8,128)} %constant.2.clone.small) | copy-start | bytes 442372
  2.8 10.5 %collective-permute-start.5 = (bf16[544,128]{1,0:T(8,128)(2,1)}, bf16[544,128]{1,0:T(8,128)(2,1)S(1)}, u32[]{:S(2)}, u32[]{:S(2)}) collective-permute-start(bf16[544,128]{1,0:T(8,128)(2,1)} %get-tuple-element.16.refs_2_.refs_3_.refs_5_.refs_6_), channel_id=1, source_target_pairs={{0,28},{2,30},{4,0},{6,2},{8,4},{10,6},{12,8},{14,10},{16,12},{18,... | collective-permute-start | bytes 417800 | tf_op jit(solution)/shard_map/ppermute | solution.py:292
  8.8 7.4 %collective-permute-start.2 = (bf16[544,128]{1,0:T(8,128)(2,1)}, bf16[544,128]{1,0:T(8,128)(2,1)S(1)}, u32[]{:S(2)}, u32[]{:S(2)}) collective-permute-start(bf16[544,128]{1,0:T(8,128)(2,1)} %get-tuple-element.16.refs_2_.refs_3_.refs_5_.refs_6_), channel_id=1, source_target_pairs={{0,24},{2,26},{4,28},{6,30},{8,0},{10,2},{12,4},{14,6},{16,8},{18,... | collective-permute-start | bytes 417800 | tf_op jit(solution)/shard_map/ppermute | solution.py:292
  9.3 9.3 %collective-permute-start.3 = (bf16[544,128]{1,0:T(8,128)(2,1)}, bf16[544,128]{1,0:T(8,128)(2,1)S(1)}, u32[]{:S(2)}, u32[]{:S(2)}) collective-permute-start(bf16[544,128]{1,0:T(8,128)(2,1)} %get-tuple-element.16.refs_2_.refs_3_.refs_5_.refs_6_), channel_id=1, source_target_pairs={{0,2},{2,0},{4,6},{6,4},{8,10},{10,8},{12,14},{14,12},{16,18},{18,... | collective-permute-start | bytes 417800 | tf_op jit(solution)/shard_map/ppermute | solution.py:297
  9.3 7.0 %copy-start.1 = (bf16[512,128]{1,0:T(8,128)(2,1)S(1)}, bf16[512,128]{1,0:T(8,128)(2,1)}, u32[]{:S(2)}) copy-start(bf16[512,128]{1,0:T(8,128)(2,1)} %get-tuple-element.15.refs_3_.refs_4_) | copy-start | bytes 393220
  9.3 7.5 %copy-start = (bf16[544,128]{1,0:T(8,128)(2,1)S(1)}, bf16[544,128]{1,0:T(8,128)(2,1)}, u32[]{:S(2)}) copy-start(bf16[544,128]{1,0:T(8,128)(2,1)} %get-tuple-element.16.refs_2_.refs_3_.refs_5_.refs_6_) | copy-start | bytes 417796
  9.3 11.7 %collective-permute-start = (bf16[512,128]{1,0:T(8,128)(2,1)}, bf16[512,128]{1,0:T(8,128)(2,1)S(1)}, u32[]{:S(2)}, u32[]{:S(2)}) collective-permute-start(bf16[512,128]{1,0:T(8,128)(2,1)} %get-tuple-element.15.refs_3_.refs_4_), channel_id=1, source_target_pairs={{0,4},{2,6},{4,8},{6,10},{8,12},{10,14},{12,16},{14,18},{16,20},{1... | collective-permute-start | bytes 393224 | tf_op jit(solution)/shard_map/ppermute | solution.py:292
  9.9 11.0 %collective-permute-start.1 = (bf16[512,128]{1,0:T(8,128)(2,1)}, bf16[512,128]{1,0:T(8,128)(2,1)S(1)}, u32[]{:S(2)}, u32[]{:S(2)}) collective-permute-start(bf16[512,128]{1,0:T(8,128)(2,1)} %get-tuple-element.15.refs_3_.refs_4_), channel_id=1, source_target_pairs={{0,8},{2,10},{4,12},{6,14},{8,16},{10,18},{12,20},{14,22},{16,24},... | collective-permute-start | bytes 393224 | tf_op jit(solution)/shard_map/ppermute | solution.py:292
  13.3 3.0 %collective-permute-start.6 = (bf16[544,128]{1,0:T(8,128)(2,1)S(1)}, bf16[544,128]{1,0:T(8,128)(2,1)S(1)}, u32[]{:S(2)}, u32[]{:S(2)}) collective-permute-start(bf16[544,128]{1,0:T(8,128)(2,1)S(1)} %collective-permute-done.5.refs_0_), channel_id=1, source_target_pairs={{0,2},{2,0},{4,6},{6,4},{8,10},{10,8},{12,14},{14,12},{16,18},{18,... | collective-permute-start | bytes 417800 | tf_op jit(solution)/shard_map/ppermute | solution.py:297
  16.3 6.8 %collective-permute-start.8 = (bf16[512,128]{1,0:T(8,128)(2,1)S(1)}, bf16[512,128]{1,0:T(8,128)(2,1)S(1)}, u32[]{:S(2)}, u32[]{:S(2)}) collective-permute-start(bf16[512,128]{1,0:T(8,128)(2,1)S(1)} %copy-done.1), channel_id=1, source_target_pairs={{0,2},{2,0},{4,6},{6,4},{8,10},{10,8},{12,14},{14,12},{16,18},{18,... | collective-permute-start | bytes 393224 | tf_op jit(solution)/shard_map/ppermute | solution.py:297
  16.3 2.3 %collective-permute-start.4 = (bf16[544,128]{1,0:T(8,128)(2,1)S(1)}, bf16[544,128]{1,0:T(8,128)(2,1)S(1)}, u32[]{:S(2)}, u32[]{:S(2)}) collective-permute-start(bf16[544,128]{1,0:T(8,128)(2,1)S(1)} %collective-permute-done.2.refs_0_), channel_id=1, source_target_pairs={{0,2},{2,0},{4,6},{6,4},{8,10},{10,8},{12,14},{14,12},{16,18},{18,... | collective-permute-start | bytes 417800 | tf_op jit(solution)/shard_map/ppermute | solution.py:297
  21.0 2.1 %collective-permute-start.7 = (bf16[512,128]{1,0:T(8,128)(2,1)S(1)}, bf16[512,128]{1,0:T(8,128)(2,1)S(1)}, u32[]{:S(2)}, u32[]{:S(2)}) collective-permute-start(bf16[512,128]{1,0:T(8,128)(2,1)S(1)} %collective-permute-done.refs_0_), channel_id=1, source_target_pairs={{0,2},{2,0},{4,6},{6,4},{8,10},{10,8},{12,14},{14,12},{16,18},{18,... | collective-permute-start | bytes 393224 | tf_op jit(solution)/shard_map/ppermute | solution.py:297
  21.1 2.0 %collective-permute-start.9 = (bf16[512,128]{1,0:T(8,128)(2,1)S(1)}, bf16[512,128]{1,0:T(8,128)(2,1)S(1)}, u32[]{:S(2)}, u32[]{:S(2)}) collective-permute-start(bf16[512,128]{1,0:T(8,128)(2,1)S(1)} %collective-permute-done.1.refs_1_), channel_id=1, source_target_pairs={{0,2},{2,0},{4,6},{6,4},{8,10},{10,8},{12,14},{14,12},{16,18},{18,... | collective-permute-start | bytes 393224 | tf_op jit(solution)/shard_map/ppermute | solution.py:297
  21.5 5.8 %collective-permute-start.10 = (f32[2,16,1024]{2,1,0:T(8,128)S(1)}, f32[2,16,1024]{2,1,0:T(8,128)S(1)}, u32[]{:S(2)}, u32[]{:S(2)}) collective-permute-start(f32[2,16,1024]{2,1,0:T(8,128)S(1)} %bitcast.2), channel_id=1, source_target_pairs={{0,1},{1,0},{2,3},{3,2},{4,5},{5,4},{6,7},{7,6},{8,9},{9,8},{10,11... | collective-permute-start | bytes 393224 | tf_op jit(solution)/shard_map/ppermute | solution.py:402

commit v3 on v2

--- a/solution.py
+++ b/solution.py
@@ -87,7 +87,9 @@
 def table_times(table, x):
     x_high, x_low = halves(x)
     high, low = table[: table.shape[0] // 2], table[table.shape[0] // 2 :]
-    return dot(high, x_high) + (dot(high, x_low) + dot(low, x_high))
+    return dot(
+        jnp.concatenate([high, high, low], axis=1), jnp.concatenate([x_high, x_low, x_high], axis=0)
+    )
 
 
 def spread(quadrants):
@@ -99,11 +101,11 @@
     return -(-(steps * slots * 3 + 2) // 16) * 16
 
 
-def store_folded(fields, target):
+def store_folded(fields, table, target):
     count, edge, plane = fields.shape
     half, lanes = plane // 2, plane // 8
     rows = [fields[i, :, h * half : (h + 1) * half] for i in range(count) for h in (0, 1)]
-    folded = dot(jnp.concatenate(rows, axis=0), fold_table(edge, False)).astype(jnp.bfloat16)
+    folded = dot(jnp.concatenate(rows, axis=0), table).astype(jnp.bfloat16)
     for i in range(count):
         for h in (0, 1):
             start = (2 * i + h) * edge
@@ -112,14 +114,16 @@
                 target[row : row + edge, :] = folded[start : start + edge, q * lanes : (q + 1) * lanes]
 
 
-def pack_kernel(axes, residents, travellers, pairs, packed, moving, fields, moving_fields, entries_ref, sems):
+def pack_kernel(axes, residents, travellers, pairs, packed, moving, fields, moving_fields, entries_ref, folded, moving_folded, sems):
     count, edge, plane = residents.shape
-    load = pltpu.make_async_copy(residents, fields, sems.at[0])
+    loads = [pltpu.make_async_copy(residents.at[i], fields.at[i], sems.at[5 + i]) for i in range(count)]
     load_entries = pltpu.make_async_copy(pairs, entries_ref, sems.at[1])
     load_moving = pltpu.make_async_copy(travellers, moving_fields, sems.at[2])
-    load.start()
+    for load in loads:
+        load.start()
+    load_entries.start()
     load_moving.start()
-    load_entries.start()
+    table = fold_table(edge, False)
     load_entries.wait()
     _, entries, slots, steps = pairs.shape
     row = lax.broadcasted_iota(jnp.int32, (info_rows(steps, slots), packed.shape[1]), 0)
@@ -127,11 +131,18 @@
     scalars = [entries_ref[0, e, p, s] for s in range(steps) for p in range(slots) for e in range(entries)]
     for k, value in enumerate([lax.axis_index(axes[0]) % 2, lax.axis_index(axes[1]), *scalars]):
         values = jnp.where(row == k, value, values)
-    packed[8 * count * edge :, :] = values.astype(jnp.float32).astype(jnp.bfloat16)
-    load.wait()
-    store_folded(fields, packed)
+    folded[8 * count * edge :, :] = values.astype(jnp.float32).astype(jnp.bfloat16)
+    for load in loads:
+        load.wait()
+    store_folded(fields, table, folded)
+    store = pltpu.make_async_copy(folded, packed, sems.at[3])
+    store.start()
     load_moving.wait()
-    store_folded(moving_fields, moving)
+    store_folded(moving_fields, table, moving_folded)
+    store_moving = pltpu.make_async_copy(moving_folded, moving, sems.at[4])
+    store_moving.start()
+    store.wait()
+    store_moving.wait()
 
 
 def tables_kernel(count, small, plane_table, along, inverse):
@@ -200,11 +211,11 @@
     return [[jnp.zeros_like(q) for q in field] for field in home]
 
 
-def unfold(total, edge):
-    table = fold_table(edge, True)
-    lanes = edge * edge // 8
+def unfold(fields, table):
+    rows = fields[0][0].shape[0]
+    lanes = table.shape[0] // 4
     stack = []
-    for field in total:
+    for field in fields:
         for h in (0, 1):
             tiles = [tile_of(q, h) for q in range(4)]
             stack.append(
@@ -215,8 +226,8 @@
     high, low = halves(jnp.concatenate(stack, axis=0))
     plain = dot(high, table) + dot(low, table)
     return [
-        jnp.concatenate([plain[2 * i * edge : (2 * i + 1) * edge], plain[(2 * i + 1) * edge : (2 * i + 2) * edge]], axis=1)
-        for i in range(len(total))
+        jnp.concatenate([plain[k * rows : (k + 1) * rows] for k in (2 * i, 2 * i + 1)], axis=1)
+        for i in range(len(fields))
     ]
 
 
@@ -232,12 +243,12 @@
     return found
 
 
-def terms_kernel(plan, accumulate, finish, slots, edge, for_travellers, *refs):
+def terms_kernel(plan, accumulate, cut, slots, edge, for_travellers, after, *refs):
+    outputs = 2 if cut else 1
+    refs, outs = refs[: len(refs) - outputs - after], refs[-outputs:]
     blocks = sum(number for number, _ in plan)
-    outputs = 2 if finish and for_travellers else 1
-    refs, outs = refs[:-outputs], refs[-outputs:]
     moving, (own, home, *refs) = refs[:blocks], refs[blocks:]
-    tables, early = refs[:3], refs[3:]
+    tables, before = refs[:3], refs[3:]
     held = home.shape[0] // (8 * edge)
     count = moving[0].shape[0] // (8 * edge)
     own = Fields(own.shape[0] // (8 * edge), edge, own).info()
@@ -249,31 +260,48 @@
         block, moving = Fields(count, edge, *moving[:number], near=near), moving[number:]
         info = block.info() if for_travellers else own
         found += slots_of(block, info, near, arrivals, slots, 0 if for_travellers else 1)
-    total = [[early[0][j, q] for q in range(4)] for j in range(held)] if accumulate else zero_total(home)
-    gather_terms(found, home, total, tables)
-    if not finish:
+    total = [[before[0][j, q] for q in range(4)] for j in range(held)] if accumulate else zero_total(home)
+    group = 2 * slots
+    for start in range(0, len(found), group):
+        gather_terms(found[start : start + group], home, total, tables)
+    if not cut:
         for j, field in enumerate(total):
             for q in range(4):
                 outs[0][j, q] = field[q]
         return
-    total = unfold(total, edge)
-    if not for_travellers:
+    mine, others = outs
+    rows = mine.shape[2]
+    parts = edge // rows
+    for k in range(parts):
+        group = wide(own[1:2], rows, home[0][0].shape[1]) + k
+        group = jnp.where(group >= parts, group - parts, group)
         for j, field in enumerate(total):
-            outs[0][j] = field
-        return
-    mine, others = outs
-    rows = mine.shape[1]
-    parts = edge // rows
-    for j, field in enumerate(total):
-        cuts = [[field[p * rows : (p + 1) * rows]] for p in range(parts)]
-        for k in range(parts):
-            group = wide(own[1:2], rows, field.shape[1]) + k
-            group = jnp.where(group >= parts, group - parts, group)
-            cut = choose(cuts, group)[0]
-            if k == 0:
-                mine[j] = cut
-            else:
-                others[k - 1, j] = cut
+            cuts = [[q[p * rows : (p + 1) * rows] for q in field] for p in range(parts)]
+            for q, piece in enumerate(choose(cuts, group)):
+                if k == 0:
+                    mine[j, q] = piece
+                else:
+                    others[k - 1, j, q] = piece
+
+
+def unfold_table_kernel(edge, _, table):
+    table[...] = fold_table(edge, True)
+
+
+def gate_kernel(_, out):
+    out[...] = jnp.zeros_like(out)
+
+
+def sum_kernel(number, *refs):
+    parts, (table, terms, trav_total, res_total) = refs[:number], refs[number:]
+    fields = [[terms[j, q] for q in range(4)] for j in range(terms.shape[0])]
+    for j, field in enumerate(unfold(fields, table[...])):
+        res_total[j] = field
+    total = []
+    for j in range(parts[0].shape[0]):
+        total.append([sum((part[j, q] for part in parts[1:]), parts[0][j, q]) for q in range(4)])
+    for j, field in enumerate(unfold(total, table[...])):
+        trav_total[j] = field
 
 
 VMEM = pl.BlockSpec(memory_space=pltpu.VMEM)
@@ -305,22 +333,24 @@
     arrivals = len(direct)
     groups = lax.axis_size("grp")
     part = edge // groups
-    fields = 2 * arrivals * slots
+    fields = 2 * slots
     small = jnp.asarray(small_tables(edge, fields))
 
+    shapes = (
+        (8 * count * edge + info_rows(steps, slots), plane // 8),
+        (8 * held * edge, plane // 8),
+    )
     packed, moving = pl.pallas_call(
         functools.partial(pack_kernel, ("blk", "grp")),
-        out_shape=(
-            jax.ShapeDtypeStruct((8 * count * edge + info_rows(steps, slots), plane // 8), jnp.bfloat16),
-            jax.ShapeDtypeStruct((8 * held * edge, plane // 8), jnp.bfloat16),
-        ),
+        out_shape=tuple(jax.ShapeDtypeStruct(shape, jnp.bfloat16) for shape in shapes),
         in_specs=[HBM, HBM, HBM],
-        out_specs=(VMEM, VMEM),
+        out_specs=(HBM, HBM),
         scratch_shapes=[
             pltpu.VMEM(residents.shape, jnp.bfloat16),
             pltpu.VMEM(travellers.shape, jnp.bfloat16),
             pltpu.SMEM((1, 3, slots, steps), jnp.int32),
-            pltpu.SemaphoreType.DMA((3,)),
+            *(pltpu.VMEM(shape, jnp.bfloat16) for shape in shapes),
+            pltpu.SemaphoreType.DMA((5 + count,)),
         ],
         compiler_params=LIMIT_U,
         cost_estimate=cost(1),
@@ -340,27 +370,27 @@
         name="tables",
     )(small)
 
-    def stage(plan, operands, home, accumulate, finish, for_travellers, microseconds, name):
+    def stage(plan, blocks, home, total, for_travellers, microseconds, name, cut=False, after=()):
         number = home[1].shape[0] // (8 * edge)
-        if not finish:
-            out_shape = jax.ShapeDtypeStruct((number, 4, edge, plane // 4), jnp.float32)
-        elif for_travellers:
+        if cut:
             out_shape = (
-                jax.ShapeDtypeStruct((number, part, plane), jnp.float32),
-                jax.ShapeDtypeStruct((groups - 1, number, part, plane), jnp.float32),
+                jax.ShapeDtypeStruct((number, 4, part, plane // 4), jnp.float32),
+                jax.ShapeDtypeStruct((groups - 1, number, 4, part, plane // 4), jnp.float32),
             )
         else:
-            out_shape = jax.ShapeDtypeStruct((number, edge, plane), jnp.float32)
-        operands = (*operands, *home, *tables, *([] if accumulate is None else [accumulate]))
+            out_shape = jax.ShapeDtypeStruct((number, 4, edge, plane // 4), jnp.float32)
+        operands = (*blocks, *home, *tables) + (() if total is None else (total,))
         return pl.pallas_call(
-            functools.partial(terms_kernel, plan, accumulate is not None, finish, slots, edge, for_travellers),
+            functools.partial(
+                terms_kernel, plan, total is not None, cut, slots, edge, for_travellers, len(after)
+            ),
             out_shape=out_shape,
-            in_specs=[VMEM] * len(operands),
+            in_specs=[VMEM] * (len(operands) + len(after)),
             out_specs=jax.tree.map(lambda _: VMEM, out_shape),
             compiler_params=LIMIT,
             cost_estimate=cost(microseconds),
             name=name,
-        )(*operands)
+        )(*operands, *after)
 
     last = arrivals - 1
 
@@ -375,28 +405,35 @@
     trav_moved = [from_behind(moving, s) for s in direct]
     trav_swapped = [other_core(moving)]
 
+    unfolding = pl.pallas_call(
+        functools.partial(unfold_table_kernel, edge),
+        out_shape=jax.ShapeDtypeStruct((plane // 2, plane // 2), jnp.bfloat16),
+        in_specs=[HBM],
+        out_specs=VMEM,
+        compiler_params=LIMIT,
+        cost_estimate=cost(20),
+        name="unfold_table",
+    )(res_moved[0])
+
     home = (packed, moving)
-    early = stage(
-        [straight(k) for k in range(last)] + middle,
-        res_moved[:last] + res_swapped[1:-1],
-        home,
-        None,
-        False,
-        True,
-        10,
-        "early_traveller_terms",
-    )
-    mine, others = stage(
-        [straight(last)] + ends,
-        [res_moved[last], res_swapped[0], res_swapped[-1]],
-        home,
-        early,
-        True,
-        True,
-        2,
-        "late_traveller_terms",
-    )
-    trav_moved, mine, others = lax.optimization_barrier((trav_moved, mine, others))
+    blocks = [res_moved[last], res_swapped[0], res_swapped[-1]]
+    total = stage([straight(last)] + ends, blocks, home, None, True, 10, "early_traveller_terms")
+    for k in range(last):
+        res_moved[k], total = lax.optimization_barrier((res_moved[k], total))
+        total = stage([straight(k)], [res_moved[k]], home, total, True, 1, "middle_traveller_terms")
+    blocks = [other_core(value) for value in res_moved[:last]]
+    mine, others = stage(middle, blocks, home, total, True, 2, "late_traveller_terms", cut=True, after=(unfolding,))
+
+    gate = pl.pallas_call(
+        gate_kernel,
+        out_shape=jax.ShapeDtypeStruct((8, 128), jnp.float32),
+        in_specs=[HBM],
+        out_specs=VMEM,
+        compiler_params=LIMIT,
+        cost_estimate=cost(1),
+        name="gate",
+    )(others)
+    trav_moved, gate = lax.optimization_barrier((trav_moved, gate))
     trav_swapped += [other_core(value) for value in trav_moved]
     sent = [
         lax.ppermute(others[k - 1], "grp", [(g, (g + k) % groups) for g in range(groups)])
@@ -407,15 +444,26 @@
         [*trav_moved, *trav_swapped[1:-1], trav_swapped[0], trav_swapped[-1]],
         (packed, packed),
         None,
-        True,
         False,
         0.5,
         "resident_terms",
+        after=(gate,),
     )
     res_total, sent = lax.optimization_barrier((res_total, sent))
-    for value in sent:
-        mine = mine + value
-    return res_total, mine
+    parts = [mine, *sent]
+    trav_total, res_total = pl.pallas_call(
+        functools.partial(sum_kernel, len(parts)),
+        out_shape=(
+            jax.ShapeDtypeStruct((held, part, plane), jnp.float32),
+            jax.ShapeDtypeStruct(residents.shape, jnp.float32),
+        ),
+        in_specs=[VMEM] * (len(parts) + 2),
+        out_specs=(VMEM, VMEM),
+        compiler_params=LIMIT,
+        cost_estimate=cost(0.5),
+        name="sums",
+    )(*parts, unfolding, res_total)
+    return res_total, trav_total
 
 
 def solution(mesh):

time: 28.2 us -> 25.6 us (0.908)
  Pallas kernels: 10.7 us -> 9.36 us
  other arithmetic: 0.67 us -> 0 us
  waiting for transfers between devices: 5.22 us -> 4.56 us
    ppermute x4, waiting for transfers between devices: 5.2 us -> 2.33 us  [from_behind(): lax.ppermute(value, 'blk', [(i, (i + by) % peers) for i in range(peers)])]
    ppermute x1, waiting for transfers between devices: 0.01 us -> 1.42 us  [local(): lax.ppermute(others[k - 1], 'grp', [(g, (g + k) % groups) for g in range(...]
    pallas_call x3 -> x7, Pallas kernels: 8.43 us -> 7.2 us  [the longest x4 5.9 us: stage(): pl.pallas_call(functools.partial(terms_kernel, plan, total is not None, c...]
    ppermute x6, waiting for transfers between devices: 0.02 us -> 0.82 us  [other_core(): return lax.ppermute(value, 'blk', [(i, i ^ 1) for i in range(peers)])]
    add x1 -> x0, other arithmetic: 0.67 us -> none  [local(): mine = mine + value]
  transfers between devices with their start and end apart: 11 -> 11, of which waited for: 2 -> 6; matrix products, arithmetic and copies ran while one was open for 0% -> 0% of each run, Pallas kernels for 30% -> 24%
where the time goes in v3:
time: 25.6 us; the launch traced here: 25.5 us
  starting transfers between devices  10.8 us (42%)
  Pallas kernels  9.36 us (37%)
  waiting for transfers between devices  4.56 us (18%)
  between operations  0.72 us (3%)
    ppermute x4, starting transfers between devices, from_behind(): lax.ppermute(value, 'blk', [(i, (i + by) % peers) for i in range(peers)])  8.12 us
    pallas_call x4, Pallas kernels, stage(): pl.pallas_call(functools.partial(terms_kernel, plan, total is not None, c...  5.9 us
    ppermute x4, waiting for transfers between devices, from_behind(): lax.ppermute(value, 'blk', [(i, (i + by) % peers) for i in range(peers)])  2.33 us
    pallas_call x1, Pallas kernels, local(): pl.pallas_call(functools.partial(pack_kernel, ('blk', 'grp')), out_shape=...  2.07 us
    ppermute x1, starting transfers between devices, local(): lax.ppermute(others[k - 1], 'grp', [(g, (g + k) % groups) for g in range(...  1.52 us
    ppermute x1, waiting for transfers between devices, local(): lax.ppermute(others[k - 1], 'grp', [(g, (g + k) % groups) for g in range(...  1.42 us
    ppermute x6, starting transfers between devices, other_core(): return lax.ppermute(value, 'blk', [(i, i ^ 1) for i in range(peers)])  1.15 us
    pallas_call x1, Pallas kernels, local(): pl.pallas_call(functools.partial(sum_kernel, len(parts)), out_shape=(jax....  1.12 us
  transfers between devices with their start and end apart: 11, of which 6 were waited for; matrix products, arithmetic and copies ran while one was open for 0% of the time, Pallas kernels for 24%

profile of v3, /device:TPU:0, one launch (start us, length us, event | category | flops | bytes accessed | tf_op | source)
XLA Modules:
  0.0 25.5 jit_solution(6065419370396851730)
XLA Ops:
  0.6 0.0 copy-start.2
  0.6 2.1 %pack.1 = (bf16[544,128]{1,0:T(8,128)(2,1)}, bf16[512,128]{1,0:T(8,128)(2,1)}) custom-call(bf16[2,32,1024]{2,1,0:T(8,128)(2,1)} %residents.1, bf16[2,32,1024]{2,1,0:T(8,128)(2,1)} %travellers.1, s32[1,3,2,4]{3,2,1,0:T(2,128)} %bitcast.3), custom_call_target="tpu_custom_call" | custom-call | flops 1000000000 | bytes 1024 | tf_op jit(solution)/shard_map/pack/pallas_call | solution.py:343
  2.7 5.1 %collective-permute-start.1 = (bf16[544,128]{1,0:T(8,128)(2,1)}, bf16[544,128]{1,0:T(8,128)(2,1)S(1)}, u32[]{:S(2)}, u32[]{:S(2)}) collective-permute-start(bf16[544,128]{1,0:T(8,128)(2,1)} %get-tuple-element.18.refs_3_.refs_1_.refs_5_.refs_6_), channel_id=1, source_target_pairs={{0,24},{2,26},{4,28},{6,30},{8,0},{10,2},{12,4},{14,6},{16,8},{18,... | collective-permute-start | bytes 417800 | tf_op jit(solution)/shard_map/ppermute | solution.py:320
  7.8 1.4 %collective-permute-start = (bf16[544,128]{1,0:T(8,128)(2,1)}, bf16[544,128]{1,0:T(8,128)(2,1)S(1)}, u32[]{:S(2)}, u32[]{:S(2)}) collective-permute-start(bf16[544,128]{1,0:T(8,128)(2,1)} %get-tuple-element.18.refs_3_.refs_1_.refs_5_.refs_6_), channel_id=1, source_target_pairs={{0,28},{2,30},{4,0},{6,2},{8,4},{10,6},{12,8},{14,10},{16,12},{18,... | collective-permute-start | bytes 417800 | tf_op jit(solution)/shard_map/ppermute | solution.py:320
  9.2 0.0 collective-permute-start.2
  9.2 0.7 %collective-permute-start.5 = (bf16[512,128]{1,0:T(8,128)(2,1)}, bf16[512,128]{1,0:T(8,128)(2,1)S(1)}, u32[]{:S(2)}, u32[]{:S(2)}) collective-permute-start(bf16[512,128]{1,0:T(8,128)(2,1)} %get-tuple-element.19.refs_4_.refs_2_), channel_id=1, source_target_pairs={{0,4},{2,6},{4,8},{6,10},{8,12},{10,14},{12,16},{14,18},{16,20},{1... | collective-permute-start | bytes 393224 | tf_op jit(solution)/shard_map/ppermute | solution.py:320
  9.9 1.0 %collective-permute-start.6 = (bf16[512,128]{1,0:T(8,128)(2,1)}, bf16[512,128]{1,0:T(8,128)(2,1)S(1)}, u32[]{:S(2)}, u32[]{:S(2)}) collective-permute-start(bf16[512,128]{1,0:T(8,128)(2,1)} %get-tuple-element.19.refs_4_.refs_2_), channel_id=1, source_target_pairs={{0,8},{2,10},{4,12},{6,14},{8,16},{10,18},{12,20},{14,22},{16,24},... | collective-permute-start | bytes 393224 | tf_op jit(solution)/shard_map/ppermute | solution.py:320
  10.8 1.4 %collective-permute-done.1.refs_0_ = bf16[544,128]{1,0:T(8,128)(2,1)S(1)} collective-permute-done((bf16[544,128]{1,0:T(8,128)(2,1)}, bf16[544,128]{1,0:T(8,128)(2,1)S(1)}, u32[]{:S(2)}, u32[]{:S(2)}) %collective-permute-start.1) | collective-permute-done | bytes 139296 | tf_op jit(solution)/shard_map/ppermute | solution.py:320
  12.2 0.0 collective-permute-start.3
  12.2 0.0 copy-done.2
  12.2 0.1 tables.1
  12.3 0.0 collective-permute-done.2.refs_1_
  12.4 0.6 %collective-permute-start.8 = (bf16[512,128]{1,0:T(8,128)(2,1)S(1)}, bf16[512,128]{1,0:T(8,128)(2,1)S(1)}, u32[]{:S(2)}, u32[]{:S(2)}) collective-permute-start(bf16[512,128]{1,0:T(8,128)(2,1)S(1)} %copy-done.1), channel_id=1, source_target_pairs={{0,2},{2,0},{4,6},{6,4},{8,10},{10,8},{12,14},{14,12},{16,18},{18,... | collective-permute-start | bytes 393224 | tf_op jit(solution)/shard_map/ppermute | solution.py:325
  12.9 0.7 %collective-permute-done.3.refs_2_ = bf16[544,128]{1,0:T(8,128)(2,1)S(1)} collective-permute-done((bf16[544,128]{1,0:T(8,128)(2,1)S(1)}, bf16[544,128]{1,0:T(8,128)(2,1)S(1)}, u32[]{:S(2)}, u32[]{:S(2)}) %collective-permute-start.3) | collective-permute-done | bytes 139296 | tf_op jit(solution)/shard_map/ppermute | solution.py:325
  13.6 1.5 %early_traveller_terms.1.refs_6_ = f32[2,4,32,256]{3,2,1,0:T(8,128)S(1)} custom-call(bf16[544,128]{1,0:T(8,128)(2,1)S(1)} %collective-permute-done.1.refs_0_, bf16[544,128]{1,0:T(8,128)(2,1)S(1)} %collective-permute-done.2.refs_1_, bf16[544,128]{1,0:T(8,128)(2,1)S(1)} %collective-permute-done.3.refs_2_, bf16[544,128]{1,0:T(8,128)(2,1)S(1)} %copy-done, ...), custom_call_target="tpu_custom_call" | custom-call | flops 10000000000 | bytes 1024 | tf_op jit(solution)/shard_map/early_traveller_terms/pallas_call | solution.py:383
  15.1 0.2 collective-permute-done.refs_0_._
  15.3 0.1 collective-permute-start.4
  15.3 0.2 unfold_table.1.refs_7_.refs_2_
  15.5 1.0 %middle_traveller_terms.1.refs_6_ = f32[2,4,32,256]{3,2,1,0:T(8,128)S(1)} custom-call(bf16[544,128]{1,0:T(8,128)(2,1)S(1)} %collective-permute-done.refs_0_._, bf16[544,128]{1,0:T(8,128)(2,1)S(1)} %copy-done, bf16[512,128]{1,0:T(8,128)(2,1)S(1)} %copy-done.1, bf16[512,256]{1,0:T(8,128)(2,1)S(1)} %get-tuple-element.20.refs_5_.refs_3_.refs_7_, ...), custom_call_target="tpu_custom_call" | custom-call | flops 1000000000 | bytes 1024 | tf_op jit(solution)/shard_map/middle_traveller_terms/pallas_call | solution.py:383
  16.5 0.1 collective-permute-done.4.refs_0_
  16.6 1.0 %late_traveller_terms.1 = (f32[2,4,16,256]{3,2,1,0:T(8,128)S(1)}, f32[1,2,4,16,256]{4,3,2,1,0:T(8,128)S(1)}) custom-call(bf16[544,128]{1,0:T(8,128)(2,1)S(1)} %collective-permute-done.4.refs_0_, bf16[544,128]{1,0:T(8,128)(2,1)S(1)} %copy-done, bf16[512,128]{1,0:T(8,128)(2,1)S(1)} %copy-done.1, ...), custom_call_target="tpu_custom_call" | custom-call | flops 2000000000 | bytes 1024 | tf_op jit(solution)/shard_map/late_traveller_terms/pallas_call | solution.py:383
  17.6 0.8 %collective-permute-done.5.refs_0_ = bf16[512,128]{1,0:T(8,128)(2,1)S(1)} collective-permute-done((bf16[512,128]{1,0:T(8,128)(2,1)}, bf16[512,128]{1,0:T(8,128)(2,1)S(1)}, u32[]{:S(2)}, u32[]{:S(2)}) %collective-permute-start.5) | collective-permute-done | bytes 131104 | tf_op jit(solution)/shard_map/ppermute | solution.py:320
  18.4 0.0 collective-permute-done.6.refs_1_
  18.4 0.0 collective-permute-start.7
  18.4 0.5 %collective-permute-start.9 = (bf16[512,128]{1,0:T(8,128)(2,1)S(1)}, bf16[512,128]{1,0:T(8,128)(2,1)S(1)}, u32[]{:S(2)}, u32[]{:S(2)}) collective-permute-start(bf16[512,128]{1,0:T(8,128)(2,1)S(1)} %collective-permute-done.6.refs_1_), channel_id=1, source_target_pairs={{0,2},{2,0},{4,6},{6,4},{8,10},{10,8},{12,14},{14,12},{16,18},{18,... | collective-permute-start | bytes 393224 | tf_op jit(solution)/shard_map/ppermute | solution.py:325
  18.9 1.5 %collective-permute-start.10 = (f32[2,4,16,256]{3,2,1,0:T(8,128)S(1)}, f32[2,4,16,256]{3,2,1,0:T(8,128)S(1)}, u32[]{:S(2)}, u32[]{:S(2)}) collective-permute-start(f32[2,4,16,256]{3,2,1,0:T(8,128)S(1)} %bitcast.2), channel_id=1, source_target_pairs={{0,1},{1,0},{2,3},{3,2},{4,5},{5,4},{6,7},{7,6},{8,9},{9,8},{10,11... | collective-permute-start | bytes 393224 | tf_op jit(solution)/shard_map/ppermute | solution.py:439
  20.4 0.0 collective-permute-done.8.refs_3_
  20.4 0.0 collective-permute-done.7.refs_2_
  20.5 0.0 collective-permute-done.9.refs_4_
  20.5 2.5 %resident_terms.1.refs_3_ = f32[2,4,32,256]{3,2,1,0:T(8,128)S(1)} custom-call(bf16[512,128]{1,0:T(8,128)(2,1)S(1)} %collective-permute-done.5.refs_0_, bf16[512,128]{1,0:T(8,128)(2,1)S(1)} %collective-permute-done.6.refs_1_, bf16[512,128]{1,0:T(8,128)(2,1)S(1)} %collective-permute-done.7.refs_2_, bf16[512,128]{1,0:T(8,128)(2,1)S(1)} %collective-permute-done.8.refs_3_, ...), custom_call_target="tpu_custom_call" | custom-call | flops 500000000 | bytes 1024 | tf_op jit(solution)/shard_map/resident_terms/pallas_call | solution.py:383
  22.9 1.4 %collective-permute-done.10.refs_1_ = f32[2,4,16,256]{3,2,1,0:T(8,128)S(1)} collective-permute-done((f32[2,4,16,256]{3,2,1,0:T(8,128)S(1)}, f32[2,4,16,256]{3,2,1,0:T(8,128)S(1)}, u32[]{:S(2)}, u32[]{:S(2)}) %collective-permute-start.10) | collective-permute-done | bytes 131104 | tf_op jit(solution)/shard_map/ppermute | solution.py:439
  24.3 1.1 %sums.1 = (f32[2,16,1024]{2,1,0:T(8,128)}, f32[2,32,1024]{2,1,0:T(8,128)}) custom-call(f32[2,4,16,256]{3,2,1,0:T(8,128)S(1)} %get-tuple-element.25.refs_0_, f32[2,4,16,256]{3,2,1,0:T(8,128)S(1)} %collective-permute-done.10.refs_1_, bf16[512,512]{1,0:T(8,128)(2,1)S(1)} %unfold_table.1.refs_7_.refs_2_, f32[2,4,32,256]{3,2,1,0:T(8,128)S(1)} %resident_terms.1.refs_3_), custom_call_target="tpu_custom_call" | custom-call | flops 500000000 | bytes 1024 | tf_op jit(solution)/shard_map/sums/pallas_call | solution.py:454
  (5 shorter events, 0.0 us)
Async XLA Ops:
  0.6 11.6 %copy-start.2 = (f32[72,256]{1,0:T(8,128)S(1)}, f32[72,256]{1,0:T(8,128)}, u32[]{:S(2)}) copy-start(f32[72,256]{1,0:T(8,128)} %constant.2.clone.small) | copy-start | bytes 221188
  2.7 9.5 %collective-permute-start.1 = (bf16[544,128]{1,0:T(8,128)(2,1)}, bf16[544,128]{1,0:T(8,128)(2,1)S(1)}, u32[]{:S(2)}, u32[]{:S(2)}) collective-permute-start(bf16[544,128]{1,0:T(8,128)(2,1)} %get-tuple-element.18.refs_3_.refs_1_.refs_5_.refs_6_), channel_id=1, source_target_pairs={{0,24},{2,26},{4,28},{6,30},{8,0},{10,2},{12,4},{14,6},{16,8},{18,... | collective-permute-start | bytes 417800 | tf_op jit(solution)/shard_map/ppermute | solution.py:320
  7.8 7.4 %collective-permute-start = (bf16[544,128]{1,0:T(8,128)(2,1)}, bf16[544,128]{1,0:T(8,128)(2,1)S(1)}, u32[]{:S(2)}, u32[]{:S(2)}) collective-permute-start(bf16[544,128]{1,0:T(8,128)(2,1)} %get-tuple-element.18.refs_3_.refs_1_.refs_5_.refs_6_), channel_id=1, source_target_pairs={{0,28},{2,30},{4,0},{6,2},{8,4},{10,6},{12,8},{14,10},{16,12},{18,... | collective-permute-start | bytes 417800 | tf_op jit(solution)/shard_map/ppermute | solution.py:320
  9.2 3.1 %collective-permute-start.2 = (bf16[544,128]{1,0:T(8,128)(2,1)}, bf16[544,128]{1,0:T(8,128)(2,1)S(1)}, u32[]{:S(2)}, u32[]{:S(2)}) collective-permute-start(bf16[544,128]{1,0:T(8,128)(2,1)} %get-tuple-element.18.refs_3_.refs_1_.refs_5_.refs_6_), channel_id=1, source_target_pairs={{0,2},{2,0},{4,6},{6,4},{8,10},{10,8},{12,14},{14,12},{16,18},{18,... | collective-permute-start | bytes 417800 | tf_op jit(solution)/shard_map/ppermute | solution.py:325
  9.2 3.1 %copy-start.1 = (bf16[512,128]{1,0:T(8,128)(2,1)S(1)}, bf16[512,128]{1,0:T(8,128)(2,1)}, u32[]{:S(2)}) copy-start(bf16[512,128]{1,0:T(8,128)(2,1)} %get-tuple-element.19.refs_4_.refs_2_) | copy-start | bytes 393220
  9.2 4.4 %copy-start = (bf16[544,128]{1,0:T(8,128)(2,1)S(1)}, bf16[544,128]{1,0:T(8,128)(2,1)}, u32[]{:S(2)}) copy-start(bf16[544,128]{1,0:T(8,128)(2,1)} %get-tuple-element.18.refs_3_.refs_1_.refs_5_.refs_6_) | copy-start | bytes 417796
  9.2 9.2 %collective-permute-start.5 = (bf16[512,128]{1,0:T(8,128)(2,1)}, bf16[512,128]{1,0:T(8,128)(2,1)S(1)}, u32[]{:S(2)}, u32[]{:S(2)}) collective-permute-start(bf16[512,128]{1,0:T(8,128)(2,1)} %get-tuple-element.19.refs_4_.refs_2_), channel_id=1, source_target_pairs={{0,4},{2,6},{4,8},{6,10},{8,12},{10,14},{12,16},{14,18},{16,20},{1... | collective-permute-start | bytes 393224 | tf_op jit(solution)/shard_map/ppermute | solution.py:320
  9.9 8.6 %collective-permute-start.6 = (bf16[512,128]{1,0:T(8,128)(2,1)}, bf16[512,128]{1,0:T(8,128)(2,1)S(1)}, u32[]{:S(2)}, u32[]{:S(2)}) collective-permute-start(bf16[512,128]{1,0:T(8,128)(2,1)} %get-tuple-element.19.refs_4_.refs_2_), channel_id=1, source_target_pairs={{0,8},{2,10},{4,12},{6,14},{8,16},{10,18},{12,20},{14,22},{16,24},... | collective-permute-start | bytes 393224 | tf_op jit(solution)/shard_map/ppermute | solution.py:320
  12.2 1.4 %collective-permute-start.3 = (bf16[544,128]{1,0:T(8,128)(2,1)S(1)}, bf16[544,128]{1,0:T(8,128)(2,1)S(1)}, u32[]{:S(2)}, u32[]{:S(2)}) collective-permute-start(bf16[544,128]{1,0:T(8,128)(2,1)S(1)} %collective-permute-done.1.refs_0_), channel_id=1, source_target_pairs={{0,2},{2,0},{4,6},{6,4},{8,10},{10,8},{12,14},{14,12},{16,18},{18,... | collective-permute-start | bytes 417800 | tf_op jit(solution)/shard_map/ppermute | solution.py:325
  12.4 8.1 %collective-permute-start.8 = (bf16[512,128]{1,0:T(8,128)(2,1)S(1)}, bf16[512,128]{1,0:T(8,128)(2,1)S(1)}, u32[]{:S(2)}, u32[]{:S(2)}) collective-permute-start(bf16[512,128]{1,0:T(8,128)(2,1)S(1)} %copy-done.1), channel_id=1, source_target_pairs={{0,2},{2,0},{4,6},{6,4},{8,10},{10,8},{12,14},{14,12},{16,18},{18,... | collective-permute-start | bytes 393224 | tf_op jit(solution)/shard_map/ppermute | solution.py:325
  15.3 1.4 %collective-permute-start.4 = (bf16[544,128]{1,0:T(8,128)(2,1)S(1)}, bf16[544,128]{1,0:T(8,128)(2,1)S(1)}, u32[]{:S(2)}, u32[]{:S(2)}) collective-permute-start(bf16[544,128]{1,0:T(8,128)(2,1)S(1)} %collective-permute-done.refs_0_._), channel_id=1, source_target_pairs={{0,2},{2,0},{4,6},{6,4},{8,10},{10,8},{12,14},{14,12},{16,18},{18,... | collective-permute-start | bytes 417800 | tf_op jit(solution)/shard_map/ppermute | solution.py:325
  18.4 2.0 %collective-permute-start.7 = (bf16[512,128]{1,0:T(8,128)(2,1)S(1)}, bf16[512,128]{1,0:T(8,128)(2,1)S(1)}, u32[]{:S(2)}, u32[]{:S(2)}) collective-permute-start(bf16[512,128]{1,0:T(8,128)(2,1)S(1)} %collective-permute-done.5.refs_0_), channel_id=1, source_target_pairs={{0,2},{2,0},{4,6},{6,4},{8,10},{10,8},{12,14},{14,12},{16,18},{18,... | collective-permute-start | bytes 393224 | tf_op jit(solution)/shard_map/ppermute | solution.py:325
  18.4 2.0 %collective-permute-start.9 = (bf16[512,128]{1,0:T(8,128)(2,1)S(1)}, bf16[512,128]{1,0:T(8,128)(2,1)S(1)}, u32[]{:S(2)}, u32[]{:S(2)}) collective-permute-start(bf16[512,128]{1,0:T(8,128)(2,1)S(1)} %collective-permute-done.6.refs_1_), channel_id=1, source_target_pairs={{0,2},{2,0},{4,6},{6,4},{8,10},{10,8},{12,14},{14,12},{16,18},{18,... | collective-permute-start | bytes 393224 | tf_op jit(solution)/shard_map/ppermute | solution.py:325
  18.9 5.4 %collective-permute-start.10 = (f32[2,4,16,256]{3,2,1,0:T(8,128)S(1)}, f32[2,4,16,256]{3,2,1,0:T(8,128)S(1)}, u32[]{:S(2)}, u32[]{:S(2)}) collective-permute-start(f32[2,4,16,256]{3,2,1,0:T(8,128)S(1)} %bitcast.2), channel_id=1, source_target_pairs={{0,1},{1,0},{2,3},{3,2},{4,5},{5,4},{6,7},{7,6},{8,9},{9,8},{10,11... | collective-permute-start | bytes 393224 | tf_op jit(solution)/shard_map/ppermute | solution.py:439

commit v4 on v3

--- a/solution.py
+++ b/solution.py
@@ -114,15 +114,13 @@
                 target[row : row + edge, :] = folded[start : start + edge, q * lanes : (q + 1) * lanes]
 
 
-def pack_kernel(axes, residents, travellers, pairs, packed, moving, fields, moving_fields, entries_ref, folded, moving_folded, sems):
+def pack_kernel(axes, residents, pairs, packed, fields, entries_ref, folded, sems):
     count, edge, plane = residents.shape
-    loads = [pltpu.make_async_copy(residents.at[i], fields.at[i], sems.at[5 + i]) for i in range(count)]
+    loads = [pltpu.make_async_copy(residents.at[i], fields.at[i], sems.at[2 + i]) for i in range(count)]
     load_entries = pltpu.make_async_copy(pairs, entries_ref, sems.at[1])
-    load_moving = pltpu.make_async_copy(travellers, moving_fields, sems.at[2])
     for load in loads:
         load.start()
     load_entries.start()
-    load_moving.start()
     table = fold_table(edge, False)
     load_entries.wait()
     _, entries, slots, steps = pairs.shape
@@ -135,18 +133,17 @@
     for load in loads:
         load.wait()
     store_folded(fields, table, folded)
-    store = pltpu.make_async_copy(folded, packed, sems.at[3])
+    store = pltpu.make_async_copy(folded, packed, sems.at[0])
     store.start()
-    load_moving.wait()
-    store_folded(moving_fields, table, moving_folded)
-    store_moving = pltpu.make_async_copy(moving_folded, moving, sems.at[4])
-    store_moving.start()
     store.wait()
-    store_moving.wait()
-
-
-def tables_kernel(count, small, plane_table, along, inverse):
-    make_tables(small, inverse.shape[0], count, plane_table, along, inverse)
+
+
+def tables_kernel(count, small, travellers, plane_table, along, inverse, folding, unfolding, moving):
+    edge = inverse.shape[0]
+    make_tables(small, edge, count, plane_table, along, inverse)
+    folding[...] = fold_table(edge, False)
+    unfolding[...] = fold_table(edge, True)
+    store_folded(travellers, folding[...], moving)
 
 
 class Fields:
@@ -164,6 +161,30 @@
     def info(self, count=None):
         start = 8 * self.count * self.edge
         return self.rows(start, self.refs[0].shape[0] - start)
+
+
+class PlainFields:
+    def __init__(self, count, edge, *refs, near=None, table=None):
+        self.count, self.edge, self.near = count, edge, near
+        half = edge * edge // 2
+        values = [[ref[i].astype(jnp.float32) for i in range(count)] for ref in refs]
+        fields = values[0]
+        if len(values) == 2:
+            fields = [jnp.where(near, *pair) for pair in zip(*values)]
+        rows = [field[:, h * half : (h + 1) * half] for field in fields for h in (0, 1)]
+        self.folded = dot(jnp.concatenate(rows, axis=0).astype(jnp.bfloat16), table)
+
+    def quadrants(self, i):
+        edge, lanes = self.edge, self.folded.shape[1] // 4
+        found = []
+        for q in range(4):
+            order = (0, 1) if q < 2 else (1, 0)
+            tiles = [
+                self.folded[(2 * i + h) * edge : (2 * i + h + 1) * edge, q * lanes : (q + 1) * lanes]
+                for h in order
+            ]
+            found.append(jnp.concatenate(tiles, axis=1))
+        return found
 
 
 def wide(row, edge, lanes):
@@ -248,16 +269,20 @@
     refs, outs = refs[: len(refs) - outputs - after], refs[-outputs:]
     blocks = sum(number for number, _ in plan)
     moving, (own, home, *refs) = refs[:blocks], refs[blocks:]
-    tables, before = refs[:3], refs[3:]
+    tables, folding, before = refs[:3], refs[3], refs[4:]
     held = home.shape[0] // (8 * edge)
-    count = moving[0].shape[0] // (8 * edge)
+    count = moving[0].shape[0] // (8 * edge) if for_travellers else moving[0].shape[0]
     own = Fields(own.shape[0] // (8 * edge), edge, own).info()
     near = own[0:1] == (0 if for_travellers else 1)
     home = Fields(held, edge, home)
     home = [home.quadrants(j) for j in range(held)]
     found = []
     for number, arrivals in plan:
-        block, moving = Fields(count, edge, *moving[:number], near=near), moving[number:]
+        sources, moving = moving[:number], moving[number:]
+        if for_travellers:
+            block = Fields(count, edge, *sources, near=near)
+        else:
+            block = PlainFields(count, edge, *sources, near=near[0:1, 0:1], table=folding[...])
         info = block.info() if for_travellers else own
         found += slots_of(block, info, near, arrivals, slots, 0 if for_travellers else 1)
     total = [[before[0][j, q] for q in range(4)] for j in range(held)] if accumulate else zero_total(home)
@@ -284,10 +309,6 @@
                     others[k - 1, j, q] = piece
 
 
-def unfold_table_kernel(edge, _, table):
-    table[...] = fold_table(edge, True)
-
-
 def gate_kernel(_, out):
     out[...] = jnp.zeros_like(out)
 
@@ -336,39 +357,38 @@
     fields = 2 * slots
     small = jnp.asarray(small_tables(edge, fields))
 
-    shapes = (
-        (8 * count * edge + info_rows(steps, slots), plane // 8),
-        (8 * held * edge, plane // 8),
-    )
-    packed, moving = pl.pallas_call(
+    shape = (8 * count * edge + info_rows(steps, slots), plane // 8)
+    packed = pl.pallas_call(
         functools.partial(pack_kernel, ("blk", "grp")),
-        out_shape=tuple(jax.ShapeDtypeStruct(shape, jnp.bfloat16) for shape in shapes),
-        in_specs=[HBM, HBM, HBM],
-        out_specs=(HBM, HBM),
+        out_shape=jax.ShapeDtypeStruct(shape, jnp.bfloat16),
+        in_specs=[HBM, HBM],
+        out_specs=HBM,
         scratch_shapes=[
             pltpu.VMEM(residents.shape, jnp.bfloat16),
-            pltpu.VMEM(travellers.shape, jnp.bfloat16),
             pltpu.SMEM((1, 3, slots, steps), jnp.int32),
-            *(pltpu.VMEM(shape, jnp.bfloat16) for shape in shapes),
-            pltpu.SemaphoreType.DMA((5 + count,)),
+            pltpu.VMEM(shape, jnp.bfloat16),
+            pltpu.SemaphoreType.DMA((2 + count,)),
         ],
         compiler_params=LIMIT_U,
         cost_estimate=cost(1),
         name="pack",
-    )(residents, travellers, jnp.transpose(pair_list, (0, 3, 2, 1)))
-    tables = pl.pallas_call(
+    )(residents, jnp.transpose(pair_list, (0, 3, 2, 1)))
+    *tables, folding, unfolding, moving = pl.pallas_call(
         functools.partial(tables_kernel, fields),
         out_shape=(
             jax.ShapeDtypeStruct((plane // 2, plane // 4), jnp.bfloat16),
             jax.ShapeDtypeStruct((2 * fields * edge, fields * edge), jnp.bfloat16),
             jax.ShapeDtypeStruct((edge, plane), jnp.float32),
+            jax.ShapeDtypeStruct((plane // 2, plane // 2), jnp.bfloat16),
+            jax.ShapeDtypeStruct((plane // 2, plane // 2), jnp.bfloat16),
+            jax.ShapeDtypeStruct((8 * held * edge, plane // 8), jnp.bfloat16),
         ),
-        in_specs=[VMEM],
-        out_specs=(VMEM,) * 3,
+        in_specs=[VMEM, VMEM],
+        out_specs=(VMEM,) * 6,
         compiler_params=LIMIT,
         cost_estimate=cost(20),
         name="tables",
-    )(small)
+    )(small, travellers)
 
     def stage(plan, blocks, home, total, for_travellers, microseconds, name, cut=False, after=()):
         number = home[1].shape[0] // (8 * edge)
@@ -379,7 +399,7 @@
             )
         else:
             out_shape = jax.ShapeDtypeStruct((number, 4, edge, plane // 4), jnp.float32)
-        operands = (*blocks, *home, *tables) + (() if total is None else (total,))
+        operands = (*blocks, *home, *tables, folding) + (() if total is None else (total,))
         return pl.pallas_call(
             functools.partial(
                 terms_kernel, plan, total is not None, cut, slots, edge, for_travellers, len(after)
@@ -402,18 +422,22 @@
 
     res_moved = [from_behind(packed, -s) for s in direct]
     res_swapped = [other_core(packed)] + [other_core(value) for value in res_moved]
-    trav_moved = [from_behind(moving, s) for s in direct]
-    trav_swapped = [other_core(moving)]
-
-    unfolding = pl.pallas_call(
-        functools.partial(unfold_table_kernel, edge),
-        out_shape=jax.ShapeDtypeStruct((plane // 2, plane // 2), jnp.bfloat16),
-        in_specs=[HBM],
-        out_specs=VMEM,
-        compiler_params=LIMIT,
-        cost_estimate=cost(20),
-        name="unfold_table",
-    )(res_moved[0])
+    passed, packed_first = lax.optimization_barrier((travellers, packed))
+    trav_moved = [from_behind(passed, s) for s in direct]
+    trav_swapped = [other_core(passed)]
+
+    def gate(value, microseconds):
+        return pl.pallas_call(
+            gate_kernel,
+            out_shape=jax.ShapeDtypeStruct((8, 128), jnp.float32),
+            in_specs=[HBM],
+            out_specs=VMEM,
+            compiler_params=LIMIT,
+            cost_estimate=cost(microseconds),
+            name="gate",
+        )(value)
+
+    arrived = gate(res_moved[0], 20)
 
     home = (packed, moving)
     blocks = [res_moved[last], res_swapped[0], res_swapped[-1]]
@@ -422,18 +446,10 @@
         res_moved[k], total = lax.optimization_barrier((res_moved[k], total))
         total = stage([straight(k)], [res_moved[k]], home, total, True, 1, "middle_traveller_terms")
     blocks = [other_core(value) for value in res_moved[:last]]
-    mine, others = stage(middle, blocks, home, total, True, 2, "late_traveller_terms", cut=True, after=(unfolding,))
-
-    gate = pl.pallas_call(
-        gate_kernel,
-        out_shape=jax.ShapeDtypeStruct((8, 128), jnp.float32),
-        in_specs=[HBM],
-        out_specs=VMEM,
-        compiler_params=LIMIT,
-        cost_estimate=cost(1),
-        name="gate",
-    )(others)
-    trav_moved, gate = lax.optimization_barrier((trav_moved, gate))
+    mine, others = stage(middle, blocks, home, total, True, 2, "late_traveller_terms", cut=True, after=(arrived,))
+
+    summed = gate(others, 1)
+    trav_moved, summed = lax.optimization_barrier((trav_moved, summed))
     trav_swapped += [other_core(value) for value in trav_moved]
     sent = [
         lax.ppermute(others[k - 1], "grp", [(g, (g + k) % groups) for g in range(groups)])
@@ -447,7 +463,7 @@
         False,
         0.5,
         "resident_terms",
-        after=(gate,),
+        after=(summed,),
     )
     res_total, sent = lax.optimization_barrier((res_total, sent))
     parts = [mine, *sent]

time: 25.6 us -> 25.2 us (0.984)
  waiting for transfers between devices: 4.56 us -> 3.86 us
    pallas_call x1, Pallas kernels: 0.09 us -> 0.48 us  [local(): pl.pallas_call(functools.partial(tables_kernel, fields), out_shape=(jax.S...]
    ppermute x1, waiting for transfers between devices: 1.42 us -> 1.13 us  [local(): lax.ppermute(others[k - 1], 'grp', [(g, (g + k) % groups) for g in range(...]
    pallas_call x4, Pallas kernels: 5.9 us -> 6.16 us  [stage(): pl.pallas_call(functools.partial(terms_kernel, plan, total is not None, c...]
  transfers between devices with their start and end apart: 11 -> 11, of which waited for: 6 -> 6; matrix products, arithmetic and copies ran while one was open for 0% -> 0% of each run, Pallas kernels for 24% -> 27%
where the time goes in v4:
time: 25.2 us; the launch traced here: 25 us
  starting transfers between devices  10.8 us (43%)
  Pallas kernels  9.58 us (38%)
  waiting for transfers between devices  3.86 us (15%)
  between operations  0.73 us (3%)
    ppermute x4, starting transfers between devices, from_behind(): lax.ppermute(value, 'blk', [(i, (i + by) % peers) for i in range(peers)])  8.11 us
    pallas_call x4, Pallas kernels, stage(): pl.pallas_call(functools.partial(terms_kernel, plan, total is not None, c...  6.16 us
    ppermute x4, waiting for transfers between devices, from_behind(): lax.ppermute(value, 'blk', [(i, (i + by) % peers) for i in range(peers)])  2.14 us
    pallas_call x1, Pallas kernels, local(): pl.pallas_call(functools.partial(pack_kernel, ('blk', 'grp')), out_shape=...  1.82 us
    ppermute x1, starting transfers between devices, local(): lax.ppermute(others[k - 1], 'grp', [(g, (g + k) % groups) for g in range(...  1.52 us
    ppermute x6, starting transfers between devices, other_core(): return lax.ppermute(value, 'blk', [(i, i ^ 1) for i in range(peers)])  1.18 us
    ppermute x1, waiting for transfers between devices, local(): lax.ppermute(others[k - 1], 'grp', [(g, (g + k) % groups) for g in range(...  1.13 us
    pallas_call x1, Pallas kernels, local(): pl.pallas_call(functools.partial(sum_kernel, len(parts)), out_shape=(jax....  1.12 us
  transfers between devices with their start and end apart: 11, of which 6 were waited for; matrix products, arithmetic and copies ran while one was open for 0% of the time, Pallas kernels for 27%

profile of v4, /device:TPU:0, one launch (start us, length us, event | category | flops | bytes accessed | tf_op | source)
XLA Modules:
  0.0 25.0 jit_solution(13620531307772799061)
XLA Ops:
  0.6 0.0 copy-start.1
  0.6 0.0 copy-start.2
  0.7 1.8 %pack.1.refs_3_.refs_1_.refs_5_.refs_6_ = bf16[544,128]{1,0:T(8,128)(2,1)} custom-call(bf16[2,32,1024]{2,1,0:T(8,128)(2,1)} %residents.1, s32[1,3,2,4]{3,2,1,0:T(2,128)} %bitcast.3), custom_call_target="tpu_custom_call" | custom-call | flops 1000000000 | bytes 1024 | tf_op jit(solution)/shard_map/pack/pallas_call | solution.py:361
  2.5 0.0 copy-start
  2.5 5.1 %collective-permute-start.1 = (bf16[544,128]{1,0:T(8,128)(2,1)}, bf16[544,128]{1,0:T(8,128)(2,1)S(1)}, u32[]{:S(2)}, u32[]{:S(2)}) collective-permute-start(bf16[544,128]{1,0:T(8,128)(2,1)} %pack.1.refs_3_.refs_1_.refs_5_.refs_6_), channel_id=1, source_target_pairs={{0,24},{2,26},{4,28},{6,30},{8,0},{10,2},{12,4},{14,6},{16,8},{18,... | collective-permute-start | bytes 417800 | tf_op jit(solution)/shard_map/ppermute | solution.py:341
  7.6 1.4 %collective-permute-start = (bf16[544,128]{1,0:T(8,128)(2,1)}, bf16[544,128]{1,0:T(8,128)(2,1)S(1)}, u32[]{:S(2)}, u32[]{:S(2)}) collective-permute-start(bf16[544,128]{1,0:T(8,128)(2,1)} %pack.1.refs_3_.refs_1_.refs_5_.refs_6_), channel_id=1, source_target_pairs={{0,28},{2,30},{4,0},{6,2},{8,4},{10,6},{12,8},{14,10},{16,12},{18,... | collective-permute-start | bytes 417800 | tf_op jit(solution)/shard_map/ppermute | solution.py:341
  9.0 0.0 collective-permute-start.2
  9.0 0.6 %collective-permute-start.5 = (bf16[2,32,1024]{2,1,0:T(8,128)(2,1)S(1)}, bf16[2,32,1024]{2,1,0:T(8,128)(2,1)S(1)}, u32[]{:S(2)}, u32[]{:S(2)}) collective-permute-start(bf16[2,32,1024]{2,1,0:T(8,128)(2,1)S(1)} %copy-done.1), channel_id=1, source_target_pairs={{0,4},{2,6},{4,8},{6,10},{8,12},{10,14},{12,16},{14,18},{16,20},{1... | collective-permute-start | bytes 393224 | tf_op jit(solution)/shard_map/ppermute | solution.py:341
  9.6 1.0 %collective-permute-start.6 = (bf16[2,32,1024]{2,1,0:T(8,128)(2,1)S(1)}, bf16[2,32,1024]{2,1,0:T(8,128)(2,1)S(1)}, u32[]{:S(2)}, u32[]{:S(2)}) collective-permute-start(bf16[2,32,1024]{2,1,0:T(8,128)(2,1)S(1)} %copy-done.1), channel_id=1, source_target_pairs={{0,8},{2,10},{4,12},{6,14},{8,16},{10,18},{12,20},{14,22},{16,24},... | collective-permute-start | bytes 393224 | tf_op jit(solution)/shard_map/ppermute | solution.py:341
  10.6 1.4 %collective-permute-done.1.refs_0_ = bf16[544,128]{1,0:T(8,128)(2,1)S(1)} collective-permute-done((bf16[544,128]{1,0:T(8,128)(2,1)}, bf16[544,128]{1,0:T(8,128)(2,1)S(1)}, u32[]{:S(2)}, u32[]{:S(2)}) %collective-permute-start.1) | collective-permute-done | bytes 139296 | tf_op jit(solution)/shard_map/ppermute | solution.py:341
  12.0 0.0 collective-permute-start.3
  12.0 0.5 %tables.1 = (bf16[512,256]{1,0:T(8,128)(2,1)S(1)}, bf16[256,128]{1,0:T(8,128)(2,1)S(1)}, f32[32,1024]{1,0:T(8,128)S(1)}, bf16[512,512]{1,0:T(8,128)(2,1)S(1)}, b...) custom-call(f32[72,256]{1,0:T(8,128)S(1)} %copy-done.2, bf16[2,32,1024]{2,1,0:T(8,128)(2,1)S(1)} %copy-done.1), custom_call_target="tpu_custom_call" | custom-call | flops 20000000000 | bytes 1024 | tf_op jit(solution)/shard_map/tables/pallas_call | solution.py:376
  12.5 0.0 collective-permute-done.2.refs_1_
  12.5 0.6 %collective-permute-start.8 = (bf16[2,32,1024]{2,1,0:T(8,128)(2,1)S(1)}, bf16[2,32,1024]{2,1,0:T(8,128)(2,1)S(1)}, u32[]{:S(2)}, u32[]{:S(2)}) collective-permute-start(bf16[2,32,1024]{2,1,0:T(8,128)(2,1)S(1)} %copy-done.1), channel_id=1, source_target_pairs={{0,2},{2,0},{4,6},{6,4},{8,10},{10,8},{12,14},{14,12},{16,18},{18,... | collective-permute-start | bytes 393224 | tf_op jit(solution)/shard_map/ppermute | solution.py:346
  13.1 0.3 %collective-permute-done.3.refs_2_ = bf16[544,128]{1,0:T(8,128)(2,1)S(1)} collective-permute-done((bf16[544,128]{1,0:T(8,128)(2,1)S(1)}, bf16[544,128]{1,0:T(8,128)(2,1)S(1)}, u32[]{:S(2)}, u32[]{:S(2)}) %collective-permute-start.3) | collective-permute-done | bytes 139296 | tf_op jit(solution)/shard_map/ppermute | solution.py:346
  13.4 1.5 %early_traveller_terms.1.refs_7_ = f32[2,4,32,256]{3,2,1,0:T(8,128)S(1)} custom-call(bf16[544,128]{1,0:T(8,128)(2,1)S(1)} %collective-permute-done.1.refs_0_, bf16[544,128]{1,0:T(8,128)(2,1)S(1)} %collective-permute-done.2.refs_1_, bf16[544,128]{1,0:T(8,128)(2,1)S(1)} %collective-permute-done.3.refs_2_, bf16[544,128]{1,0:T(8,128)(2,1)S(1)} %copy-done, ...), custom_call_target="tpu_custom_call" | custom-call | flops 10000000000 | bytes 1024 | tf_op jit(solution)/shard_map/early_traveller_terms/pallas_call | solution.py:403
  14.9 0.1 collective-permute-done.refs_0_._
  15.0 0.1 collective-permute-start.4
  15.1 1.0 %middle_traveller_terms.1.refs_7_ = f32[2,4,32,256]{3,2,1,0:T(8,128)S(1)} custom-call(bf16[544,128]{1,0:T(8,128)(2,1)S(1)} %collective-permute-done.refs_0_._, bf16[544,128]{1,0:T(8,128)(2,1)S(1)} %copy-done, bf16[512,128]{1,0:T(8,128)(2,1)S(1)} %get-tuple-element.20.refs_4_.refs_2_, bf16[512,256]{1,0:T(8,128)(2,1)S(1)} %get-tuple-element.21.refs_5_.refs_3_.refs_7_, ...), custom_call_target="tpu_custom_call" | custom-call | flops 1000000000 | bytes 1024 | tf_op jit(solution)/shard_map/middle_traveller_terms/pallas_call | solution.py:403
  16.1 0.3 %collective-permute-done.4.refs_0_ = bf16[544,128]{1,0:T(8,128)(2,1)S(1)} collective-permute-done((bf16[544,128]{1,0:T(8,128)(2,1)S(1)}, bf16[544,128]{1,0:T(8,128)(2,1)S(1)}, u32[]{:S(2)}, u32[]{:S(2)}) %collective-permute-start.4) | collective-permute-done | bytes 139296 | tf_op jit(solution)/shard_map/ppermute | solution.py:346
  16.4 1.0 %late_traveller_terms.1 = (f32[2,4,16,256]{3,2,1,0:T(8,128)S(1)}, f32[1,2,4,16,256]{4,3,2,1,0:T(8,128)S(1)}) custom-call(bf16[544,128]{1,0:T(8,128)(2,1)S(1)} %collective-permute-done.4.refs_0_, bf16[544,128]{1,0:T(8,128)(2,1)S(1)} %copy-done, bf16[512,128]{1,0:T(8,128)(2,1)S(1)} %get-tuple-element.20.refs_4_.refs_2_, ...), custom_call_target="tpu_custom_call" | custom-call | flops 2000000000 | bytes 1024 | tf_op jit(solution)/shard_map/late_traveller_terms/pallas_call | solution.py:403
  17.4 0.6 %collective-permute-done.5.refs_0_ = bf16[2,32,1024]{2,1,0:T(8,128)(2,1)S(1)} collective-permute-done((bf16[2,32,1024]{2,1,0:T(8,128)(2,1)S(1)}, bf16[2,32,1024]{2,1,0:T(8,128)(2,1)S(1)}, u32[]{:S(2)}, u32[]{:S(2)}) %collective-permute-start.5) | collective-permute-done | bytes 131104 | tf_op jit(solution)/shard_map/ppermute | solution.py:341
  18.0 0.0 collective-permute-done.6.refs_1_
  18.0 0.0 collective-permute-start.7
  18.0 0.5 %collective-permute-start.9 = (bf16[2,32,1024]{2,1,0:T(8,128)(2,1)S(1)}, bf16[2,32,1024]{2,1,0:T(8,128)(2,1)S(1)}, u32[]{:S(2)}, u32[]{:S(2)}) collective-permute-start(bf16[2,32,1024]{2,1,0:T(8,128)(2,1)S(1)} %collective-permute-done.6.refs_1_), channel_id=1, source_target_pairs={{0,2},{2,0},{4,6},{6,4},{8,10},{10,8},{12,14},{14,12},{16,18},{18,... | collective-permute-start | bytes 393224 | tf_op jit(solution)/shard_map/ppermute | solution.py:346
  18.5 1.5 %collective-permute-start.10 = (f32[2,4,16,256]{3,2,1,0:T(8,128)S(1)}, f32[2,4,16,256]{3,2,1,0:T(8,128)S(1)}, u32[]{:S(2)}, u32[]{:S(2)}) collective-permute-start(f32[2,4,16,256]{3,2,1,0:T(8,128)S(1)} %bitcast.2), channel_id=1, source_target_pairs={{0,1},{1,0},{2,3},{3,2},{4,5},{5,4},{6,7},{7,6},{8,9},{9,8},{10,11... | collective-permute-start | bytes 393224 | tf_op jit(solution)/shard_map/ppermute | solution.py:455
  20.0 0.0 collective-permute-done.8.refs_3_
  20.0 0.0 collective-permute-done.7.refs_2_
  20.0 0.0 collective-permute-done.9.refs_4_
  20.0 2.7 %resident_terms.1.refs_3_ = f32[2,4,32,256]{3,2,1,0:T(8,128)S(1)} custom-call(bf16[2,32,1024]{2,1,0:T(8,128)(2,1)S(1)} %collective-permute-done.5.refs_0_, bf16[2,32,1024]{2,1,0:T(8,128)(2,1)S(1)} %collective-permute-done.6.refs_1_, bf16[2,32,1024]{2,1,0:T(8,128)(2,1)S(1)} %collective-permute-done.7.refs_2_, ...), custom_call_target="tpu_custom_call" | custom-call | flops 500000000 | bytes 1024 | tf_op jit(solution)/shard_map/resident_terms/pallas_call | solution.py:403
  22.8 1.1 %collective-permute-done.10.refs_1_ = f32[2,4,16,256]{3,2,1,0:T(8,128)S(1)} collective-permute-done((f32[2,4,16,256]{3,2,1,0:T(8,128)S(1)}, f32[2,4,16,256]{3,2,1,0:T(8,128)S(1)}, u32[]{:S(2)}, u32[]{:S(2)}) %collective-permute-start.10) | collective-permute-done | bytes 131104 | tf_op jit(solution)/shard_map/ppermute | solution.py:455
  23.9 1.1 %sums.1 = (f32[2,16,1024]{2,1,0:T(8,128)}, f32[2,32,1024]{2,1,0:T(8,128)}) custom-call(f32[2,4,16,256]{3,2,1,0:T(8,128)S(1)} %get-tuple-element.27.refs_0_, f32[2,4,16,256]{3,2,1,0:T(8,128)S(1)} %collective-permute-done.10.refs_1_, bf16[512,512]{1,0:T(8,128)(2,1)S(1)} %get-tuple-element.34.refs_2_, f32[2,4,32,256]{3,2,1,0:T(8,128)S(1)} %resident_terms.1.refs_3_), custom_call_target="tpu_custom_call" | custom-call | flops 500000000 | bytes 1024 | tf_op jit(solution)/shard_map/sums/pallas_call | solution.py:470
  (5 shorter events, 0.0 us)
Async XLA Ops:
  0.6 8.3 %copy-start.1 = (bf16[2,32,1024]{2,1,0:T(8,128)(2,1)S(1)}, bf16[2,32,1024]{2,1,0:T(8,128)(2,1)}, u32[]{:S(2)}) copy-start(bf16[2,32,1024]{2,1,0:T(8,128)(2,1)} %travellers.1) | copy-start | bytes 393220
  0.6 11.4 %copy-start.2 = (f32[72,256]{1,0:T(8,128)S(1)}, f32[72,256]{1,0:T(8,128)}, u32[]{:S(2)}) copy-start(f32[72,256]{1,0:T(8,128)} %constant.2.clone.small) | copy-start | bytes 221188
  2.5 10.9 %copy-start = (bf16[544,128]{1,0:T(8,128)(2,1)S(1)}, bf16[544,128]{1,0:T(8,128)(2,1)}, u32[]{:S(2)}) copy-start(bf16[544,128]{1,0:T(8,128)(2,1)} %pack.1.refs_3_.refs_1_.refs_5_.refs_6_) | copy-start | bytes 417796
  2.5 9.5 %collective-permute-start.1 = (bf16[544,128]{1,0:T(8,128)(2,1)}, bf16[544,128]{1,0:T(8,128)(2,1)S(1)}, u32[]{:S(2)}, u32[]{:S(2)}) collective-permute-start(bf16[544,128]{1,0:T(8,128)(2,1)} %pack.1.refs_3_.refs_1_.refs_5_.refs_6_), channel_id=1, source_target_pairs={{0,24},{2,26},{4,28},{6,30},{8,0},{10,2},{12,4},{14,6},{16,8},{18,... | collective-permute-start | bytes 417800 | tf_op jit(solution)/shard_map/ppermute | solution.py:341
  7.6 7.4 %collective-permute-start = (bf16[544,128]{1,0:T(8,128)(2,1)}, bf16[544,128]{1,0:T(8,128)(2,1)S(1)}, u32[]{:S(2)}, u32[]{:S(2)}) collective-permute-start(bf16[544,128]{1,0:T(8,128)(2,1)} %pack.1.refs_3_.refs_1_.refs_5_.refs_6_), channel_id=1, source_target_pairs={{0,28},{2,30},{4,0},{6,2},{8,4},{10,6},{12,8},{14,10},{16,12},{18,... | collective-permute-start | bytes 417800 | tf_op jit(solution)/shard_map/ppermute | solution.py:341
  9.0 3.6 %collective-permute-start.2 = (bf16[544,128]{1,0:T(8,128)(2,1)}, bf16[544,128]{1,0:T(8,128)(2,1)S(1)}, u32[]{:S(2)}, u32[]{:S(2)}) collective-permute-start(bf16[544,128]{1,0:T(8,128)(2,1)} %pack.1.refs_3_.refs_1_.refs_5_.refs_6_), channel_id=1, source_target_pairs={{0,2},{2,0},{4,6},{6,4},{8,10},{10,8},{12,14},{14,12},{16,18},{18,... | collective-permute-start | bytes 417800 | tf_op jit(solution)/shard_map/ppermute | solution.py:346
  9.0 9.0 %collective-permute-start.5 = (bf16[2,32,1024]{2,1,0:T(8,128)(2,1)S(1)}, bf16[2,32,1024]{2,1,0:T(8,128)(2,1)S(1)}, u32[]{:S(2)}, u32[]{:S(2)}) collective-permute-start(bf16[2,32,1024]{2,1,0:T(8,128)(2,1)S(1)} %copy-done.1), channel_id=1, source_target_pairs={{0,4},{2,6},{4,8},{6,10},{8,12},{10,14},{12,16},{14,18},{16,20},{1... | collective-permute-start | bytes 393224 | tf_op jit(solution)/shard_map/ppermute | solution.py:341
  9.6 8.3 %collective-permute-start.6 = (bf16[2,32,1024]{2,1,0:T(8,128)(2,1)S(1)}, bf16[2,32,1024]{2,1,0:T(8,128)(2,1)S(1)}, u32[]{:S(2)}, u32[]{:S(2)}) collective-permute-start(bf16[2,32,1024]{2,1,0:T(8,128)(2,1)S(1)} %copy-done.1), channel_id=1, source_target_pairs={{0,8},{2,10},{4,12},{6,14},{8,16},{10,18},{12,20},{14,22},{16,24},... | collective-permute-start | bytes 393224 | tf_op jit(solution)/shard_map/ppermute | solution.py:341
  12.0 1.4 %collective-permute-start.3 = (bf16[544,128]{1,0:T(8,128)(2,1)S(1)}, bf16[544,128]{1,0:T(8,128)(2,1)S(1)}, u32[]{:S(2)}, u32[]{:S(2)}) collective-permute-start(bf16[544,128]{1,0:T(8,128)(2,1)S(1)} %collective-permute-done.1.refs_0_), channel_id=1, source_target_pairs={{0,2},{2,0},{4,6},{6,4},{8,10},{10,8},{12,14},{14,12},{16,18},{18,... | collective-permute-start | bytes 417800 | tf_op jit(solution)/shard_map/ppermute | solution.py:346
  12.5 7.5 %collective-permute-start.8 = (bf16[2,32,1024]{2,1,0:T(8,128)(2,1)S(1)}, bf16[2,32,1024]{2,1,0:T(8,128)(2,1)S(1)}, u32[]{:S(2)}, u32[]{:S(2)}) collective-permute-start(bf16[2,32,1024]{2,1,0:T(8,128)(2,1)S(1)} %copy-done.1), channel_id=1, source_target_pairs={{0,2},{2,0},{4,6},{6,4},{8,10},{10,8},{12,14},{14,12},{16,18},{18,... | collective-permute-start | bytes 393224 | tf_op jit(solution)/shard_map/ppermute | solution.py:346
  15.0 1.4 %collective-permute-start.4 = (bf16[544,128]{1,0:T(8,128)(2,1)S(1)}, bf16[544,128]{1,0:T(8,128)(2,1)S(1)}, u32[]{:S(2)}, u32[]{:S(2)}) collective-permute-start(bf16[544,128]{1,0:T(8,128)(2,1)S(1)} %collective-permute-done.refs_0_._), channel_id=1, source_target_pairs={{0,2},{2,0},{4,6},{6,4},{8,10},{10,8},{12,14},{14,12},{16,18},{18,... | collective-permute-start | bytes 417800 | tf_op jit(solution)/shard_map/ppermute | solution.py:346
  18.0 2.0 %collective-permute-start.7 = (bf16[2,32,1024]{2,1,0:T(8,128)(2,1)S(1)}, bf16[2,32,1024]{2,1,0:T(8,128)(2,1)S(1)}, u32[]{:S(2)}, u32[]{:S(2)}) collective-permute-start(bf16[2,32,1024]{2,1,0:T(8,128)(2,1)S(1)} %collective-permute-done.5.refs_0_), channel_id=1, source_target_pairs={{0,2},{2,0},{4,6},{6,4},{8,10},{10,8},{12,14},{14,12},{16,18},{18,... | collective-permute-start | bytes 393224 | tf_op jit(solution)/shard_map/ppermute | solution.py:346
  18.0 2.0 %collective-permute-start.9 = (bf16[2,32,1024]{2,1,0:T(8,128)(2,1)S(1)}, bf16[2,32,1024]{2,1,0:T(8,128)(2,1)S(1)}, u32[]{:S(2)}, u32[]{:S(2)}) collective-permute-start(bf16[2,32,1024]{2,1,0:T(8,128)(2,1)S(1)} %collective-permute-done.6.refs_1_), channel_id=1, source_target_pairs={{0,2},{2,0},{4,6},{6,4},{8,10},{10,8},{12,14},{14,12},{16,18},{18,... | collective-permute-start | bytes 393224 | tf_op jit(solution)/shard_map/ppermute | solution.py:346
  18.5 5.4 %collective-permute-start.10 = (f32[2,4,16,256]{3,2,1,0:T(8,128)S(1)}, f32[2,4,16,256]{3,2,1,0:T(8,128)S(1)}, u32[]{:S(2)}, u32[]{:S(2)}) collective-permute-start(f32[2,4,16,256]{3,2,1,0:T(8,128)S(1)} %bitcast.2), channel_id=1, source_target_pairs={{0,1},{1,0},{2,3},{3,2},{4,5},{5,4},{6,7},{7,6},{8,9},{9,8},{10,11... | collective-permute-start | bytes 393224 | tf_op jit(solution)/shard_map/ppermute | solution.py:455

commit v5 on v4

--- a/solution.py
+++ b/solution.py
@@ -7,6 +7,9 @@
 from jax.experimental import pallas as pl
 from jax.experimental.pallas import tpu as pltpu
 from jax.sharding import PartitionSpec as P
+
+
+SPARE_ROWS = 8
 
 
 @functools.lru_cache
@@ -295,6 +298,7 @@
                 outs[0][j, q] = field[q]
         return
     mine, others = outs
+    others[...] = jnp.zeros_like(others)
     rows = mine.shape[2]
     parts = edge // rows
     for k in range(parts):
@@ -306,7 +310,7 @@
                 if k == 0:
                     mine[j, q] = piece
                 else:
-                    others[k - 1, j, q] = piece
+                    others[k - 1, (4 * j + q) * rows : (4 * j + q + 1) * rows, :] = piece
 
 
 def gate_kernel(_, out):
@@ -319,8 +323,10 @@
     for j, field in enumerate(unfold(fields, table[...])):
         res_total[j] = field
     total = []
+    size = parts[0].shape[2]
     for j in range(parts[0].shape[0]):
-        total.append([sum((part[j, q] for part in parts[1:]), parts[0][j, q]) for q in range(4)])
+        starts = [(4 * j + q) * size for q in range(4)]
+        total.append([sum((part[k : k + size, :] for part in parts[1:]), parts[0][j, q]) for q, k in enumerate(starts)])
     for j, field in enumerate(unfold(total, table[...])):
         trav_total[j] = field
 
@@ -395,7 +401,7 @@
         if cut:
             out_shape = (
                 jax.ShapeDtypeStruct((number, 4, part, plane // 4), jnp.float32),
-                jax.ShapeDtypeStruct((groups - 1, number, 4, part, plane // 4), jnp.float32),
+                jax.ShapeDtypeStruct((groups - 1, number * 4 * part + SPARE_ROWS, plane // 4), jnp.float32),
             )
         else:
             out_shape = jax.ShapeDtypeStruct((number, 4, edge, plane // 4), jnp.float32)
@@ -421,7 +427,8 @@
     ends = [(2, (0, 2 * last))]
 
     res_moved = [from_behind(packed, -s) for s in direct]
-    res_swapped = [other_core(packed)] + [other_core(value) for value in res_moved]
+    res_moved[last], own, moving = lax.optimization_barrier((res_moved[last], packed, moving))
+    res_swapped = [other_core(own)] + [other_core(value) for value in res_moved]
     passed, packed_first = lax.optimization_barrier((travellers, packed))
     trav_moved = [from_behind(passed, s) for s in direct]
     trav_swapped = [other_core(passed)]
@@ -440,8 +447,9 @@
     arrived = gate(res_moved[0], 20)
 
     home = (packed, moving)
-    blocks = [res_moved[last], res_swapped[0], res_swapped[-1]]
-    total = stage([straight(last)] + ends, blocks, home, None, True, 10, "early_traveller_terms")
+    total = stage([straight(last)], [res_moved[last]], home, None, True, 10, "first_traveller_terms")
+    blocks = [res_swapped[0], res_swapped[-1]]
+    total = stage(ends, blocks, home, total, True, 10, "early_traveller_terms")
     for k in range(last):
         res_moved[k], total = lax.optimization_barrier((res_moved[k], total))
         total = stage([straight(k)], [res_moved[k]], home, total, True, 1, "middle_traveller_terms")
@@ -455,16 +463,19 @@
         lax.ppermute(others[k - 1], "grp", [(g, (g + k) % groups) for g in range(groups)])
         for k in range(1, groups)
     ]
-    res_total = stage(
-        [straight(k) for k in range(arrivals)] + middle + ends,
-        [*trav_moved, *trav_swapped[1:-1], trav_swapped[0], trav_swapped[-1]],
-        (packed, packed),
+    home = (packed, packed)
+    total = stage(
+        [straight(k) for k in range(arrivals)],
+        trav_moved,
+        home,
         None,
         False,
-        0.5,
-        "resident_terms",
+        0.001,
+        "early_resident_terms",
         after=(summed,),
     )
+    blocks = [*trav_swapped[1:-1], trav_swapped[0], trav_swapped[-1]]
+    res_total = stage(middle + ends, blocks, home, total, False, 0.001, "late_resident_terms")
     res_total, sent = lax.optimization_barrier((res_total, sent))
     parts = [mine, *sent]
     trav_total, res_total = pl.pallas_call(

time: 25.2 us -> 24.5 us (0.972)
  waiting for transfers between devices: 3.86 us -> 1.9 us
  Pallas kernels: 9.58 us -> 10.7 us
    pallas_call x4 -> x6, Pallas kernels: 6.16 us -> 7.28 us  [stage(): pl.pallas_call(functools.partial(terms_kernel, plan, total is not None, c...]
    ppermute x1, waiting for transfers between devices: 1.13 us -> 0.17 us  [local(): lax.ppermute(others[k - 1], 'grp', [(g, (g + k) % groups) for g in range(...]
    ppermute x4, waiting for transfers between devices: 2.14 us -> 1.47 us  [from_behind(): lax.ppermute(value, 'blk', [(i, (i + by) % peers) for i in range(peers)])]
    ppermute x6, waiting for transfers between devices: 0.59 us -> 0.26 us  [other_core(): return lax.ppermute(value, 'blk', [(i, i ^ 1) for i in range(peers)])]
  transfers between devices with their start and end apart: 11 -> 11, of which waited for: 6 -> 4; matrix products, arithmetic and copies ran while one was open for 0% -> 0% of each run, Pallas kernels for 27% -> 32%
where the time goes in v5:
time: 24.5 us; the launch traced here: 24.3 us
  starting transfers between devices  10.9 us (44%)
  Pallas kernels  10.7 us (44%)
  waiting for transfers between devices  1.9 us (8%)
  between operations  0.79 us (3%)
    ppermute x4, starting transfers between devices, from_behind(): lax.ppermute(value, 'blk', [(i, (i + by) % peers) for i in range(peers)])  8.06 us
    pallas_call x6, Pallas kernels, stage(): pl.pallas_call(functools.partial(terms_kernel, plan, total is not None, c...  7.28 us
    pallas_call x1, Pallas kernels, local(): pl.pallas_call(functools.partial(pack_kernel, ('blk', 'grp')), out_shape=...  1.82 us
    ppermute x1, starting transfers between devices, local(): lax.ppermute(others[k - 1], 'grp', [(g, (g + k) % groups) for g in range(...  1.58 us
    ppermute x4, waiting for transfers between devices, from_behind(): lax.ppermute(value, 'blk', [(i, (i + by) % peers) for i in range(peers)])  1.47 us
    ppermute x6, starting transfers between devices, other_core(): return lax.ppermute(value, 'blk', [(i, i ^ 1) for i in range(peers)])  1.29 us
    pallas_call x1, Pallas kernels, local(): pl.pallas_call(functools.partial(sum_kernel, len(parts)), out_shape=(jax....  1.12 us
  transfers between devices with their start and end apart: 11, of which 4 were waited for; matrix products, arithmetic and copies ran while one was open for 0% of the time, Pallas kernels for 32%

profile of v5, /device:TPU:0, one launch (start us, length us, event | category | flops | bytes accessed | tf_op | source)
XLA Modules:
  0.0 24.3 jit_solution(3186032860420652043)
XLA Ops:
  0.6 0.0 copy-start.2
  0.7 1.8 %pack.1.refs_1_.refs_2_.refs_3_.refs_4_ = bf16[544,128]{1,0:T(8,128)(2,1)} custom-call(bf16[2,32,1024]{2,1,0:T(8,128)(2,1)} %residents.1, s32[1,3,2,4]{3,2,1,0:T(2,128)} %bitcast.3), custom_call_target="tpu_custom_call" | custom-call | flops 1000000000 | bytes 1024 | tf_op jit(solution)/shard_map/pack/pallas_call | solution.py:367
  2.5 0.0 copy-start
  2.5 5.1 %collective-permute-start.1 = (bf16[544,128]{1,0:T(8,128)(2,1)}, bf16[544,128]{1,0:T(8,128)(2,1)S(1)}, u32[]{:S(2)}, u32[]{:S(2)}) collective-permute-start(bf16[544,128]{1,0:T(8,128)(2,1)} %pack.1.refs_1_.refs_2_.refs_3_.refs_4_), channel_id=1, source_target_pairs={{0,24},{2,26},{4,28},{6,30},{8,0},{10,2},{12,4},{14,6},{16,8},{18,... | collective-permute-start | bytes 417800 | tf_op jit(solution)/shard_map/ppermute | solution.py:347
  7.6 1.4 %collective-permute-start = (bf16[544,128]{1,0:T(8,128)(2,1)}, bf16[544,128]{1,0:T(8,128)(2,1)S(1)}, u32[]{:S(2)}, u32[]{:S(2)}) collective-permute-start(bf16[544,128]{1,0:T(8,128)(2,1)} %pack.1.refs_1_.refs_2_.refs_3_.refs_4_), channel_id=1, source_target_pairs={{0,28},{2,30},{4,0},{6,2},{8,4},{10,6},{12,8},{14,10},{16,12},{18,... | collective-permute-start | bytes 417800 | tf_op jit(solution)/shard_map/ppermute | solution.py:347
  9.0 0.6 %collective-permute-start.5 = (bf16[2,32,1024]{2,1,0:T(8,128)(2,1)S(1)}, bf16[2,32,1024]{2,1,0:T(8,128)(2,1)S(1)}, u32[]{:S(2)}, u32[]{:S(2)}) collective-permute-start(bf16[2,32,1024]{2,1,0:T(8,128)(2,1)S(1)} %copy-done.1), channel_id=1, source_target_pairs={{0,4},{2,6},{4,8},{6,10},{8,12},{10,14},{12,16},{14,18},{16,20},{1... | collective-permute-start | bytes 393224 | tf_op jit(solution)/shard_map/ppermute | solution.py:347
  9.6 0.9 %collective-permute-start.6 = (bf16[2,32,1024]{2,1,0:T(8,128)(2,1)S(1)}, bf16[2,32,1024]{2,1,0:T(8,128)(2,1)S(1)}, u32[]{:S(2)}, u32[]{:S(2)}) collective-permute-start(bf16[2,32,1024]{2,1,0:T(8,128)(2,1)S(1)} %copy-done.1), channel_id=1, source_target_pairs={{0,8},{2,10},{4,12},{6,14},{8,16},{10,18},{12,20},{14,22},{16,24},... | collective-permute-start | bytes 393224 | tf_op jit(solution)/shard_map/ppermute | solution.py:347
  10.6 0.5 %tables.1 = (bf16[512,256]{1,0:T(8,128)(2,1)S(1)}, bf16[256,128]{1,0:T(8,128)(2,1)S(1)}, f32[32,1024]{1,0:T(8,128)S(1)}, bf16[512,512]{1,0:T(8,128)(2,1)S(1)}, b...) custom-call(f32[72,256]{1,0:T(8,128)S(1)} %copy-done.2, bf16[2,32,1024]{2,1,0:T(8,128)(2,1)S(1)} %copy-done.1), custom_call_target="tpu_custom_call" | custom-call | flops 20000000000 | bytes 1024 | tf_op jit(solution)/shard_map/tables/pallas_call | solution.py:382
  11.0 1.0 %collective-permute-done.1.refs_0_ = bf16[544,128]{1,0:T(8,128)(2,1)S(1)} collective-permute-done((bf16[544,128]{1,0:T(8,128)(2,1)}, bf16[544,128]{1,0:T(8,128)(2,1)S(1)}, u32[]{:S(2)}, u32[]{:S(2)}) %collective-permute-start.1) | collective-permute-done | bytes 139296 | tf_op jit(solution)/shard_map/ppermute | solution.py:347
  12.1 0.0 collective-permute-start.3
  12.1 0.5 %collective-permute-start.2 = (bf16[544,128]{1,0:T(8,128)(2,1)S(1)}, bf16[544,128]{1,0:T(8,128)(2,1)S(1)}, u32[]{:S(2)}, u32[]{:S(2)}) collective-permute-start(bf16[544,128]{1,0:T(8,128)(2,1)S(1)} %copy-done), channel_id=1, source_target_pairs={{0,2},{2,0},{4,6},{6,4},{8,10},{10,8},{12,14},{14,12},{16,18},{18,... | collective-permute-start | bytes 417800 | tf_op jit(solution)/shard_map/ppermute | solution.py:352
  12.6 1.0 %first_traveller_terms.1.refs_8_ = f32[2,4,32,256]{3,2,1,0:T(8,128)S(1)} custom-call(bf16[544,128]{1,0:T(8,128)(2,1)S(1)} %collective-permute-done.1.refs_0_, bf16[544,128]{1,0:T(8,128)(2,1)S(1)} %copy-done, bf16[512,128]{1,0:T(8,128)(2,1)S(1)} %get-tuple-element.26.refs_2_.refs_3_, bf16[512,256]{1,0:T(8,128)(2,1)S(1)} %get-tuple-element.27.refs_3_.refs_4_.refs_5_, ...), custom_call_target="tpu_custom_call" | custom-call | flops 10000000000 | bytes 1024 | tf_op jit(solution)/shard_map/first_traveller_terms/pallas_call | solution.py:409
  13.6 0.0 collective-permute-done.3.refs_1_
  13.6 0.1 collective-permute-start.8
  13.7 0.0 collective-permute-done.2.refs_0_
  13.7 1.0 %early_traveller_terms.1.refs_7_ = f32[2,4,32,256]{3,2,1,0:T(8,128)S(1)} custom-call(bf16[544,128]{1,0:T(8,128)(2,1)S(1)} %collective-permute-done.2.refs_0_, bf16[544,128]{1,0:T(8,128)(2,1)S(1)} %collective-permute-done.3.refs_1_, bf16[544,128]{1,0:T(8,128)(2,1)S(1)} %copy-done, bf16[512,128]{1,0:T(8,128)(2,1)S(1)} %get-tuple-element.26.refs_2_.refs_3_, ...), custom_call_target="tpu_custom_call" | custom-call | flops 10000000000 | bytes 1024 | tf_op jit(solution)/shard_map/early_traveller_terms/pallas_call | solution.py:409
  14.7 0.4 %collective-permute-done.refs_0_._ = bf16[544,128]{1,0:T(8,128)(2,1)S(1)} collective-permute-done((bf16[544,128]{1,0:T(8,128)(2,1)}, bf16[544,128]{1,0:T(8,128)(2,1)S(1)}, u32[]{:S(2)}, u32[]{:S(2)}) %collective-permute-start) | collective-permute-done | bytes 139296 | tf_op jit(solution)/shard_map/ppermute | solution.py:347
  15.1 0.1 collective-permute-start.4
  15.2 1.0 %middle_traveller_terms.1.refs_7_ = f32[2,4,32,256]{3,2,1,0:T(8,128)S(1)} custom-call(bf16[544,128]{1,0:T(8,128)(2,1)S(1)} %collective-permute-done.refs_0_._, bf16[544,128]{1,0:T(8,128)(2,1)S(1)} %copy-done, bf16[512,128]{1,0:T(8,128)(2,1)S(1)} %get-tuple-element.26.refs_2_.refs_3_, bf16[512,256]{1,0:T(8,128)(2,1)S(1)} %get-tuple-element.27.refs_3_.refs_4_.refs_5_, ...), custom_call_target="tpu_custom_call" | custom-call | flops 1000000000 | bytes 1024 | tf_op jit(solution)/shard_map/middle_traveller_terms/pallas_call | solution.py:409
  16.2 0.2 collective-permute-done.4.refs_0_
  16.4 1.0 %late_traveller_terms.1 = (f32[2,4,16,256]{3,2,1,0:T(8,128)S(1)}, f32[1,136,256]{2,1,0:T(8,128)S(1)}) custom-call(bf16[544,128]{1,0:T(8,128)(2,1)S(1)} %collective-permute-done.4.refs_0_, bf16[544,128]{1,0:T(8,128)(2,1)S(1)} %copy-done, bf16[512,128]{1,0:T(8,128)(2,1)S(1)} %get-tuple-element.26.refs_2_.refs_3_, ...), custom_call_target="tpu_custom_call" | custom-call | flops 2000000000 | bytes 1024 | tf_op jit(solution)/shard_map/late_traveller_terms/pallas_call | solution.py:409
  17.4 1.6 %collective-permute-start.10 = (f32[136,256]{1,0:T(8,128)S(1)}, f32[136,256]{1,0:T(8,128)S(1)}, u32[]{:S(2)}, u32[]{:S(2)}) collective-permute-start(f32[136,256]{1,0:T(8,128)S(1)} %bitcast.2), channel_id=1, source_target_pairs={{0,1},{1,0},{2,3},{3,2},{4,5},{5,4},{6,7},{7,6},{8,9},{9,8},{10,11... | collective-permute-start | bytes 417800 | tf_op jit(solution)/shard_map/ppermute | solution.py:463
  19.0 0.0 collective-permute-done.5.refs_0_
  19.0 0.0 collective-permute-done.6.refs_1_
  19.0 0.1 collective-permute-start.7
  19.1 0.5 %collective-permute-start.9 = (bf16[2,32,1024]{2,1,0:T(8,128)(2,1)S(1)}, bf16[2,32,1024]{2,1,0:T(8,128)(2,1)S(1)}, u32[]{:S(2)}, u32[]{:S(2)}) collective-permute-start(bf16[2,32,1024]{2,1,0:T(8,128)(2,1)S(1)} %collective-permute-done.6.refs_1_), channel_id=1, source_target_pairs={{0,2},{2,0},{4,6},{6,4},{8,10},{10,8},{12,14},{14,12},{16,18},{18,... | collective-permute-start | bytes 393224 | tf_op jit(solution)/shard_map/ppermute | solution.py:352
  19.6 1.7 %early_resident_terms.1.refs_9_ = f32[2,4,32,256]{3,2,1,0:T(8,128)S(1)} custom-call(bf16[2,32,1024]{2,1,0:T(8,128)(2,1)S(1)} %collective-permute-done.5.refs_0_, bf16[2,32,1024]{2,1,0:T(8,128)(2,1)S(1)} %collective-permute-done.6.refs_1_, bf16[544,128]{1,0:T(8,128)(2,1)S(1)} %copy-done, bf16[544,128]{1,0:T(8,128)(2,1)S(1)} %copy-done, ...), custom_call_target="tpu_custom_call" | custom-call | flops 1000000 | bytes 1024 | tf_op jit(solution)/shard_map/early_resident_terms/pallas_call | solution.py:409
  21.3 0.0 collective-permute-done.7.refs_0_
  21.3 0.0 collective-permute-done.9.refs_2_
  21.3 1.7 %late_resident_terms.1.refs_3_ = f32[2,4,32,256]{3,2,1,0:T(8,128)S(1)} custom-call(bf16[2,32,1024]{2,1,0:T(8,128)(2,1)S(1)} %collective-permute-done.7.refs_0_, bf16[2,32,1024]{2,1,0:T(8,128)(2,1)S(1)} %collective-permute-done.8.refs_1_, bf16[2,32,1024]{2,1,0:T(8,128)(2,1)S(1)} %collective-permute-done.9.refs_2_, bf16[544,128]{1,0:T(8,128)(2,1)S(1)} %copy-done, ...), custom_call_target="tpu_custom_call" | custom-call | flops 1000000 | bytes 1024 | tf_op jit(solution)/shard_map/late_resident_terms/pallas_call | solution.py:409
  23.0 0.2 collective-permute-done.10.refs_1_
  23.2 1.1 %sums.1 = (f32[2,16,1024]{2,1,0:T(8,128)}, f32[2,32,1024]{2,1,0:T(8,128)}) custom-call(f32[2,4,16,256]{3,2,1,0:T(8,128)S(1)} %get-tuple-element.33.refs_0_, f32[136,256]{1,0:T(8,128)S(1)} %collective-permute-done.10.refs_1_, bf16[512,512]{1,0:T(8,128)(2,1)S(1)} %get-tuple-element.40.refs_2_, f32[2,4,32,256]{3,2,1,0:T(8,128)S(1)} %late_resident_terms.1.refs_3_), custom_call_target="tpu_custom_call" | custom-call | flops 500000000 | bytes 1024 | tf_op jit(solution)/shard_map/sums/pallas_call | solution.py:481
  (7 shorter events, 0.0 us)
Async XLA Ops:
  0.6 8.3 %copy-start.1 = (bf16[2,32,1024]{2,1,0:T(8,128)(2,1)S(1)}, bf16[2,32,1024]{2,1,0:T(8,128)(2,1)}, u32[]{:S(2)}) copy-start(bf16[2,32,1024]{2,1,0:T(8,128)(2,1)} %travellers.1) | copy-start | bytes 393220
  0.6 9.9 %copy-start.2 = (f32[72,256]{1,0:T(8,128)S(1)}, f32[72,256]{1,0:T(8,128)}, u32[]{:S(2)}) copy-start(f32[72,256]{1,0:T(8,128)} %constant.2.clone.small) | copy-start | bytes 221188
  2.5 9.6 %copy-start = (bf16[544,128]{1,0:T(8,128)(2,1)S(1)}, bf16[544,128]{1,0:T(8,128)(2,1)}, u32[]{:S(2)}) copy-start(bf16[544,128]{1,0:T(8,128)(2,1)} %pack.1.refs_1_.refs_2_.refs_3_.refs_4_) | copy-start | bytes 417796
  2.5 9.6 %collective-permute-start.1 = (bf16[544,128]{1,0:T(8,128)(2,1)}, bf16[544,128]{1,0:T(8,128)(2,1)S(1)}, u32[]{:S(2)}, u32[]{:S(2)}) collective-permute-start(bf16[544,128]{1,0:T(8,128)(2,1)} %pack.1.refs_1_.refs_2_.refs_3_.refs_4_), channel_id=1, source_target_pairs={{0,24},{2,26},{4,28},{6,30},{8,0},{10,2},{12,4},{14,6},{16,8},{18,... | collective-permute-start | bytes 417800 | tf_op jit(solution)/shard_map/ppermute | solution.py:347
  7.6 7.5 %collective-permute-start = (bf16[544,128]{1,0:T(8,128)(2,1)}, bf16[544,128]{1,0:T(8,128)(2,1)S(1)}, u32[]{:S(2)}, u32[]{:S(2)}) collective-permute-start(bf16[544,128]{1,0:T(8,128)(2,1)} %pack.1.refs_1_.refs_2_.refs_3_.refs_4_), channel_id=1, source_target_pairs={{0,28},{2,30},{4,0},{6,2},{8,4},{10,6},{12,8},{14,10},{16,12},{18,... | collective-permute-start | bytes 417800 | tf_op jit(solution)/shard_map/ppermute | solution.py:347
  9.0 10.0 %collective-permute-start.5 = (bf16[2,32,1024]{2,1,0:T(8,128)(2,1)S(1)}, bf16[2,32,1024]{2,1,0:T(8,128)(2,1)S(1)}, u32[]{:S(2)}, u32[]{:S(2)}) collective-permute-start(bf16[2,32,1024]{2,1,0:T(8,128)(2,1)S(1)} %copy-done.1), channel_id=1, source_target_pairs={{0,4},{2,6},{4,8},{6,10},{8,12},{10,14},{12,16},{14,18},{16,20},{1... | collective-permute-start | bytes 393224 | tf_op jit(solution)/shard_map/ppermute | solution.py:347
  9.6 9.4 %collective-permute-start.6 = (bf16[2,32,1024]{2,1,0:T(8,128)(2,1)S(1)}, bf16[2,32,1024]{2,1,0:T(8,128)(2,1)S(1)}, u32[]{:S(2)}, u32[]{:S(2)}) collective-permute-start(bf16[2,32,1024]{2,1,0:T(8,128)(2,1)S(1)} %copy-done.1), channel_id=1, source_target_pairs={{0,8},{2,10},{4,12},{6,14},{8,16},{10,18},{12,20},{14,22},{16,24},... | collective-permute-start | bytes 393224 | tf_op jit(solution)/shard_map/ppermute | solution.py:347
  12.1 1.5 %collective-permute-start.3 = (bf16[544,128]{1,0:T(8,128)(2,1)S(1)}, bf16[544,128]{1,0:T(8,128)(2,1)S(1)}, u32[]{:S(2)}, u32[]{:S(2)}) collective-permute-start(bf16[544,128]{1,0:T(8,128)(2,1)S(1)} %collective-permute-done.1.refs_0_), channel_id=1, source_target_pairs={{0,2},{2,0},{4,6},{6,4},{8,10},{10,8},{12,14},{14,12},{16,18},{18,... | collective-permute-start | bytes 417800 | tf_op jit(solution)/shard_map/ppermute | solution.py:352
  12.1 1.6 %collective-permute-start.2 = (bf16[544,128]{1,0:T(8,128)(2,1)S(1)}, bf16[544,128]{1,0:T(8,128)(2,1)S(1)}, u32[]{:S(2)}, u32[]{:S(2)}) collective-permute-start(bf16[544,128]{1,0:T(8,128)(2,1)S(1)} %copy-done), channel_id=1, source_target_pairs={{0,2},{2,0},{4,6},{6,4},{8,10},{10,8},{12,14},{14,12},{16,18},{18,... | collective-permute-start | bytes 417800 | tf_op jit(solution)/shard_map/ppermute | solution.py:352
  13.6 7.7 %collective-permute-start.8 = (bf16[2,32,1024]{2,1,0:T(8,128)(2,1)S(1)}, bf16[2,32,1024]{2,1,0:T(8,128)(2,1)S(1)}, u32[]{:S(2)}, u32[]{:S(2)}) collective-permute-start(bf16[2,32,1024]{2,1,0:T(8,128)(2,1)S(1)} %copy-done.1), channel_id=1, source_target_pairs={{0,2},{2,0},{4,6},{6,4},{8,10},{10,8},{12,14},{14,12},{16,18},{18,... | collective-permute-start | bytes 393224 | tf_op jit(solution)/shard_map/ppermute | solution.py:352
  15.1 1.4 %collective-permute-start.4 = (bf16[544,128]{1,0:T(8,128)(2,1)S(1)}, bf16[544,128]{1,0:T(8,128)(2,1)S(1)}, u32[]{:S(2)}, u32[]{:S(2)}) collective-permute-start(bf16[544,128]{1,0:T(8,128)(2,1)S(1)} %collective-permute-done.refs_0_._), channel_id=1, source_target_pairs={{0,2},{2,0},{4,6},{6,4},{8,10},{10,8},{12,14},{14,12},{16,18},{18,... | collective-permute-start | bytes 417800 | tf_op jit(solution)/shard_map/ppermute | solution.py:352
  17.4 5.8 %collective-permute-start.10 = (f32[136,256]{1,0:T(8,128)S(1)}, f32[136,256]{1,0:T(8,128)S(1)}, u32[]{:S(2)}, u32[]{:S(2)}) collective-permute-start(f32[136,256]{1,0:T(8,128)S(1)} %bitcast.2), channel_id=1, source_target_pairs={{0,1},{1,0},{2,3},{3,2},{4,5},{5,4},{6,7},{7,6},{8,9},{9,8},{10,11... | collective-permute-start | bytes 417800 | tf_op jit(solution)/shard_map/ppermute | solution.py:463
  19.0 2.3 %collective-permute-start.7 = (bf16[2,32,1024]{2,1,0:T(8,128)(2,1)S(1)}, bf16[2,32,1024]{2,1,0:T(8,128)(2,1)S(1)}, u32[]{:S(2)}, u32[]{:S(2)}) collective-permute-start(bf16[2,32,1024]{2,1,0:T(8,128)(2,1)S(1)} %collective-permute-done.5.refs_0_), channel_id=1, source_target_pairs={{0,2},{2,0},{4,6},{6,4},{8,10},{10,8},{12,14},{14,12},{16,18},{18,... | collective-permute-start | bytes 393224 | tf_op jit(solution)/shard_map/ppermute | solution.py:352
  19.1 2.2 %collective-permute-start.9 = (bf16[2,32,1024]{2,1,0:T(8,128)(2,1)S(1)}, bf16[2,32,1024]{2,1,0:T(8,128)(2,1)S(1)}, u32[]{:S(2)}, u32[]{:S(2)}) collective-permute-start(bf16[2,32,1024]{2,1,0:T(8,128)(2,1)S(1)} %collective-permute-done.6.refs_1_), channel_id=1, source_target_pairs={{0,2},{2,0},{4,6},{6,4},{8,10},{10,8},{12,14},{14,12},{16,18},{18,... | collective-permute-start | bytes 393224 | tf_op jit(solution)/shard_map/ppermute | solution.py:352

commit v6 on v5

--- a/solution.py
+++ b/solution.py
@@ -10,6 +10,7 @@
 
 
 SPARE_ROWS = 8
+LANES = 128
 
 
 @functools.lru_cache
@@ -82,17 +83,22 @@
 
 
 def times_table(x, table):
-    x_high, x_low = halves(x)
     high, low = table[: table.shape[0] // 2], table[table.shape[0] // 2 :]
-    return dot(x_high, high) + (dot(x_low, high) + dot(x_high, low))
+    parts = []
+    for start in range(0, x.shape[0], LANES):
+        x_high, x_low = halves(x[start : start + LANES])
+        parts.append(dot(x_high, high) + (dot(x_low, high) + dot(x_high, low)))
+    return jnp.concatenate(parts, axis=0)
 
 
 def table_times(table, x):
-    x_high, x_low = halves(x)
     high, low = table[: table.shape[0] // 2], table[table.shape[0] // 2 :]
-    return dot(
-        jnp.concatenate([high, high, low], axis=1), jnp.concatenate([x_high, x_low, x_high], axis=0)
-    )
+    table = jnp.concatenate([high, high, low], axis=1)
+    parts = []
+    for start in range(0, x.shape[1], 2 * LANES):
+        x_high, x_low = halves(x[:, start : start + 2 * LANES])
+        parts.append(dot(table, jnp.concatenate([x_high, x_low, x_high], axis=0)))
+    return jnp.concatenate(parts, axis=1)
 
 
 def spread(quadrants):

time: 24.5 us -> 24.5 us (level)
  waiting for transfers between devices: 1.9 us -> 2.59 us
  Pallas kernels: 10.7 us -> 10.1 us
    pallas_call x6, Pallas kernels: 7.28 us -> 6.66 us  [stage(): pl.pallas_call(functools.partial(terms_kernel, plan, total is not None, c...]
    ppermute x1, waiting for transfers between devices: 0.17 us -> 0.57 us  [local(): lax.ppermute(others[k - 1], 'grp', [(g, (g + k) % groups) for g in range(...]
  transfers between devices with their start and end apart: 11 -> 11, of which waited for: 4 -> 5; matrix products, arithmetic and copies ran while one was open for 0% -> 0% of each run, Pallas kernels for 32% -> 29%
where the time goes in v6:
time: 24.5 us; the launch traced here: 24.3 us
  starting transfers between devices  10.8 us (44%)
  Pallas kernels  10.1 us (41%)
  waiting for transfers between devices  2.59 us (11%)
  between operations  0.77 us (3%)
    ppermute x4, starting transfers between devices, from_behind(): lax.ppermute(value, 'blk', [(i, (i + by) % peers) for i in range(peers)])  8.06 us
    pallas_call x6, Pallas kernels, stage(): pl.pallas_call(functools.partial(terms_kernel, plan, total is not None, c...  6.66 us
    pallas_call x1, Pallas kernels, local(): pl.pallas_call(functools.partial(pack_kernel, ('blk', 'grp')), out_shape=...  1.82 us
    ppermute x1, starting transfers between devices, local(): lax.ppermute(others[k - 1], 'grp', [(g, (g + k) % groups) for g in range(...  1.58 us
    ppermute x4, waiting for transfers between devices, from_behind(): lax.ppermute(value, 'blk', [(i, (i + by) % peers) for i in range(peers)])  1.54 us
    ppermute x6, starting transfers between devices, other_core(): return lax.ppermute(value, 'blk', [(i, i ^ 1) for i in range(peers)])  1.18 us
    pallas_call x1, Pallas kernels, local(): pl.pallas_call(functools.partial(sum_kernel, len(parts)), out_shape=(jax....  1.12 us
    ppermute x1, waiting for transfers between devices, local(): lax.ppermute(others[k - 1], 'grp', [(g, (g + k) % groups) for g in range(...  0.57 us
  transfers between devices with their start and end apart: 11, of which 5 were waited for; matrix products, arithmetic and copies ran while one was open for 0% of the time, Pallas kernels for 29%

profile of v6, /device:TPU:0, one launch (start us, length us, event | category | flops | bytes accessed | tf_op | source)
XLA Modules:
  0.0 24.3 jit_solution(18319742813658722475)
XLA Ops:
  0.6 0.0 copy-start.2
  0.7 1.8 %pack.1.refs_1_.refs_2_.refs_3_.refs_4_ = bf16[544,128]{1,0:T(8,128)(2,1)} custom-call(bf16[2,32,1024]{2,1,0:T(8,128)(2,1)} %residents.1, s32[1,3,2,4]{3,2,1,0:T(2,128)} %bitcast.3), custom_call_target="tpu_custom_call" | custom-call | flops 1000000000 | bytes 1024 | tf_op jit(solution)/shard_map/pack/pallas_call | solution.py:373
  2.5 0.0 copy-start
  2.5 5.1 %collective-permute-start.1 = (bf16[544,128]{1,0:T(8,128)(2,1)}, bf16[544,128]{1,0:T(8,128)(2,1)S(1)}, u32[]{:S(2)}, u32[]{:S(2)}) collective-permute-start(bf16[544,128]{1,0:T(8,128)(2,1)} %pack.1.refs_1_.refs_2_.refs_3_.refs_4_), channel_id=1, source_target_pairs={{0,24},{2,26},{4,28},{6,30},{8,0},{10,2},{12,4},{14,6},{16,8},{18,... | collective-permute-start | bytes 417800 | tf_op jit(solution)/shard_map/ppermute | solution.py:353
  7.6 1.4 %collective-permute-start = (bf16[544,128]{1,0:T(8,128)(2,1)}, bf16[544,128]{1,0:T(8,128)(2,1)S(1)}, u32[]{:S(2)}, u32[]{:S(2)}) collective-permute-start(bf16[544,128]{1,0:T(8,128)(2,1)} %pack.1.refs_1_.refs_2_.refs_3_.refs_4_), channel_id=1, source_target_pairs={{0,28},{2,30},{4,0},{6,2},{8,4},{10,6},{12,8},{14,10},{16,12},{18,... | collective-permute-start | bytes 417800 | tf_op jit(solution)/shard_map/ppermute | solution.py:353
  9.0 0.6 %collective-permute-start.5 = (bf16[2,32,1024]{2,1,0:T(8,128)(2,1)S(1)}, bf16[2,32,1024]{2,1,0:T(8,128)(2,1)S(1)}, u32[]{:S(2)}, u32[]{:S(2)}) collective-permute-start(bf16[2,32,1024]{2,1,0:T(8,128)(2,1)S(1)} %copy-done.1), channel_id=1, source_target_pairs={{0,4},{2,6},{4,8},{6,10},{8,12},{10,14},{12,16},{14,18},{16,20},{1... | collective-permute-start | bytes 393224 | tf_op jit(solution)/shard_map/ppermute | solution.py:353
  9.6 0.9 %collective-permute-start.6 = (bf16[2,32,1024]{2,1,0:T(8,128)(2,1)S(1)}, bf16[2,32,1024]{2,1,0:T(8,128)(2,1)S(1)}, u32[]{:S(2)}, u32[]{:S(2)}) collective-permute-start(bf16[2,32,1024]{2,1,0:T(8,128)(2,1)S(1)} %copy-done.1), channel_id=1, source_target_pairs={{0,8},{2,10},{4,12},{6,14},{8,16},{10,18},{12,20},{14,22},{16,24},... | collective-permute-start | bytes 393224 | tf_op jit(solution)/shard_map/ppermute | solution.py:353
  10.6 0.5 %tables.1 = (bf16[512,256]{1,0:T(8,128)(2,1)S(1)}, bf16[256,128]{1,0:T(8,128)(2,1)S(1)}, f32[32,1024]{1,0:T(8,128)S(1)}, bf16[512,512]{1,0:T(8,128)(2,1)S(1)}, b...) custom-call(f32[72,256]{1,0:T(8,128)S(1)} %copy-done.2, bf16[2,32,1024]{2,1,0:T(8,128)(2,1)S(1)} %copy-done.1), custom_call_target="tpu_custom_call" | custom-call | flops 20000000000 | bytes 1024 | tf_op jit(solution)/shard_map/tables/pallas_call | solution.py:388
  11.0 1.0 %collective-permute-done.1.refs_0_ = bf16[544,128]{1,0:T(8,128)(2,1)S(1)} collective-permute-done((bf16[544,128]{1,0:T(8,128)(2,1)}, bf16[544,128]{1,0:T(8,128)(2,1)S(1)}, u32[]{:S(2)}, u32[]{:S(2)}) %collective-permute-start.1) | collective-permute-done | bytes 139296 | tf_op jit(solution)/shard_map/ppermute | solution.py:353
  12.1 0.0 collective-permute-start.3
  12.1 0.5 %collective-permute-start.2 = (bf16[544,128]{1,0:T(8,128)(2,1)S(1)}, bf16[544,128]{1,0:T(8,128)(2,1)S(1)}, u32[]{:S(2)}, u32[]{:S(2)}) collective-permute-start(bf16[544,128]{1,0:T(8,128)(2,1)S(1)} %copy-done), channel_id=1, source_target_pairs={{0,2},{2,0},{4,6},{6,4},{8,10},{10,8},{12,14},{14,12},{16,18},{18,... | collective-permute-start | bytes 417800 | tf_op jit(solution)/shard_map/ppermute | solution.py:358
  12.6 0.9 %first_traveller_terms.1.refs_8_ = f32[2,4,32,256]{3,2,1,0:T(8,128)S(1)} custom-call(bf16[544,128]{1,0:T(8,128)(2,1)S(1)} %collective-permute-done.1.refs_0_, bf16[544,128]{1,0:T(8,128)(2,1)S(1)} %copy-done, bf16[512,128]{1,0:T(8,128)(2,1)S(1)} %get-tuple-element.26.refs_2_.refs_3_, bf16[512,256]{1,0:T(8,128)(2,1)S(1)} %get-tuple-element.27.refs_3_.refs_4_.refs_5_, ...), custom_call_target="tpu_custom_call" | custom-call | flops 10000000000 | bytes 1024 | tf_op jit(solution)/shard_map/first_traveller_terms/pallas_call | solution.py:415
  13.5 0.0 collective-permute-done.3.refs_1_
  13.5 0.1 collective-permute-start.8
  13.6 0.1 collective-permute-done.2.refs_0_
  13.6 0.9 %early_traveller_terms.1.refs_7_ = f32[2,4,32,256]{3,2,1,0:T(8,128)S(1)} custom-call(bf16[544,128]{1,0:T(8,128)(2,1)S(1)} %collective-permute-done.2.refs_0_, bf16[544,128]{1,0:T(8,128)(2,1)S(1)} %collective-permute-done.3.refs_1_, bf16[544,128]{1,0:T(8,128)(2,1)S(1)} %copy-done, bf16[512,128]{1,0:T(8,128)(2,1)S(1)} %get-tuple-element.26.refs_2_.refs_3_, ...), custom_call_target="tpu_custom_call" | custom-call | flops 10000000000 | bytes 1024 | tf_op jit(solution)/shard_map/early_traveller_terms/pallas_call | solution.py:415
  14.6 0.5 %collective-permute-done.refs_0_._ = bf16[544,128]{1,0:T(8,128)(2,1)S(1)} collective-permute-done((bf16[544,128]{1,0:T(8,128)(2,1)}, bf16[544,128]{1,0:T(8,128)(2,1)S(1)}, u32[]{:S(2)}, u32[]{:S(2)}) %collective-permute-start) | collective-permute-done | bytes 139296 | tf_op jit(solution)/shard_map/ppermute | solution.py:353
  15.1 0.0 collective-permute-start.4
  15.1 0.9 %middle_traveller_terms.1.refs_7_ = f32[2,4,32,256]{3,2,1,0:T(8,128)S(1)} custom-call(bf16[544,128]{1,0:T(8,128)(2,1)S(1)} %collective-permute-done.refs_0_._, bf16[544,128]{1,0:T(8,128)(2,1)S(1)} %copy-done, bf16[512,128]{1,0:T(8,128)(2,1)S(1)} %get-tuple-element.26.refs_2_.refs_3_, bf16[512,256]{1,0:T(8,128)(2,1)S(1)} %get-tuple-element.27.refs_3_.refs_4_.refs_5_, ...), custom_call_target="tpu_custom_call" | custom-call | flops 1000000000 | bytes 1024 | tf_op jit(solution)/shard_map/middle_traveller_terms/pallas_call | solution.py:415
  16.0 0.4 %collective-permute-done.4.refs_0_ = bf16[544,128]{1,0:T(8,128)(2,1)S(1)} collective-permute-done((bf16[544,128]{1,0:T(8,128)(2,1)S(1)}, bf16[544,128]{1,0:T(8,128)(2,1)S(1)}, u32[]{:S(2)}, u32[]{:S(2)}) %collective-permute-start.4) | collective-permute-done | bytes 139296 | tf_op jit(solution)/shard_map/ppermute | solution.py:358
  16.4 0.9 %late_traveller_terms.1 = (f32[2,4,16,256]{3,2,1,0:T(8,128)S(1)}, f32[1,136,256]{2,1,0:T(8,128)S(1)}) custom-call(bf16[544,128]{1,0:T(8,128)(2,1)S(1)} %collective-permute-done.4.refs_0_, bf16[544,128]{1,0:T(8,128)(2,1)S(1)} %copy-done, bf16[512,128]{1,0:T(8,128)(2,1)S(1)} %get-tuple-element.26.refs_2_.refs_3_, ...), custom_call_target="tpu_custom_call" | custom-call | flops 2000000000 | bytes 1024 | tf_op jit(solution)/shard_map/late_traveller_terms/pallas_call | solution.py:415
  17.4 1.6 %collective-permute-start.10 = (f32[136,256]{1,0:T(8,128)S(1)}, f32[136,256]{1,0:T(8,128)S(1)}, u32[]{:S(2)}, u32[]{:S(2)}) collective-permute-start(f32[136,256]{1,0:T(8,128)S(1)} %bitcast.2), channel_id=1, source_target_pairs={{0,1},{1,0},{2,3},{3,2},{4,5},{5,4},{6,7},{7,6},{8,9},{9,8},{10,11... | collective-permute-start | bytes 417800 | tf_op jit(solution)/shard_map/ppermute | solution.py:469
  19.0 0.0 collective-permute-done.5.refs_0_
  19.0 0.0 collective-permute-done.6.refs_1_
  19.0 0.1 collective-permute-start.7
  19.0 0.5 %collective-permute-start.9 = (bf16[2,32,1024]{2,1,0:T(8,128)(2,1)S(1)}, bf16[2,32,1024]{2,1,0:T(8,128)(2,1)S(1)}, u32[]{:S(2)}, u32[]{:S(2)}) collective-permute-start(bf16[2,32,1024]{2,1,0:T(8,128)(2,1)S(1)} %collective-permute-done.6.refs_1_), channel_id=1, source_target_pairs={{0,2},{2,0},{4,6},{6,4},{8,10},{10,8},{12,14},{14,12},{16,18},{18,... | collective-permute-start | bytes 393224 | tf_op jit(solution)/shard_map/ppermute | solution.py:358
  19.5 1.5 %early_resident_terms.1.refs_9_ = f32[2,4,32,256]{3,2,1,0:T(8,128)S(1)} custom-call(bf16[2,32,1024]{2,1,0:T(8,128)(2,1)S(1)} %collective-permute-done.5.refs_0_, bf16[2,32,1024]{2,1,0:T(8,128)(2,1)S(1)} %collective-permute-done.6.refs_1_, bf16[544,128]{1,0:T(8,128)(2,1)S(1)} %copy-done, bf16[544,128]{1,0:T(8,128)(2,1)S(1)} %copy-done, ...), custom_call_target="tpu_custom_call" | custom-call | flops 1000000 | bytes 1024 | tf_op jit(solution)/shard_map/early_resident_terms/pallas_call | solution.py:415
  21.1 0.0 collective-permute-done.8.refs_1_
  21.1 0.0 collective-permute-done.9.refs_2_
  21.1 1.5 %late_resident_terms.1.refs_3_ = f32[2,4,32,256]{3,2,1,0:T(8,128)S(1)} custom-call(bf16[2,32,1024]{2,1,0:T(8,128)(2,1)S(1)} %collective-permute-done.7.refs_0_, bf16[2,32,1024]{2,1,0:T(8,128)(2,1)S(1)} %collective-permute-done.8.refs_1_, bf16[2,32,1024]{2,1,0:T(8,128)(2,1)S(1)} %collective-permute-done.9.refs_2_, bf16[544,128]{1,0:T(8,128)(2,1)S(1)} %copy-done, ...), custom_call_target="tpu_custom_call" | custom-call | flops 1000000 | bytes 1024 | tf_op jit(solution)/shard_map/late_resident_terms/pallas_call | solution.py:415
  22.6 0.6 %collective-permute-done.10.refs_1_ = f32[136,256]{1,0:T(8,128)S(1)} collective-permute-done((f32[136,256]{1,0:T(8,128)S(1)}, f32[136,256]{1,0:T(8,128)S(1)}, u32[]{:S(2)}, u32[]{:S(2)}) %collective-permute-start.10) | collective-permute-done | bytes 139296 | tf_op jit(solution)/shard_map/ppermute | solution.py:469
  23.2 1.1 %sums.1 = (f32[2,16,1024]{2,1,0:T(8,128)}, f32[2,32,1024]{2,1,0:T(8,128)}) custom-call(f32[2,4,16,256]{3,2,1,0:T(8,128)S(1)} %get-tuple-element.33.refs_0_, f32[136,256]{1,0:T(8,128)S(1)} %collective-permute-done.10.refs_1_, bf16[512,512]{1,0:T(8,128)(2,1)S(1)} %get-tuple-element.40.refs_2_, f32[2,4,32,256]{3,2,1,0:T(8,128)S(1)} %late_resident_terms.1.refs_3_), custom_call_target="tpu_custom_call" | custom-call | flops 500000000 | bytes 1024 | tf_op jit(solution)/shard_map/sums/pallas_call | solution.py:487
  (7 shorter events, 0.0 us)
Async XLA Ops:
  0.6 8.3 %copy-start.1 = (bf16[2,32,1024]{2,1,0:T(8,128)(2,1)S(1)}, bf16[2,32,1024]{2,1,0:T(8,128)(2,1)}, u32[]{:S(2)}) copy-start(bf16[2,32,1024]{2,1,0:T(8,128)(2,1)} %travellers.1) | copy-start | bytes 393220
  0.6 9.9 %copy-start.2 = (f32[72,256]{1,0:T(8,128)S(1)}, f32[72,256]{1,0:T(8,128)}, u32[]{:S(2)}) copy-start(f32[72,256]{1,0:T(8,128)} %constant.2.clone.small) | copy-start | bytes 221188
  2.5 9.6 %copy-start = (bf16[544,128]{1,0:T(8,128)(2,1)S(1)}, bf16[544,128]{1,0:T(8,128)(2,1)}, u32[]{:S(2)}) copy-start(bf16[544,128]{1,0:T(8,128)(2,1)} %pack.1.refs_1_.refs_2_.refs_3_.refs_4_) | copy-start | bytes 417796
  2.5 9.6 %collective-permute-start.1 = (bf16[544,128]{1,0:T(8,128)(2,1)}, bf16[544,128]{1,0:T(8,128)(2,1)S(1)}, u32[]{:S(2)}, u32[]{:S(2)}) collective-permute-start(bf16[544,128]{1,0:T(8,128)(2,1)} %pack.1.refs_1_.refs_2_.refs_3_.refs_4_), channel_id=1, source_target_pairs={{0,24},{2,26},{4,28},{6,30},{8,0},{10,2},{12,4},{14,6},{16,8},{18,... | collective-permute-start | bytes 417800 | tf_op jit(solution)/shard_map/ppermute | solution.py:353
  7.6 7.5 %collective-permute-start = (bf16[544,128]{1,0:T(8,128)(2,1)}, bf16[544,128]{1,0:T(8,128)(2,1)S(1)}, u32[]{:S(2)}, u32[]{:S(2)}) collective-permute-start(bf16[544,128]{1,0:T(8,128)(2,1)} %pack.1.refs_1_.refs_2_.refs_3_.refs_4_), channel_id=1, source_target_pairs={{0,28},{2,30},{4,0},{6,2},{8,4},{10,6},{12,8},{14,10},{16,12},{18,... | collective-permute-start | bytes 417800 | tf_op jit(solution)/shard_map/ppermute | solution.py:353
  9.0 10.0 %collective-permute-start.5 = (bf16[2,32,1024]{2,1,0:T(8,128)(2,1)S(1)}, bf16[2,32,1024]{2,1,0:T(8,128)(2,1)S(1)}, u32[]{:S(2)}, u32[]{:S(2)}) collective-permute-start(bf16[2,32,1024]{2,1,0:T(8,128)(2,1)S(1)} %copy-done.1), channel_id=1, source_target_pairs={{0,4},{2,6},{4,8},{6,10},{8,12},{10,14},{12,16},{14,18},{16,20},{1... | collective-permute-start | bytes 393224 | tf_op jit(solution)/shard_map/ppermute | solution.py:353
  9.6 9.3 %collective-permute-start.6 = (bf16[2,32,1024]{2,1,0:T(8,128)(2,1)S(1)}, bf16[2,32,1024]{2,1,0:T(8,128)(2,1)S(1)}, u32[]{:S(2)}, u32[]{:S(2)}) collective-permute-start(bf16[2,32,1024]{2,1,0:T(8,128)(2,1)S(1)} %copy-done.1), channel_id=1, source_target_pairs={{0,8},{2,10},{4,12},{6,14},{8,16},{10,18},{12,20},{14,22},{16,24},... | collective-permute-start | bytes 393224 | tf_op jit(solution)/shard_map/ppermute | solution.py:353
  12.1 1.4 %collective-permute-start.3 = (bf16[544,128]{1,0:T(8,128)(2,1)S(1)}, bf16[544,128]{1,0:T(8,128)(2,1)S(1)}, u32[]{:S(2)}, u32[]{:S(2)}) collective-permute-start(bf16[544,128]{1,0:T(8,128)(2,1)S(1)} %collective-permute-done.1.refs_0_), channel_id=1, source_target_pairs={{0,2},{2,0},{4,6},{6,4},{8,10},{10,8},{12,14},{14,12},{16,18},{18,... | collective-permute-start | bytes 417800 | tf_op jit(solution)/shard_map/ppermute | solution.py:358
  12.1 1.6 %collective-permute-start.2 = (bf16[544,128]{1,0:T(8,128)(2,1)S(1)}, bf16[544,128]{1,0:T(8,128)(2,1)S(1)}, u32[]{:S(2)}, u32[]{:S(2)}) collective-permute-start(bf16[544,128]{1,0:T(8,128)(2,1)S(1)} %copy-done), channel_id=1, source_target_pairs={{0,2},{2,0},{4,6},{6,4},{8,10},{10,8},{12,14},{14,12},{16,18},{18,... | collective-permute-start | bytes 417800 | tf_op jit(solution)/shard_map/ppermute | solution.py:358
  13.5 7.5 %collective-permute-start.8 = (bf16[2,32,1024]{2,1,0:T(8,128)(2,1)S(1)}, bf16[2,32,1024]{2,1,0:T(8,128)(2,1)S(1)}, u32[]{:S(2)}, u32[]{:S(2)}) collective-permute-start(bf16[2,32,1024]{2,1,0:T(8,128)(2,1)S(1)} %copy-done.1), channel_id=1, source_target_pairs={{0,2},{2,0},{4,6},{6,4},{8,10},{10,8},{12,14},{14,12},{16,18},{18,... | collective-permute-start | bytes 393224 | tf_op jit(solution)/shard_map/ppermute | solution.py:358
  15.1 1.4 %collective-permute-start.4 = (bf16[544,128]{1,0:T(8,128)(2,1)S(1)}, bf16[544,128]{1,0:T(8,128)(2,1)S(1)}, u32[]{:S(2)}, u32[]{:S(2)}) collective-permute-start(bf16[544,128]{1,0:T(8,128)(2,1)S(1)} %collective-permute-done.refs_0_._), channel_id=1, source_target_pairs={{0,2},{2,0},{4,6},{6,4},{8,10},{10,8},{12,14},{14,12},{16,18},{18,... | collective-permute-start | bytes 417800 | tf_op jit(solution)/shard_map/ppermute | solution.py:358
  17.4 5.8 %collective-permute-start.10 = (f32[136,256]{1,0:T(8,128)S(1)}, f32[136,256]{1,0:T(8,128)S(1)}, u32[]{:S(2)}, u32[]{:S(2)}) collective-permute-start(f32[136,256]{1,0:T(8,128)S(1)} %bitcast.2), channel_id=1, source_target_pairs={{0,1},{1,0},{2,3},{3,2},{4,5},{5,4},{6,7},{7,6},{8,9},{9,8},{10,11... | collective-permute-start | bytes 417800 | tf_op jit(solution)/shard_map/ppermute | solution.py:469
  19.0 2.1 %collective-permute-start.7 = (bf16[2,32,1024]{2,1,0:T(8,128)(2,1)S(1)}, bf16[2,32,1024]{2,1,0:T(8,128)(2,1)S(1)}, u32[]{:S(2)}, u32[]{:S(2)}) collective-permute-start(bf16[2,32,1024]{2,1,0:T(8,128)(2,1)S(1)} %collective-permute-done.5.refs_0_), channel_id=1, source_target_pairs={{0,2},{2,0},{4,6},{6,4},{8,10},{10,8},{12,14},{14,12},{16,18},{18,... | collective-permute-start | bytes 393224 | tf_op jit(solution)/shard_map/ppermute | solution.py:358
  19.0 2.0 %collective-permute-start.9 = (bf16[2,32,1024]{2,1,0:T(8,128)(2,1)S(1)}, bf16[2,32,1024]{2,1,0:T(8,128)(2,1)S(1)}, u32[]{:S(2)}, u32[]{:S(2)}) collective-permute-start(bf16[2,32,1024]{2,1,0:T(8,128)(2,1)S(1)} %collective-permute-done.6.refs_1_), channel_id=1, source_target_pairs={{0,2},{2,0},{4,6},{6,4},{8,10},{10,8},{12,14},{14,12},{16,18},{18,... | collective-permute-start | bytes 393224 | tf_op jit(solution)/shard_map/ppermute | solution.py:358

commit v7 on v6

--- a/solution.py
+++ b/solution.py
@@ -273,9 +273,10 @@
     return found
 
 
-def terms_kernel(plan, accumulate, cut, slots, edge, for_travellers, after, *refs):
+def terms_kernel(plan, accumulate, cut, plain, slots, edge, for_travellers, after, *refs):
     outputs = 2 if cut else 1
-    refs, outs = refs[: len(refs) - outputs - after], refs[-outputs:]
+    refs, outs = refs[:-outputs], refs[-outputs:]
+    refs, others = refs[: len(refs) - after], refs[len(refs) - after :]
     blocks = sum(number for number, _ in plan)
     moving, (own, home, *refs) = refs[:blocks], refs[blocks:]
     tables, folding, before = refs[:3], refs[3], refs[4:]
@@ -298,6 +299,10 @@
     group = 2 * slots
     for start in range(0, len(found), group):
         gather_terms(found[start : start + group], home, total, tables)
+    if plain:
+        for j, field in enumerate(unfold(total, others[0][...])):
+            outs[0][j] = field
+        return
     if not cut:
         for j, field in enumerate(total):
             for q in range(4):
@@ -324,10 +329,9 @@
 
 
 def sum_kernel(number, *refs):
-    parts, (table, terms, trav_total, res_total) = refs[:number], refs[number:]
-    fields = [[terms[j, q] for q in range(4)] for j in range(terms.shape[0])]
-    for j, field in enumerate(unfold(fields, table[...])):
-        res_total[j] = field
+    parts, (table, terms, trav_out, res_out, trav_total, sems) = refs[:number], refs[number:]
+    copies = [pltpu.make_async_copy(terms, res_out, sems.at[0])]
+    copies[0].start()
     total = []
     size = parts[0].shape[2]
     for j in range(parts[0].shape[0]):
@@ -335,6 +339,10 @@
         total.append([sum((part[k : k + size, :] for part in parts[1:]), parts[0][j, q]) for q, k in enumerate(starts)])
     for j, field in enumerate(unfold(total, table[...])):
         trav_total[j] = field
+    copies.append(pltpu.make_async_copy(trav_total, trav_out, sems.at[1]))
+    copies[-1].start()
+    for copy in copies:
+        copy.wait()
 
 
 VMEM = pl.BlockSpec(memory_space=pltpu.VMEM)
@@ -402,19 +410,21 @@
         name="tables",
     )(small, travellers)
 
-    def stage(plan, blocks, home, total, for_travellers, microseconds, name, cut=False, after=()):
+    def stage(plan, blocks, home, total, for_travellers, microseconds, name, cut=False, plain=False, after=()):
         number = home[1].shape[0] // (8 * edge)
         if cut:
             out_shape = (
                 jax.ShapeDtypeStruct((number, 4, part, plane // 4), jnp.float32),
                 jax.ShapeDtypeStruct((groups - 1, number * 4 * part + SPARE_ROWS, plane // 4), jnp.float32),
             )
+        elif plain:
+            out_shape = jax.ShapeDtypeStruct((number, edge, plane), jnp.float32)
         else:
             out_shape = jax.ShapeDtypeStruct((number, 4, edge, plane // 4), jnp.float32)
         operands = (*blocks, *home, *tables, folding) + (() if total is None else (total,))
         return pl.pallas_call(
             functools.partial(
-                terms_kernel, plan, total is not None, cut, slots, edge, for_travellers, len(after)
+                terms_kernel, plan, total is not None, cut, plain, slots, edge, for_travellers, len(after)
             ),
             out_shape=out_shape,
             in_specs=[VMEM] * (len(operands) + len(after)),
@@ -481,7 +491,7 @@
         after=(summed,),
     )
     blocks = [*trav_swapped[1:-1], trav_swapped[0], trav_swapped[-1]]
-    res_total = stage(middle + ends, blocks, home, total, False, 0.001, "late_resident_terms")
+    res_total = stage(middle + ends, blocks, home, total, False, 0.001, "late_resident_terms", plain=True, after=(unfolding,))
     res_total, sent = lax.optimization_barrier((res_total, sent))
     parts = [mine, *sent]
     trav_total, res_total = pl.pallas_call(
@@ -491,7 +501,11 @@
             jax.ShapeDtypeStruct(residents.shape, jnp.float32),
         ),
         in_specs=[VMEM] * (len(parts) + 2),
-        out_specs=(VMEM, VMEM),
+        out_specs=(HBM, HBM),
+        scratch_shapes=[
+            pltpu.VMEM((held, part, plane), jnp.float32),
+            pltpu.SemaphoreType.DMA((2,)),
+        ],
         compiler_params=LIMIT,
         cost_estimate=cost(0.5),
         name="sums",

time: 24.5 us -> 24.3 us (level)
  waiting for transfers between devices: 2.59 us -> 2.32 us
    pallas_call x6, Pallas kernels: 6.66 us -> 6.92 us  [stage(): pl.pallas_call(functools.partial(terms_kernel, plan, total is not None, c...]
    ppermute x1, waiting for transfers between devices: 0.57 us -> 0.32 us  [local(): lax.ppermute(others[k - 1], 'grp', [(g, (g + k) % groups) for g in range(...]
  transfers between devices with their start and end apart: 11 -> 11, of which waited for: 5 -> 4; matrix products, arithmetic and copies ran while one was open for 0% -> 0% of each run, Pallas kernels for 29% -> 31%
where the time goes in v7:
time: 24.3 us; the launch traced here: 24.1 us
  starting transfers between devices  10.8 us (44%)
  Pallas kernels  10.2 us (42%)
  waiting for transfers between devices  2.32 us (10%)
  between operations  0.77 us (3%)
    ppermute x4, starting transfers between devices, from_behind(): lax.ppermute(value, 'blk', [(i, (i + by) % peers) for i in range(peers)])  8.06 us
    pallas_call x6, Pallas kernels, stage(): pl.pallas_call(functools.partial(terms_kernel, plan, total is not None, c...  6.92 us
    pallas_call x1, Pallas kernels, local(): pl.pallas_call(functools.partial(pack_kernel, ('blk', 'grp')), out_shape=...  1.82 us
    ppermute x1, starting transfers between devices, local(): lax.ppermute(others[k - 1], 'grp', [(g, (g + k) % groups) for g in range(...  1.58 us
    ppermute x4, waiting for transfers between devices, from_behind(): lax.ppermute(value, 'blk', [(i, (i + by) % peers) for i in range(peers)])  1.54 us
    ppermute x6, starting transfers between devices, other_core(): return lax.ppermute(value, 'blk', [(i, i ^ 1) for i in range(peers)])  1.19 us
    pallas_call x1, Pallas kernels, local(): pl.pallas_call(functools.partial(sum_kernel, len(parts)), out_shape=(jax....  0.98 us
  transfers between devices with their start and end apart: 11, of which 4 were waited for; matrix products, arithmetic and copies ran while one was open for 0% of the time, Pallas kernels for 31%

profile of v7, /device:TPU:0, one launch (start us, length us, event | category | flops | bytes accessed | tf_op | source)
XLA Modules:
  0.0 24.1 jit_solution(12321964676813759342)
XLA Ops:
  0.6 0.0 copy-start.2
  0.7 1.8 %pack.1.refs_1_.refs_2_.refs_3_.refs_4_ = bf16[544,128]{1,0:T(8,128)(2,1)} custom-call(bf16[2,32,1024]{2,1,0:T(8,128)(2,1)} %residents.1, s32[1,3,2,4]{3,2,1,0:T(2,128)} %bitcast.3), custom_call_target="tpu_custom_call" | custom-call | flops 1000000000 | bytes 1024 | tf_op jit(solution)/shard_map/pack/pallas_call | solution.py:381
  2.5 0.0 copy-start
  2.5 5.1 %collective-permute-start.1 = (bf16[544,128]{1,0:T(8,128)(2,1)}, bf16[544,128]{1,0:T(8,128)(2,1)S(1)}, u32[]{:S(2)}, u32[]{:S(2)}) collective-permute-start(bf16[544,128]{1,0:T(8,128)(2,1)} %pack.1.refs_1_.refs_2_.refs_3_.refs_4_), channel_id=1, source_target_pairs={{0,24},{2,26},{4,28},{6,30},{8,0},{10,2},{12,4},{14,6},{16,8},{18,... | collective-permute-start | bytes 417800 | tf_op jit(solution)/shard_map/ppermute | solution.py:361
  7.6 1.4 %collective-permute-start = (bf16[544,128]{1,0:T(8,128)(2,1)}, bf16[544,128]{1,0:T(8,128)(2,1)S(1)}, u32[]{:S(2)}, u32[]{:S(2)}) collective-permute-start(bf16[544,128]{1,0:T(8,128)(2,1)} %pack.1.refs_1_.refs_2_.refs_3_.refs_4_), channel_id=1, source_target_pairs={{0,28},{2,30},{4,0},{6,2},{8,4},{10,6},{12,8},{14,10},{16,12},{18,... | collective-permute-start | bytes 417800 | tf_op jit(solution)/shard_map/ppermute | solution.py:361
  9.0 0.6 %collective-permute-start.5 = (bf16[2,32,1024]{2,1,0:T(8,128)(2,1)S(1)}, bf16[2,32,1024]{2,1,0:T(8,128)(2,1)S(1)}, u32[]{:S(2)}, u32[]{:S(2)}) collective-permute-start(bf16[2,32,1024]{2,1,0:T(8,128)(2,1)S(1)} %copy-done.1), channel_id=1, source_target_pairs={{0,4},{2,6},{4,8},{6,10},{8,12},{10,14},{12,16},{14,18},{16,20},{1... | collective-permute-start | bytes 393224 | tf_op jit(solution)/shard_map/ppermute | solution.py:361
  9.6 0.9 %collective-permute-start.6 = (bf16[2,32,1024]{2,1,0:T(8,128)(2,1)S(1)}, bf16[2,32,1024]{2,1,0:T(8,128)(2,1)S(1)}, u32[]{:S(2)}, u32[]{:S(2)}) collective-permute-start(bf16[2,32,1024]{2,1,0:T(8,128)(2,1)S(1)} %copy-done.1), channel_id=1, source_target_pairs={{0,8},{2,10},{4,12},{6,14},{8,16},{10,18},{12,20},{14,22},{16,24},... | collective-permute-start | bytes 393224 | tf_op jit(solution)/shard_map/ppermute | solution.py:361
  10.6 0.5 %tables.1 = (bf16[512,256]{1,0:T(8,128)(2,1)S(1)}, bf16[256,128]{1,0:T(8,128)(2,1)S(1)}, f32[32,1024]{1,0:T(8,128)S(1)}, bf16[512,512]{1,0:T(8,128)(2,1)S(1)}, b...) custom-call(f32[72,256]{1,0:T(8,128)S(1)} %copy-done.2, bf16[2,32,1024]{2,1,0:T(8,128)(2,1)S(1)} %copy-done.1), custom_call_target="tpu_custom_call" | custom-call | flops 20000000000 | bytes 1024 | tf_op jit(solution)/shard_map/tables/pallas_call | solution.py:396
  11.0 1.0 %collective-permute-done.1.refs_0_ = bf16[544,128]{1,0:T(8,128)(2,1)S(1)} collective-permute-done((bf16[544,128]{1,0:T(8,128)(2,1)}, bf16[544,128]{1,0:T(8,128)(2,1)S(1)}, u32[]{:S(2)}, u32[]{:S(2)}) %collective-permute-start.1) | collective-permute-done | bytes 139296 | tf_op jit(solution)/shard_map/ppermute | solution.py:361
  12.1 0.0 collective-permute-start.3
  12.1 0.5 %collective-permute-start.2 = (bf16[544,128]{1,0:T(8,128)(2,1)S(1)}, bf16[544,128]{1,0:T(8,128)(2,1)S(1)}, u32[]{:S(2)}, u32[]{:S(2)}) collective-permute-start(bf16[544,128]{1,0:T(8,128)(2,1)S(1)} %copy-done), channel_id=1, source_target_pairs={{0,2},{2,0},{4,6},{6,4},{8,10},{10,8},{12,14},{14,12},{16,18},{18,... | collective-permute-start | bytes 417800 | tf_op jit(solution)/shard_map/ppermute | solution.py:366
  12.6 0.9 %first_traveller_terms.1.refs_8_ = f32[2,4,32,256]{3,2,1,0:T(8,128)S(1)} custom-call(bf16[544,128]{1,0:T(8,128)(2,1)S(1)} %collective-permute-done.1.refs_0_, bf16[544,128]{1,0:T(8,128)(2,1)S(1)} %copy-done, bf16[512,128]{1,0:T(8,128)(2,1)S(1)} %get-tuple-element.26.refs_2_.refs_3_, bf16[512,256]{1,0:T(8,128)(2,1)S(1)} %get-tuple-element.27.refs_3_.refs_4_.refs_5_, ...), custom_call_target="tpu_custom_call" | custom-call | flops 10000000000 | bytes 1024 | tf_op jit(solution)/shard_map/first_traveller_terms/pallas_call | solution.py:425
  13.5 0.0 collective-permute-done.3.refs_1_
  13.5 0.1 collective-permute-start.8
  13.6 0.0 collective-permute-done.2.refs_0_
  13.6 0.9 %early_traveller_terms.1.refs_7_ = f32[2,4,32,256]{3,2,1,0:T(8,128)S(1)} custom-call(bf16[544,128]{1,0:T(8,128)(2,1)S(1)} %collective-permute-done.2.refs_0_, bf16[544,128]{1,0:T(8,128)(2,1)S(1)} %collective-permute-done.3.refs_1_, bf16[544,128]{1,0:T(8,128)(2,1)S(1)} %copy-done, bf16[512,128]{1,0:T(8,128)(2,1)S(1)} %get-tuple-element.26.refs_2_.refs_3_, ...), custom_call_target="tpu_custom_call" | custom-call | flops 10000000000 | bytes 1024 | tf_op jit(solution)/shard_map/early_traveller_terms/pallas_call | solution.py:425
  14.6 0.5 %collective-permute-done.refs_0_._ = bf16[544,128]{1,0:T(8,128)(2,1)S(1)} collective-permute-done((bf16[544,128]{1,0:T(8,128)(2,1)}, bf16[544,128]{1,0:T(8,128)(2,1)S(1)}, u32[]{:S(2)}, u32[]{:S(2)}) %collective-permute-start) | collective-permute-done | bytes 139296 | tf_op jit(solution)/shard_map/ppermute | solution.py:361
  15.1 0.0 collective-permute-start.4
  15.1 0.9 %middle_traveller_terms.1.refs_7_ = f32[2,4,32,256]{3,2,1,0:T(8,128)S(1)} custom-call(bf16[544,128]{1,0:T(8,128)(2,1)S(1)} %collective-permute-done.refs_0_._, bf16[544,128]{1,0:T(8,128)(2,1)S(1)} %copy-done, bf16[512,128]{1,0:T(8,128)(2,1)S(1)} %get-tuple-element.26.refs_2_.refs_3_, bf16[512,256]{1,0:T(8,128)(2,1)S(1)} %get-tuple-element.27.refs_3_.refs_4_.refs_5_, ...), custom_call_target="tpu_custom_call" | custom-call | flops 1000000000 | bytes 1024 | tf_op jit(solution)/shard_map/middle_traveller_terms/pallas_call | solution.py:425
  16.0 0.4 %collective-permute-done.4.refs_0_ = bf16[544,128]{1,0:T(8,128)(2,1)S(1)} collective-permute-done((bf16[544,128]{1,0:T(8,128)(2,1)S(1)}, bf16[544,128]{1,0:T(8,128)(2,1)S(1)}, u32[]{:S(2)}, u32[]{:S(2)}) %collective-permute-start.4) | collective-permute-done | bytes 139296 | tf_op jit(solution)/shard_map/ppermute | solution.py:366
  16.4 0.9 %late_traveller_terms.1 = (f32[2,4,16,256]{3,2,1,0:T(8,128)S(1)}, f32[1,136,256]{2,1,0:T(8,128)S(1)}) custom-call(bf16[544,128]{1,0:T(8,128)(2,1)S(1)} %collective-permute-done.4.refs_0_, bf16[544,128]{1,0:T(8,128)(2,1)S(1)} %copy-done, bf16[512,128]{1,0:T(8,128)(2,1)S(1)} %get-tuple-element.26.refs_2_.refs_3_, ...), custom_call_target="tpu_custom_call" | custom-call | flops 2000000000 | bytes 1024 | tf_op jit(solution)/shard_map/late_traveller_terms/pallas_call | solution.py:425
  17.4 1.6 %collective-permute-start.10 = (f32[136,256]{1,0:T(8,128)S(1)}, f32[136,256]{1,0:T(8,128)S(1)}, u32[]{:S(2)}, u32[]{:S(2)}) collective-permute-start(f32[136,256]{1,0:T(8,128)S(1)} %bitcast.2), channel_id=1, source_target_pairs={{0,1},{1,0},{2,3},{3,2},{4,5},{5,4},{6,7},{7,6},{8,9},{9,8},{10,11... | collective-permute-start | bytes 417800 | tf_op jit(solution)/shard_map/ppermute | solution.py:479
  19.0 0.0 collective-permute-done.5.refs_0_
  19.0 0.0 collective-permute-done.6.refs_1_
  19.0 0.1 collective-permute-start.7
  19.0 0.5 %collective-permute-start.9 = (bf16[2,32,1024]{2,1,0:T(8,128)(2,1)S(1)}, bf16[2,32,1024]{2,1,0:T(8,128)(2,1)S(1)}, u32[]{:S(2)}, u32[]{:S(2)}) collective-permute-start(bf16[2,32,1024]{2,1,0:T(8,128)(2,1)S(1)} %collective-permute-done.6.refs_1_), channel_id=1, source_target_pairs={{0,2},{2,0},{4,6},{6,4},{8,10},{10,8},{12,14},{14,12},{16,18},{18,... | collective-permute-start | bytes 393224 | tf_op jit(solution)/shard_map/ppermute | solution.py:366
  19.5 1.5 %early_resident_terms.1.refs_9_ = f32[2,4,32,256]{3,2,1,0:T(8,128)S(1)} custom-call(bf16[2,32,1024]{2,1,0:T(8,128)(2,1)S(1)} %collective-permute-done.5.refs_0_, bf16[2,32,1024]{2,1,0:T(8,128)(2,1)S(1)} %collective-permute-done.6.refs_1_, bf16[544,128]{1,0:T(8,128)(2,1)S(1)} %copy-done, bf16[544,128]{1,0:T(8,128)(2,1)S(1)} %copy-done, ...), custom_call_target="tpu_custom_call" | custom-call | flops 1000000 | bytes 1024 | tf_op jit(solution)/shard_map/early_resident_terms/pallas_call | solution.py:425
  21.1 0.0 collective-permute-done.8.refs_1_
  21.1 0.0 collective-permute-done.9.refs_2_
  21.1 1.8 %late_resident_terms.1.refs_3_ = f32[2,32,1024]{2,1,0:T(8,128)S(1)} custom-call(bf16[2,32,1024]{2,1,0:T(8,128)(2,1)S(1)} %collective-permute-done.7.refs_0_, bf16[2,32,1024]{2,1,0:T(8,128)(2,1)S(1)} %collective-permute-done.8.refs_1_, bf16[2,32,1024]{2,1,0:T(8,128)(2,1)S(1)} %collective-permute-done.9.refs_2_, bf16[544,128]{1,0:T(8,128)(2,1)S(1)} %copy-done, ...), custom_call_target="tpu_custom_call" | custom-call | flops 1000000 | bytes 1024 | tf_op jit(solution)/shard_map/late_resident_terms/pallas_call | solution.py:425
  22.8 0.3 %collective-permute-done.10.refs_1_ = f32[136,256]{1,0:T(8,128)S(1)} collective-permute-done((f32[136,256]{1,0:T(8,128)S(1)}, f32[136,256]{1,0:T(8,128)S(1)}, u32[]{:S(2)}, u32[]{:S(2)}) %collective-permute-start.10) | collective-permute-done | bytes 139296 | tf_op jit(solution)/shard_map/ppermute | solution.py:479
  23.2 1.0 %sums.1 = (f32[2,16,1024]{2,1,0:T(8,128)}, f32[2,32,1024]{2,1,0:T(8,128)}) custom-call(f32[2,4,16,256]{3,2,1,0:T(8,128)S(1)} %get-tuple-element.33.refs_0_, f32[136,256]{1,0:T(8,128)S(1)} %collective-permute-done.10.refs_1_, bf16[512,512]{1,0:T(8,128)(2,1)S(1)} %get-tuple-element.39.refs_10_.refs_2_, f32[2,32,1024]{2,1,0:T(8,128)S(1)} %late_resident_terms.1.refs_3_), custom_call_target="tpu_custom_call" | custom-call | flops 500000000 | bytes 1024 | tf_op jit(solution)/shard_map/sums/pallas_call | solution.py:497
  (7 shorter events, 0.0 us)
Async XLA Ops:
  0.6 8.3 %copy-start.1 = (bf16[2,32,1024]{2,1,0:T(8,128)(2,1)S(1)}, bf16[2,32,1024]{2,1,0:T(8,128)(2,1)}, u32[]{:S(2)}) copy-start(bf16[2,32,1024]{2,1,0:T(8,128)(2,1)} %travellers.1) | copy-start | bytes 393220
  0.6 9.9 %copy-start.2 = (f32[72,256]{1,0:T(8,128)S(1)}, f32[72,256]{1,0:T(8,128)}, u32[]{:S(2)}) copy-start(f32[72,256]{1,0:T(8,128)} %constant.2.clone.small) | copy-start | bytes 221188
  2.5 9.6 %copy-start = (bf16[544,128]{1,0:T(8,128)(2,1)S(1)}, bf16[544,128]{1,0:T(8,128)(2,1)}, u32[]{:S(2)}) copy-start(bf16[544,128]{1,0:T(8,128)(2,1)} %pack.1.refs_1_.refs_2_.refs_3_.refs_4_) | copy-start | bytes 417796
  2.5 9.6 %collective-permute-start.1 = (bf16[544,128]{1,0:T(8,128)(2,1)}, bf16[544,128]{1,0:T(8,128)(2,1)S(1)}, u32[]{:S(2)}, u32[]{:S(2)}) collective-permute-start(bf16[544,128]{1,0:T(8,128)(2,1)} %pack.1.refs_1_.refs_2_.refs_3_.refs_4_), channel_id=1, source_target_pairs={{0,24},{2,26},{4,28},{6,30},{8,0},{10,2},{12,4},{14,6},{16,8},{18,... | collective-permute-start | bytes 417800 | tf_op jit(solution)/shard_map/ppermute | solution.py:361
  7.6 7.5 %collective-permute-start = (bf16[544,128]{1,0:T(8,128)(2,1)}, bf16[544,128]{1,0:T(8,128)(2,1)S(1)}, u32[]{:S(2)}, u32[]{:S(2)}) collective-permute-start(bf16[544,128]{1,0:T(8,128)(2,1)} %pack.1.refs_1_.refs_2_.refs_3_.refs_4_), channel_id=1, source_target_pairs={{0,28},{2,30},{4,0},{6,2},{8,4},{10,6},{12,8},{14,10},{16,12},{18,... | collective-permute-start | bytes 417800 | tf_op jit(solution)/shard_map/ppermute | solution.py:361
  9.0 10.0 %collective-permute-start.5 = (bf16[2,32,1024]{2,1,0:T(8,128)(2,1)S(1)}, bf16[2,32,1024]{2,1,0:T(8,128)(2,1)S(1)}, u32[]{:S(2)}, u32[]{:S(2)}) collective-permute-start(bf16[2,32,1024]{2,1,0:T(8,128)(2,1)S(1)} %copy-done.1), channel_id=1, source_target_pairs={{0,4},{2,6},{4,8},{6,10},{8,12},{10,14},{12,16},{14,18},{16,20},{1... | collective-permute-start | bytes 393224 | tf_op jit(solution)/shard_map/ppermute | solution.py:361
  9.6 9.3 %collective-permute-start.6 = (bf16[2,32,1024]{2,1,0:T(8,128)(2,1)S(1)}, bf16[2,32,1024]{2,1,0:T(8,128)(2,1)S(1)}, u32[]{:S(2)}, u32[]{:S(2)}) collective-permute-start(bf16[2,32,1024]{2,1,0:T(8,128)(2,1)S(1)} %copy-done.1), channel_id=1, source_target_pairs={{0,8},{2,10},{4,12},{6,14},{8,16},{10,18},{12,20},{14,22},{16,24},... | collective-permute-start | bytes 393224 | tf_op jit(solution)/shard_map/ppermute | solution.py:361
  12.1 1.4 %collective-permute-start.3 = (bf16[544,128]{1,0:T(8,128)(2,1)S(1)}, bf16[544,128]{1,0:T(8,128)(2,1)S(1)}, u32[]{:S(2)}, u32[]{:S(2)}) collective-permute-start(bf16[544,128]{1,0:T(8,128)(2,1)S(1)} %collective-permute-done.1.refs_0_), channel_id=1, source_target_pairs={{0,2},{2,0},{4,6},{6,4},{8,10},{10,8},{12,14},{14,12},{16,18},{18,... | collective-permute-start | bytes 417800 | tf_op jit(solution)/shard_map/ppermute | solution.py:366
  12.1 1.6 %collective-permute-start.2 = (bf16[544,128]{1,0:T(8,128)(2,1)S(1)}, bf16[544,128]{1,0:T(8,128)(2,1)S(1)}, u32[]{:S(2)}, u32[]{:S(2)}) collective-permute-start(bf16[544,128]{1,0:T(8,128)(2,1)S(1)} %copy-done), channel_id=1, source_target_pairs={{0,2},{2,0},{4,6},{6,4},{8,10},{10,8},{12,14},{14,12},{16,18},{18,... | collective-permute-start | bytes 417800 | tf_op jit(solution)/shard_map/ppermute | solution.py:366
  13.5 7.5 %collective-permute-start.8 = (bf16[2,32,1024]{2,1,0:T(8,128)(2,1)S(1)}, bf16[2,32,1024]{2,1,0:T(8,128)(2,1)S(1)}, u32[]{:S(2)}, u32[]{:S(2)}) collective-permute-start(bf16[2,32,1024]{2,1,0:T(8,128)(2,1)S(1)} %copy-done.1), channel_id=1, source_target_pairs={{0,2},{2,0},{4,6},{6,4},{8,10},{10,8},{12,14},{14,12},{16,18},{18,... | collective-permute-start | bytes 393224 | tf_op jit(solution)/shard_map/ppermute | solution.py:366
  15.1 1.4 %collective-permute-start.4 = (bf16[544,128]{1,0:T(8,128)(2,1)S(1)}, bf16[544,128]{1,0:T(8,128)(2,1)S(1)}, u32[]{:S(2)}, u32[]{:S(2)}) collective-permute-start(bf16[544,128]{1,0:T(8,128)(2,1)S(1)} %collective-permute-done.refs_0_._), channel_id=1, source_target_pairs={{0,2},{2,0},{4,6},{6,4},{8,10},{10,8},{12,14},{14,12},{16,18},{18,... | collective-permute-start | bytes 417800 | tf_op jit(solution)/shard_map/ppermute | solution.py:366
  17.4 5.8 %collective-permute-start.10 = (f32[136,256]{1,0:T(8,128)S(1)}, f32[136,256]{1,0:T(8,128)S(1)}, u32[]{:S(2)}, u32[]{:S(2)}) collective-permute-start(f32[136,256]{1,0:T(8,128)S(1)} %bitcast.2), channel_id=1, source_target_pairs={{0,1},{1,0},{2,3},{3,2},{4,5},{5,4},{6,7},{7,6},{8,9},{9,8},{10,11... | collective-permute-start | bytes 417800 | tf_op jit(solution)/shard_map/ppermute | solution.py:479
  19.0 2.1 %collective-permute-start.7 = (bf16[2,32,1024]{2,1,0:T(8,128)(2,1)S(1)}, bf16[2,32,1024]{2,1,0:T(8,128)(2,1)S(1)}, u32[]{:S(2)}, u32[]{:S(2)}) collective-permute-start(bf16[2,32,1024]{2,1,0:T(8,128)(2,1)S(1)} %collective-permute-done.5.refs_0_), channel_id=1, source_target_pairs={{0,2},{2,0},{4,6},{6,4},{8,10},{10,8},{12,14},{14,12},{16,18},{18,... | collective-permute-start | bytes 393224 | tf_op jit(solution)/shard_map/ppermute | solution.py:366
  19.0 2.0 %collective-permute-start.9 = (bf16[2,32,1024]{2,1,0:T(8,128)(2,1)S(1)}, bf16[2,32,1024]{2,1,0:T(8,128)(2,1)S(1)}, u32[]{:S(2)}, u32[]{:S(2)}) collective-permute-start(bf16[2,32,1024]{2,1,0:T(8,128)(2,1)S(1)} %collective-permute-done.6.refs_1_), channel_id=1, source_target_pairs={{0,2},{2,0},{4,6},{6,4},{8,10},{10,8},{12,14},{14,12},{16,18},{18,... | collective-permute-start | bytes 393224 | tf_op jit(solution)/shard_map/ppermute | solution.py:366

commit v8 on v7

--- a/solution.py
+++ b/solution.py
@@ -142,9 +142,15 @@
     for load in loads:
         load.wait()
     store_folded(fields, table, folded)
-    store = pltpu.make_async_copy(folded, packed, sems.at[0])
-    store.start()
-    store.wait()
+    cut = 4 * count * edge
+    stores = [
+        pltpu.make_async_copy(folded.at[:cut], packed.at[:cut], sems.at[0]),
+        pltpu.make_async_copy(folded.at[cut:], packed.at[cut:], sems.at[1]),
+    ]
+    for store in stores:
+        store.start()
+    for store in stores:
+        store.wait()
 
 
 def tables_kernel(count, small, travellers, plane_table, along, inverse, folding, unfolding, moving):
@@ -309,8 +315,8 @@
                 outs[0][j, q] = field[q]
         return
     mine, others = outs
-    others[...] = jnp.zeros_like(others)
     rows = mine.shape[2]
+    others[:, 4 * held * rows :, :] = jnp.zeros((others.shape[0], SPARE_ROWS, others.shape[2]), jnp.float32)
     parts = edge // rows
     for k in range(parts):
         group = wide(own[1:2], rows, home[0][0].shape[1]) + k

time: 24.3 us -> 24.3 us (level)
  no operation moved by 1% of the time
where the time goes in v8:
time: 24.3 us; the launch traced here: 24.1 us
  starting transfers between devices  10.8 us (44%)
  Pallas kernels  10.2 us (42%)
  waiting for transfers between devices  2.31 us (10%)
  between operations  0.77 us (3%)
    ppermute x4, starting transfers between devices, from_behind(): lax.ppermute(value, 'blk', [(i, (i + by) % peers) for i in range(peers)])  8.06 us
    pallas_call x6, Pallas kernels, stage(): pl.pallas_call(functools.partial(terms_kernel, plan, total is not None, c...  6.92 us
    pallas_call x1, Pallas kernels, local(): pl.pallas_call(functools.partial(pack_kernel, ('blk', 'grp')), out_shape=...  1.81 us
    ppermute x1, starting transfers between devices, local(): lax.ppermute(others[k - 1], 'grp', [(g, (g + k) % groups) for g in range(...  1.59 us
    ppermute x4, waiting for transfers between devices, from_behind(): lax.ppermute(value, 'blk', [(i, (i + by) % peers) for i in range(peers)])  1.54 us
    ppermute x6, starting transfers between devices, other_core(): return lax.ppermute(value, 'blk', [(i, i ^ 1) for i in range(peers)])  1.19 us
    pallas_call x1, Pallas kernels, local(): pl.pallas_call(functools.partial(sum_kernel, len(parts)), out_shape=(jax....  0.98 us
  transfers between devices with their start and end apart: 11, of which 4 were waited for; matrix products, arithmetic and copies ran while one was open for 0% of the time, Pallas kernels for 31%

profile of v8, /device:TPU:0, one launch (start us, length us, event | category | flops | bytes accessed | tf_op | source)
XLA Modules:
  0.0 24.1 jit_solution(12520591487548096890)
XLA Ops:
  0.6 0.0 copy-start.2
  0.7 1.8 %pack.1.refs_1_.refs_2_.refs_3_.refs_4_ = bf16[544,128]{1,0:T(8,128)(2,1)} custom-call(bf16[2,32,1024]{2,1,0:T(8,128)(2,1)} %residents.1, s32[1,3,2,4]{3,2,1,0:T(2,128)} %bitcast.3), custom_call_target="tpu_custom_call" | custom-call | flops 1000000000 | bytes 1024 | tf_op jit(solution)/shard_map/pack/pallas_call | solution.py:387
  2.5 0.0 copy-start
  2.5 5.1 %collective-permute-start.1 = (bf16[544,128]{1,0:T(8,128)(2,1)}, bf16[544,128]{1,0:T(8,128)(2,1)S(1)}, u32[]{:S(2)}, u32[]{:S(2)}) collective-permute-start(bf16[544,128]{1,0:T(8,128)(2,1)} %pack.1.refs_1_.refs_2_.refs_3_.refs_4_), channel_id=1, source_target_pairs={{0,24},{2,26},{4,28},{6,30},{8,0},{10,2},{12,4},{14,6},{16,8},{18,... | collective-permute-start | bytes 417800 | tf_op jit(solution)/shard_map/ppermute | solution.py:367
  7.6 1.4 %collective-permute-start = (bf16[544,128]{1,0:T(8,128)(2,1)}, bf16[544,128]{1,0:T(8,128)(2,1)S(1)}, u32[]{:S(2)}, u32[]{:S(2)}) collective-permute-start(bf16[544,128]{1,0:T(8,128)(2,1)} %pack.1.refs_1_.refs_2_.refs_3_.refs_4_), channel_id=1, source_target_pairs={{0,28},{2,30},{4,0},{6,2},{8,4},{10,6},{12,8},{14,10},{16,12},{18,... | collective-permute-start | bytes 417800 | tf_op jit(solution)/shard_map/ppermute | solution.py:367
  9.0 0.6 %collective-permute-start.5 = (bf16[2,32,1024]{2,1,0:T(8,128)(2,1)S(1)}, bf16[2,32,1024]{2,1,0:T(8,128)(2,1)S(1)}, u32[]{:S(2)}, u32[]{:S(2)}) collective-permute-start(bf16[2,32,1024]{2,1,0:T(8,128)(2,1)S(1)} %copy-done.1), channel_id=1, source_target_pairs={{0,4},{2,6},{4,8},{6,10},{8,12},{10,14},{12,16},{14,18},{16,20},{1... | collective-permute-start | bytes 393224 | tf_op jit(solution)/shard_map/ppermute | solution.py:367
  9.6 0.9 %collective-permute-start.6 = (bf16[2,32,1024]{2,1,0:T(8,128)(2,1)S(1)}, bf16[2,32,1024]{2,1,0:T(8,128)(2,1)S(1)}, u32[]{:S(2)}, u32[]{:S(2)}) collective-permute-start(bf16[2,32,1024]{2,1,0:T(8,128)(2,1)S(1)} %copy-done.1), channel_id=1, source_target_pairs={{0,8},{2,10},{4,12},{6,14},{8,16},{10,18},{12,20},{14,22},{16,24},... | collective-permute-start | bytes 393224 | tf_op jit(solution)/shard_map/ppermute | solution.py:367
  10.6 0.5 %tables.1 = (bf16[512,256]{1,0:T(8,128)(2,1)S(1)}, bf16[256,128]{1,0:T(8,128)(2,1)S(1)}, f32[32,1024]{1,0:T(8,128)S(1)}, bf16[512,512]{1,0:T(8,128)(2,1)S(1)}, b...) custom-call(f32[72,256]{1,0:T(8,128)S(1)} %copy-done.2, bf16[2,32,1024]{2,1,0:T(8,128)(2,1)S(1)} %copy-done.1), custom_call_target="tpu_custom_call" | custom-call | flops 20000000000 | bytes 1024 | tf_op jit(solution)/shard_map/tables/pallas_call | solution.py:402
  11.0 1.0 %collective-permute-done.1.refs_0_ = bf16[544,128]{1,0:T(8,128)(2,1)S(1)} collective-permute-done((bf16[544,128]{1,0:T(8,128)(2,1)}, bf16[544,128]{1,0:T(8,128)(2,1)S(1)}, u32[]{:S(2)}, u32[]{:S(2)}) %collective-permute-start.1) | collective-permute-done | bytes 139296 | tf_op jit(solution)/shard_map/ppermute | solution.py:367
  12.1 0.0 collective-permute-start.3
  12.1 0.5 %collective-permute-start.2 = (bf16[544,128]{1,0:T(8,128)(2,1)S(1)}, bf16[544,128]{1,0:T(8,128)(2,1)S(1)}, u32[]{:S(2)}, u32[]{:S(2)}) collective-permute-start(bf16[544,128]{1,0:T(8,128)(2,1)S(1)} %copy-done), channel_id=1, source_target_pairs={{0,2},{2,0},{4,6},{6,4},{8,10},{10,8},{12,14},{14,12},{16,18},{18,... | collective-permute-start | bytes 417800 | tf_op jit(solution)/shard_map/ppermute | solution.py:372
  12.6 0.9 %first_traveller_terms.1.refs_8_ = f32[2,4,32,256]{3,2,1,0:T(8,128)S(1)} custom-call(bf16[544,128]{1,0:T(8,128)(2,1)S(1)} %collective-permute-done.1.refs_0_, bf16[544,128]{1,0:T(8,128)(2,1)S(1)} %copy-done, bf16[512,128]{1,0:T(8,128)(2,1)S(1)} %get-tuple-element.26.refs_2_.refs_3_, bf16[512,256]{1,0:T(8,128)(2,1)S(1)} %get-tuple-element.27.refs_3_.refs_4_.refs_5_, ...), custom_call_target="tpu_custom_call" | custom-call | flops 10000000000 | bytes 1024 | tf_op jit(solution)/shard_map/first_traveller_terms/pallas_call | solution.py:431
  13.5 0.0 collective-permute-done.3.refs_1_
  13.5 0.1 collective-permute-start.8
  13.6 0.0 collective-permute-done.2.refs_0_
  13.6 0.9 %early_traveller_terms.1.refs_7_ = f32[2,4,32,256]{3,2,1,0:T(8,128)S(1)} custom-call(bf16[544,128]{1,0:T(8,128)(2,1)S(1)} %collective-permute-done.2.refs_0_, bf16[544,128]{1,0:T(8,128)(2,1)S(1)} %collective-permute-done.3.refs_1_, bf16[544,128]{1,0:T(8,128)(2,1)S(1)} %copy-done, bf16[512,128]{1,0:T(8,128)(2,1)S(1)} %get-tuple-element.26.refs_2_.refs_3_, ...), custom_call_target="tpu_custom_call" | custom-call | flops 10000000000 | bytes 1024 | tf_op jit(solution)/shard_map/early_traveller_terms/pallas_call | solution.py:431
  14.6 0.5 %collective-permute-done.refs_0_._ = bf16[544,128]{1,0:T(8,128)(2,1)S(1)} collective-permute-done((bf16[544,128]{1,0:T(8,128)(2,1)}, bf16[544,128]{1,0:T(8,128)(2,1)S(1)}, u32[]{:S(2)}, u32[]{:S(2)}) %collective-permute-start) | collective-permute-done | bytes 139296 | tf_op jit(solution)/shard_map/ppermute | solution.py:367
  15.1 0.0 collective-permute-start.4
  15.1 0.9 %middle_traveller_terms.1.refs_7_ = f32[2,4,32,256]{3,2,1,0:T(8,128)S(1)} custom-call(bf16[544,128]{1,0:T(8,128)(2,1)S(1)} %collective-permute-done.refs_0_._, bf16[544,128]{1,0:T(8,128)(2,1)S(1)} %copy-done, bf16[512,128]{1,0:T(8,128)(2,1)S(1)} %get-tuple-element.26.refs_2_.refs_3_, bf16[512,256]{1,0:T(8,128)(2,1)S(1)} %get-tuple-element.27.refs_3_.refs_4_.refs_5_, ...), custom_call_target="tpu_custom_call" | custom-call | flops 1000000000 | bytes 1024 | tf_op jit(solution)/shard_map/middle_traveller_terms/pallas_call | solution.py:431
  16.0 0.4 %collective-permute-done.4.refs_0_ = bf16[544,128]{1,0:T(8,128)(2,1)S(1)} collective-permute-done((bf16[544,128]{1,0:T(8,128)(2,1)S(1)}, bf16[544,128]{1,0:T(8,128)(2,1)S(1)}, u32[]{:S(2)}, u32[]{:S(2)}) %collective-permute-start.4) | collective-permute-done | bytes 139296 | tf_op jit(solution)/shard_map/ppermute | solution.py:372
  16.4 0.9 %late_traveller_terms.1 = (f32[2,4,16,256]{3,2,1,0:T(8,128)S(1)}, f32[1,136,256]{2,1,0:T(8,128)S(1)}) custom-call(bf16[544,128]{1,0:T(8,128)(2,1)S(1)} %collective-permute-done.4.refs_0_, bf16[544,128]{1,0:T(8,128)(2,1)S(1)} %copy-done, bf16[512,128]{1,0:T(8,128)(2,1)S(1)} %get-tuple-element.26.refs_2_.refs_3_, ...), custom_call_target="tpu_custom_call" | custom-call | flops 2000000000 | bytes 1024 | tf_op jit(solution)/shard_map/late_traveller_terms/pallas_call | solution.py:431
  17.4 1.6 %collective-permute-start.10 = (f32[136,256]{1,0:T(8,128)S(1)}, f32[136,256]{1,0:T(8,128)S(1)}, u32[]{:S(2)}, u32[]{:S(2)}) collective-permute-start(f32[136,256]{1,0:T(8,128)S(1)} %bitcast.2), channel_id=1, source_target_pairs={{0,1},{1,0},{2,3},{3,2},{4,5},{5,4},{6,7},{7,6},{8,9},{9,8},{10,11... | collective-permute-start | bytes 417800 | tf_op jit(solution)/shard_map/ppermute | solution.py:485
  19.0 0.0 collective-permute-done.5.refs_0_
  19.0 0.0 collective-permute-done.6.refs_1_
  19.0 0.1 collective-permute-start.7
  19.0 0.5 %collective-permute-start.9 = (bf16[2,32,1024]{2,1,0:T(8,128)(2,1)S(1)}, bf16[2,32,1024]{2,1,0:T(8,128)(2,1)S(1)}, u32[]{:S(2)}, u32[]{:S(2)}) collective-permute-start(bf16[2,32,1024]{2,1,0:T(8,128)(2,1)S(1)} %collective-permute-done.6.refs_1_), channel_id=1, source_target_pairs={{0,2},{2,0},{4,6},{6,4},{8,10},{10,8},{12,14},{14,12},{16,18},{18,... | collective-permute-start | bytes 393224 | tf_op jit(solution)/shard_map/ppermute | solution.py:372
  19.5 1.5 %early_resident_terms.1.refs_9_ = f32[2,4,32,256]{3,2,1,0:T(8,128)S(1)} custom-call(bf16[2,32,1024]{2,1,0:T(8,128)(2,1)S(1)} %collective-permute-done.5.refs_0_, bf16[2,32,1024]{2,1,0:T(8,128)(2,1)S(1)} %collective-permute-done.6.refs_1_, bf16[544,128]{1,0:T(8,128)(2,1)S(1)} %copy-done, bf16[544,128]{1,0:T(8,128)(2,1)S(1)} %copy-done, ...), custom_call_target="tpu_custom_call" | custom-call | flops 1000000 | bytes 1024 | tf_op jit(solution)/shard_map/early_resident_terms/pallas_call | solution.py:431
  21.1 0.0 collective-permute-done.8.refs_1_
  21.1 0.0 collective-permute-done.9.refs_2_
  21.1 1.8 %late_resident_terms.1.refs_3_ = f32[2,32,1024]{2,1,0:T(8,128)S(1)} custom-call(bf16[2,32,1024]{2,1,0:T(8,128)(2,1)S(1)} %collective-permute-done.7.refs_0_, bf16[2,32,1024]{2,1,0:T(8,128)(2,1)S(1)} %collective-permute-done.8.refs_1_, bf16[2,32,1024]{2,1,0:T(8,128)(2,1)S(1)} %collective-permute-done.9.refs_2_, bf16[544,128]{1,0:T(8,128)(2,1)S(1)} %copy-done, ...), custom_call_target="tpu_custom_call" | custom-call | flops 1000000 | bytes 1024 | tf_op jit(solution)/shard_map/late_resident_terms/pallas_call | solution.py:431
  22.8 0.3 %collective-permute-done.10.refs_1_ = f32[136,256]{1,0:T(8,128)S(1)} collective-permute-done((f32[136,256]{1,0:T(8,128)S(1)}, f32[136,256]{1,0:T(8,128)S(1)}, u32[]{:S(2)}, u32[]{:S(2)}) %collective-permute-start.10) | collective-permute-done | bytes 139296 | tf_op jit(solution)/shard_map/ppermute | solution.py:485
  23.2 1.0 %sums.1 = (f32[2,16,1024]{2,1,0:T(8,128)}, f32[2,32,1024]{2,1,0:T(8,128)}) custom-call(f32[2,4,16,256]{3,2,1,0:T(8,128)S(1)} %get-tuple-element.33.refs_0_, f32[136,256]{1,0:T(8,128)S(1)} %collective-permute-done.10.refs_1_, bf16[512,512]{1,0:T(8,128)(2,1)S(1)} %get-tuple-element.39.refs_10_.refs_2_, f32[2,32,1024]{2,1,0:T(8,128)S(1)} %late_resident_terms.1.refs_3_), custom_call_target="tpu_custom_call" | custom-call | flops 500000000 | bytes 1024 | tf_op jit(solution)/shard_map/sums/pallas_call | solution.py:503
  (7 shorter events, 0.0 us)
Async XLA Ops:
  0.6 8.3 %copy-start.1 = (bf16[2,32,1024]{2,1,0:T(8,128)(2,1)S(1)}, bf16[2,32,1024]{2,1,0:T(8,128)(2,1)}, u32[]{:S(2)}) copy-start(bf16[2,32,1024]{2,1,0:T(8,128)(2,1)} %travellers.1) | copy-start | bytes 393220
  0.6 9.9 %copy-start.2 = (f32[72,256]{1,0:T(8,128)S(1)}, f32[72,256]{1,0:T(8,128)}, u32[]{:S(2)}) copy-start(f32[72,256]{1,0:T(8,128)} %constant.2.clone.small) | copy-start | bytes 221188
  2.5 9.6 %copy-start = (bf16[544,128]{1,0:T(8,128)(2,1)S(1)}, bf16[544,128]{1,0:T(8,128)(2,1)}, u32[]{:S(2)}) copy-start(bf16[544,128]{1,0:T(8,128)(2,1)} %pack.1.refs_1_.refs_2_.refs_3_.refs_4_) | copy-start | bytes 417796
  2.5 9.6 %collective-permute-start.1 = (bf16[544,128]{1,0:T(8,128)(2,1)}, bf16[544,128]{1,0:T(8,128)(2,1)S(1)}, u32[]{:S(2)}, u32[]{:S(2)}) collective-permute-start(bf16[544,128]{1,0:T(8,128)(2,1)} %pack.1.refs_1_.refs_2_.refs_3_.refs_4_), channel_id=1, source_target_pairs={{0,24},{2,26},{4,28},{6,30},{8,0},{10,2},{12,4},{14,6},{16,8},{18,... | collective-permute-start | bytes 417800 | tf_op jit(solution)/shard_map/ppermute | solution.py:367
  7.6 7.5 %collective-permute-start = (bf16[544,128]{1,0:T(8,128)(2,1)}, bf16[544,128]{1,0:T(8,128)(2,1)S(1)}, u32[]{:S(2)}, u32[]{:S(2)}) collective-permute-start(bf16[544,128]{1,0:T(8,128)(2,1)} %pack.1.refs_1_.refs_2_.refs_3_.refs_4_), channel_id=1, source_target_pairs={{0,28},{2,30},{4,0},{6,2},{8,4},{10,6},{12,8},{14,10},{16,12},{18,... | collective-permute-start | bytes 417800 | tf_op jit(solution)/shard_map/ppermute | solution.py:367
  9.0 10.0 %collective-permute-start.5 = (bf16[2,32,1024]{2,1,0:T(8,128)(2,1)S(1)}, bf16[2,32,1024]{2,1,0:T(8,128)(2,1)S(1)}, u32[]{:S(2)}, u32[]{:S(2)}) collective-permute-start(bf16[2,32,1024]{2,1,0:T(8,128)(2,1)S(1)} %copy-done.1), channel_id=1, source_target_pairs={{0,4},{2,6},{4,8},{6,10},{8,12},{10,14},{12,16},{14,18},{16,20},{1... | collective-permute-start | bytes 393224 | tf_op jit(solution)/shard_map/ppermute | solution.py:367
  9.6 9.3 %collective-permute-start.6 = (bf16[2,32,1024]{2,1,0:T(8,128)(2,1)S(1)}, bf16[2,32,1024]{2,1,0:T(8,128)(2,1)S(1)}, u32[]{:S(2)}, u32[]{:S(2)}) collective-permute-start(bf16[2,32,1024]{2,1,0:T(8,128)(2,1)S(1)} %copy-done.1), channel_id=1, source_target_pairs={{0,8},{2,10},{4,12},{6,14},{8,16},{10,18},{12,20},{14,22},{16,24},... | collective-permute-start | bytes 393224 | tf_op jit(solution)/shard_map/ppermute | solution.py:367
  12.1 1.4 %collective-permute-start.3 = (bf16[544,128]{1,0:T(8,128)(2,1)S(1)}, bf16[544,128]{1,0:T(8,128)(2,1)S(1)}, u32[]{:S(2)}, u32[]{:S(2)}) collective-permute-start(bf16[544,128]{1,0:T(8,128)(2,1)S(1)} %collective-permute-done.1.refs_0_), channel_id=1, source_target_pairs={{0,2},{2,0},{4,6},{6,4},{8,10},{10,8},{12,14},{14,12},{16,18},{18,... | collective-permute-start | bytes 417800 | tf_op jit(solution)/shard_map/ppermute | solution.py:372
  12.1 1.6 %collective-permute-start.2 = (bf16[544,128]{1,0:T(8,128)(2,1)S(1)}, bf16[544,128]{1,0:T(8,128)(2,1)S(1)}, u32[]{:S(2)}, u32[]{:S(2)}) collective-permute-start(bf16[544,128]{1,0:T(8,128)(2,1)S(1)} %copy-done), channel_id=1, source_target_pairs={{0,2},{2,0},{4,6},{6,4},{8,10},{10,8},{12,14},{14,12},{16,18},{18,... | collective-permute-start | bytes 417800 | tf_op jit(solution)/shard_map/ppermute | solution.py:372
  13.5 7.5 %collective-permute-start.8 = (bf16[2,32,1024]{2,1,0:T(8,128)(2,1)S(1)}, bf16[2,32,1024]{2,1,0:T(8,128)(2,1)S(1)}, u32[]{:S(2)}, u32[]{:S(2)}) collective-permute-start(bf16[2,32,1024]{2,1,0:T(8,128)(2,1)S(1)} %copy-done.1), channel_id=1, source_target_pairs={{0,2},{2,0},{4,6},{6,4},{8,10},{10,8},{12,14},{14,12},{16,18},{18,... | collective-permute-start | bytes 393224 | tf_op jit(solution)/shard_map/ppermute | solution.py:372
  15.1 1.4 %collective-permute-start.4 = (bf16[544,128]{1,0:T(8,128)(2,1)S(1)}, bf16[544,128]{1,0:T(8,128)(2,1)S(1)}, u32[]{:S(2)}, u32[]{:S(2)}) collective-permute-start(bf16[544,128]{1,0:T(8,128)(2,1)S(1)} %collective-permute-done.refs_0_._), channel_id=1, source_target_pairs={{0,2},{2,0},{4,6},{6,4},{8,10},{10,8},{12,14},{14,12},{16,18},{18,... | collective-permute-start | bytes 417800 | tf_op jit(solution)/shard_map/ppermute | solution.py:372
  17.4 5.8 %collective-permute-start.10 = (f32[136,256]{1,0:T(8,128)S(1)}, f32[136,256]{1,0:T(8,128)S(1)}, u32[]{:S(2)}, u32[]{:S(2)}) collective-permute-start(f32[136,256]{1,0:T(8,128)S(1)} %bitcast.2), channel_id=1, source_target_pairs={{0,1},{1,0},{2,3},{3,2},{4,5},{5,4},{6,7},{7,6},{8,9},{9,8},{10,11... | collective-permute-start | bytes 417800 | tf_op jit(solution)/shard_map/ppermute | solution.py:485
  19.0 2.1 %collective-permute-start.7 = (bf16[2,32,1024]{2,1,0:T(8,128)(2,1)S(1)}, bf16[2,32,1024]{2,1,0:T(8,128)(2,1)S(1)}, u32[]{:S(2)}, u32[]{:S(2)}) collective-permute-start(bf16[2,32,1024]{2,1,0:T(8,128)(2,1)S(1)} %collective-permute-done.5.refs_0_), channel_id=1, source_target_pairs={{0,2},{2,0},{4,6},{6,4},{8,10},{10,8},{12,14},{14,12},{16,18},{18,... | collective-permute-start | bytes 393224 | tf_op jit(solution)/shard_map/ppermute | solution.py:372
  19.0 2.0 %collective-permute-start.9 = (bf16[2,32,1024]{2,1,0:T(8,128)(2,1)S(1)}, bf16[2,32,1024]{2,1,0:T(8,128)(2,1)S(1)}, u32[]{:S(2)}, u32[]{:S(2)}) collective-permute-start(bf16[2,32,1024]{2,1,0:T(8,128)(2,1)S(1)} %collective-permute-done.6.refs_1_), channel_id=1, source_target_pairs={{0,2},{2,0},{4,6},{6,4},{8,10},{10,8},{12,14},{14,12},{16,18},{18,... | collective-permute-start | bytes 393224 | tf_op jit(solution)/shard_map/ppermute | solution.py:372
